TPU v7x, 32 devices: a whole 2x2x4 slice. The times are simulated.
32 devices in a mesh: outer: 8 (over y, x, core), inner: 4 (over z).
Axes of the slice: x: 2, y: 2, z: 4, core: 2. Of those that a mesh axis runs over, the one named last changes fastest.
Arguments:
- queries: bfloat16 [4096, 2048], P(('outer', 'inner')), may hold values from -6 to 6
- keys: bfloat16 [4096, 2048], P(('outer', 'inner')), may hold values from -6 to 6
- values: bfloat16 [4096, 2048], P(('outer', 'inner')), may hold values from -7 to 7
- cotangent: bfloat16 [4096, 2048], P(('outer', 'inner')), may hold values from -7 to 7
Outputs:
- attended: bfloat16 [4096, 2048], P(('outer', 'inner'))
- query_grad: bfloat16 [4096, 2048], P(('outer', 'inner'))
- key_grad: bfloat16 [4096, 2048], P(('outer', 'inner'))
- value_grad: bfloat16 [4096, 2048], P(('outer', 'inner'))
All inputs are finite; a program needn't handle non-finite values.
Results may differ from a plain program's by a relative error of at most 0.013.
The roundings to bfloat16 on the way count: a program that leaves them out, or rounds other values in their place, can miss the bound.
Values sent between devices are 32-bit elements; how exact they have to be, the bound alone decides.
No kernel may reach another device: no remote copies, remote signals or barrier semaphores. Data moves between devices by JAX's collectives and lax.ppermute only.
A program may use at most 128 MiB of HBM per device.

v0:
```python
import jax
import jax.numpy as jnp
from jax import lax
from jax.sharding import PartitionSpec as P

HEADS = 16
HD = 128


def entering(shard, axis, combine, identity, reverse):
    devices, place = (lax.axis_size(axis), lax.axis_index(axis))
    everything = jax.tree.map(lambda part: lax.all_gather(part, axis), shard)
    start = jax.tree.map(
        lambda part, zero: jnp.broadcast_to(jnp.asarray(zero, part.dtype), part.shape),
        shard,
        identity,
    )

    def lap(k, before):
        at = devices - 1 - k if reverse else k
        reached = at > place if reverse else at < place
        new = combine(before, jax.tree.map(lambda part: part[at], everything))
        return jax.tree.map(lambda a, b: jnp.where(reached, a, b), new, before)

    return lax.fori_loop(0, devices, lap, start)


def features(x):
    wide = x.astype(jnp.float32)
    return jnp.where(wide > 0, wide + 1.0, jnp.exp(jnp.minimum(wide, 0.0)))


def slope(x):
    wide = x.astype(jnp.float32)
    return jnp.where(wide > 0, 1.0, jnp.exp(jnp.minimum(wide, 0.0)))


def add_pair(first, second):
    return (first[0] + second[0], first[1] + second[1])


def zero_pair(parts):
    return (jnp.zeros_like(parts[0]), jnp.zeros_like(parts[1]))


def carry_states(parts, backward):
    count = lax.axis_size("inner")
    arrived = (
        lax.all_to_all(parts[0], "inner", split_axis=0, concat_axis=0, tiled=True),
        lax.all_to_all(parts[1], "inner", split_axis=0, concat_axis=0, tiled=True),
    )
    stacked = tuple(
        (piece.reshape((count, piece.shape[0] // count) + piece.shape[1:]) for piece in arrived)
    )
    totals = tuple((jnp.sum(piece, axis=0) for piece in stacked))
    if backward:
        within = tuple(
            (total[None] - jnp.cumsum(piece, axis=0) for total, piece in zip(totals, stacked))
        )
    else:
        within = tuple((jnp.cumsum(piece, axis=0) - piece for piece in stacked))
    before = entering(totals, "outer", add_pair, zero_pair(totals), backward)
    flat_within = tuple((part_sum.reshape(piece.shape) for part_sum, piece in zip(within, arrived)))
    returned = (
        lax.all_to_all(flat_within[0], "inner", split_axis=0, concat_axis=0, tiled=True),
        lax.all_to_all(flat_within[1], "inner", split_axis=0, concat_axis=0, tiled=True),
    )
    spread = lax.all_gather(before, "inner", axis=0, tiled=True)
    return add_pair(returned, spread)


def per_device(queries, keys, values, cotangent):
    count_rows = queries.shape[0]
    shaped = (count_rows, HEADS, HD)
    query_rows = queries.reshape(shaped)
    key_rows = keys.reshape(shaped)
    value_rows = values.reshape(shaped)
    cotan_rows = cotangent.reshape(shaped)
    highest = lax.Precision.HIGHEST
    f32 = jnp.float32
    rows = lax.broadcasted_iota(jnp.int32, (count_rows, count_rows), 0)
    cols = lax.broadcasted_iota(jnp.int32, (count_rows, count_rows), 1)
    causal = (cols <= rows)[None]
    q_feat = features(query_rows).astype(jnp.bfloat16)
    k_feat = features(key_rows).astype(jnp.bfloat16)
    q_wide = q_feat.astype(f32)
    scores = jnp.einsum("thd,shd->hts", q_feat, k_feat, preferred_element_type=f32)
    scores = jnp.where(causal, scores, 0.0)
    weights = scores.astype(jnp.bfloat16)
    local_state = jnp.einsum("shd,she->hde", k_feat, value_rows, preferred_element_type=f32)
    local_norm = jnp.sum(k_feat.astype(f32), axis=0)
    intra_num = jnp.einsum("hts,she->the", weights, value_rows, preferred_element_type=f32)
    intra_den = jnp.sum(scores, axis=2).T
    state, normal = carry_states((local_state, local_norm), False)
    state_low = state.astype(jnp.bfloat16)
    den = intra_den + jnp.einsum("thd,hd->th", q_wide, normal, precision=highest)
    num = intra_num + jnp.einsum("thd,hde->the", q_feat, state_low, preferred_element_type=f32)
    ratio = num / den[:, :, None]
    attended = ratio.astype(jnp.bfloat16)
    cotan_wide = cotan_rows.astype(f32)
    grad_scaled = (cotan_wide / den[:, :, None]).astype(jnp.bfloat16)
    grad_den = -jnp.sum(cotan_wide * ratio, axis=2) / den
    grad_scores = jnp.einsum("the,she->hts", grad_scaled, value_rows, preferred_element_type=f32)
    grad_scores = jnp.where(causal, grad_scores + grad_den.T[:, :, None], 0.0).astype(jnp.bfloat16)
    later_local = jnp.einsum("thd,the->hde", q_feat, grad_scaled, preferred_element_type=f32)
    later_norm_local = jnp.einsum("th,thd->hd", grad_den, q_wide, precision=highest)
    q_lin = jnp.einsum("hts,shd->thd", grad_scores, k_feat, preferred_element_type=f32)
    q_lin = q_lin + jnp.einsum("the,hde->thd", grad_scaled, state_low, preferred_element_type=f32)
    q_lin = q_lin + grad_den[:, :, None] * normal[None]
    query_grad = (q_lin * slope(query_rows)).astype(jnp.bfloat16)
    k_intra = jnp.einsum("hts,thd->shd", grad_scores, q_feat, preferred_element_type=f32)
    v_intra = jnp.einsum("hts,the->she", weights, grad_scaled, preferred_element_type=f32)
    later, later_norm = carry_states((later_local, later_norm_local), True)
    later_low = later.astype(jnp.bfloat16)
    k_lin = k_intra + jnp.einsum("she,hde->shd", value_rows, later_low, preferred_element_type=f32)
    k_lin = k_lin + later_norm[None]
    key_grad = (k_lin * slope(key_rows)).astype(jnp.bfloat16)
    value_grad = v_intra + jnp.einsum("shd,hde->she", k_feat, later_low, preferred_element_type=f32)
    flat = (count_rows, HEADS * HD)
    return (
        attended.reshape(flat),
        query_grad.reshape(flat),
        key_grad.reshape(flat),
        value_grad.astype(jnp.bfloat16).reshape(flat),
    )


def solution(mesh):
    placed = (
        P(("outer", "inner"), None),
        P(("outer", "inner"), None),
        P(("outer", "inner"), None),
        P(("outer", "inner"), None),
    )
    return jax.shard_map(
        per_device,
        mesh=mesh,
        in_specs=placed,
        out_specs=(
            P(("outer", "inner"), None),
            P(("outer", "inner"), None),
            P(("outer", "inner"), None),
            P(("outer", "inner"), None),
        ),
        check_vma=False,
    )
```

profile of v0, /device:TPU:0, one launch (start us, length us, event | category | flops | bytes accessed | tf_op | source)
XLA Modules:
  0.0 273.0 jit_solution(10203681294903885579)
XLA Ops:
  7.2 3.0 %fusion.20 = (f32[128,2048]{1,0:T(8,128)}, f32[2048]{0:T(1024)}, bf16[16,16,8,128]{3,2,1,0:T(8,128)(2,1)S(1)}, bf16[16,8,16,128]{3,1,2,0:T(8,128)(2,1)S(1)}) fusion(bf16[128,2048]{1,0:T(8,128)(2,1)} %param.9), kind=kLoop, calls=%fused_computation.40 | loop fusion | flops 2357248 | bytes 2629632 | tf_op jit(solution)/shard_map/jit(_where)/select_n | solution.py:35
  11.2 31.8 %all_to_all.56 = f32[16,128,128]{2,1,0:T(8,128)S(1)} all-to-all(f32[16,128,128]{2,1,0:T(8,128)S(1)} %fusion.30), channel_id=1, replica_groups=mesh['outer'=8,'inner'=4] {'inner'}, dimensions={0} | all-to-all | bytes 2097152 | tf_op jit(solution)/shard_map/all_to_all | solution.py:49
  43.8 3.3 %all-to-all-start.2 = ((f32[4,4,128]{2,1,0:T(4,128)}), f32[4,4,128]{2,1,0:T(4,128)S(1)}, u32[]{:S(2)}, u32[]{:S(2)}) async-start(f32[4,4,128]{2,1,0:T(4,128)} %bitcast.4), calls=%async_computation.2 | async-start | bytes 16384 | tf_op jit(solution)/shard_map/all_to_all | solution.py:50
  47.1 2.4 fusion.16
  50.8 2.3 copy.45
  56.1 5.0 %all-to-all-start.3 = ((f32[4,4,128]{2,1,0:T(4,128)}), f32[4,4,128]{2,1,0:T(4,128)S(1)}, u32[]{:S(2)}, u32[]{:S(2)}) async-start(f32[4,4,128]{2,1,0:T(4,128)} %reduce-window_subtract_fusion.2), calls=%async_computation.3 | async-start | bytes 16384 | tf_op jit(solution)/shard_map/all_to_all | solution.py:66
  61.1 8.9 %all-gather.4 = f32[8,4,128]{2,1,0:T(4,128)S(1)} all-gather(f32[1,4,128]{2,1,0:T(4,128)S(1)} %bitcast.177), channel_id=3, replica_groups=mesh['outer'=8,'inner'=4] {'outer'}, dimensions={0}, use_global_device_ids=true | all-gather | bytes 18432 | tf_op jit(solution)/shard_map/all_gather | solution.py:12
  71.0 8.7 %while.34 = (s32[]{:T(128)}, f32[4,128,128]{2,1,0:T(8,128)S(1)}, f32[4,128]{1,0:T(4,128)S(1)}, s32[]{:T(128)}, f32[8,4,128,128]{3,2,1,0:T(8,128)}, /*index=5*/f32[8,4,128]{2,1,0:T(4,128)S(1)}, s32[]{:T(128)}, s32[]{:T(128)}) while((s32[]{:T(128)}, f32[4,128,128]{2,1,0:T(8,128)S(1)}, f32[4,128]{1,0:T(4,128)S(1)}, s32[]{:T(128)}, ...), condition=%wide.region_5.6_spmd.clone, body=%wide.region_4.5_spmd.clone.sunk | while | flops 198148 | bytes 792699 | solution.py:25
  79.7 11.9 %all-gather.5 = f32[4,4,128]{2,1,0:T(4,128)S(1)} all-gather(f32[1,4,128]{2,1,0:T(4,128)S(1)} %bitcast.173), channel_id=1, replica_groups=mesh['outer'=8,'inner'=4] {'inner'}, dimensions={0}, use_global_device_ids=true | all-gather | bytes 10240 | tf_op jit(solution)/shard_map/all_gather | solution.py:68
  93.5 1.5 fusion.53
  95.0 3.5 %all-to-all-start.4 = ((f32[16,128,128]{2,1,0:T(8,128)}), f32[16,128,128]{2,1,0:T(8,128)S(1)}, u32[]{:S(2)}, u32[]{:S(2)}) async-start(f32[16,128,128]{2,1,0:T(8,128)} %fusion.53), calls=%async_computation.4 | async-start | bytes 2097152 | tf_op jit(solution)/shard_map/all_to_all | solution.py:49
  100.4 37.0 %all-to-all-done.4 = f32[16,128,128]{2,1,0:T(8,128)S(1)} async-done(((f32[16,128,128]{2,1,0:T(8,128)}), f32[16,128,128]{2,1,0:T(8,128)S(1)}, u32[]{:S(2)}, u32[]{:S(2)}) %all-to-all-start.4) | async-done | bytes 1048608 | tf_op jit(solution)/shard_map/all_to_all | solution.py:49
  138.2 2.4 bitcast_subtract_fusion
  140.6 4.5 %all-to-all-start.1 = ((f32[16,128,128]{2,1,0:T(8,128)}), f32[16,128,128]{2,1,0:T(8,128)}, u32[]{:S(2)}, u32[]{:S(2)}) async-start(f32[16,128,128]{2,1,0:T(8,128)} %bitcast_subtract_fusion), calls=%async_computation.1 | async-start | bytes 2097152 | tf_op jit(solution)/shard_map/all_to_all | solution.py:65
  145.1 2.6 copy.52
  147.7 2.6 copy.58
  150.2 16.4 %all-to-all-done.1 = f32[16,128,128]{2,1,0:T(8,128)} async-done(((f32[16,128,128]{2,1,0:T(8,128)}), f32[16,128,128]{2,1,0:T(8,128)}, u32[]{:S(2)}, u32[]{:S(2)}) %all-to-all-start.1) | async-done | bytes 1048608 | tf_op jit(solution)/shard_map/all_to_all | solution.py:65
  166.7 1.7 add_convert_fusion.1
  168.4 1.6 convolution_bitcast_fusion.1
  170.0 2.7 multiply_reduce_fusion
  173.8 3.2 %all-to-all-start.6 = ((f32[4,4,128]{2,1,0:T(4,128)}), f32[4,4,128]{2,1,0:T(4,128)S(1)}, u32[]{:S(2)}, u32[]{:S(2)}) async-start(f32[4,4,128]{2,1,0:T(4,128)} %bitcast.27), calls=%async_computation.6 | async-start | bytes 16384 | tf_op jit(solution)/shard_map/all_to_all | solution.py:50
  178.1 4.5 %all-to-all-done.6 = f32[4,4,128]{2,1,0:T(4,128)S(1)} async-done(((f32[4,4,128]{2,1,0:T(4,128)}), f32[4,4,128]{2,1,0:T(4,128)S(1)}, u32[]{:S(2)}, u32[]{:S(2)}) %all-to-all-start.6) | async-done | bytes 8224 | tf_op jit(solution)/shard_map/all_to_all | solution.py:50
  183.2 3.2 %all-to-all-start.7 = ((f32[4,4,128]{2,1,0:T(4,128)}), f32[4,4,128]{2,1,0:T(4,128)S(1)}, u32[]{:S(2)}, u32[]{:S(2)}) async-start(f32[4,4,128]{2,1,0:T(4,128)} %reduce-window_subtract_fusion.1), calls=%async_computation.7 | async-start | bytes 16384 | tf_op jit(solution)/shard_map/all_to_all | solution.py:66
  186.5 8.9 %all-gather.6 = f32[8,4,128]{2,1,0:T(4,128)S(1)} all-gather(f32[1,4,128]{2,1,0:T(4,128)S(1)} %bitcast.176), channel_id=5, replica_groups=mesh['outer'=8,'inner'=4] {'outer'}, dimensions={0}, use_global_device_ids=true | all-gather | bytes 18432 | tf_op jit(solution)/shard_map/all_gather | solution.py:12
  195.4 8.7 %while.35 = (s32[]{:T(128)}, f32[4,128,128]{2,1,0:T(8,128)S(1)}, f32[4,128]{1,0:T(4,128)S(1)}, s32[]{:T(128)}, f32[8,4,128,128]{3,2,1,0:T(8,128)}, /*index=5*/f3...) while((s32[]{:T(128)}, f32[4,128,128]{2,1,0:T(8,128)S(1)}, ...), condition=%wide.region_13.14_spmd.clone, body=%wide.region_12.13_spmd.clone.sunk | while | flops 198152 | bytes 792761 | solution.py:25
  204.9 5.2 %all-to-all-start.5 = ((f32[16,128,128]{2,1,0:T(8,128)}), f32[16,128,128]{2,1,0:T(8,128)}, u32[]{:S(2)}, u32[]{:S(2)}) async-start(f32[16,128,128]{2,1,0:T(8,128)} %bitcast.21), calls=%async_computation.5 | async-start | bytes 2097152 | tf_op jit(solution)/shard_map/all_to_all | solution.py:65
  210.0 1.5 fusion.41
  215.2 1.5 fusion.52
  216.7 41.8 %all-gather.7 = f32[4,4,128]{2,1,0:T(4,128)S(1)} all-gather(f32[1,4,128]{2,1,0:T(4,128)S(1)} %bitcast.172), channel_id=1, replica_groups=mesh['outer'=8,'inner'=4] {'inner'}, dimensions={0}, use_global_device_ids=true | all-gather | bytes 10240 | tf_op jit(solution)/shard_map/all_gather | solution.py:68
  258.5 1.7 add_convert_fusion
  261.5 2.0 copy.64
  263.5 1.9 fusion.12
  (114 shorter events, 38.1 us)
Async XLA Ops:
  7.2 3.7 %copy-start = (bf16[128,2048]{1,0:T(8,128)(2,1)S(1)}, bf16[128,2048]{1,0:T(8,128)(2,1)}, u32[]{:S(2)}) copy-start(bf16[128,2048]{1,0:T(8,128)(2,1)} %param.10) | copy-start | bytes 1572868
  7.2 63.9 %all-gather.17.cloned.1.call-start = ((), (), s32[]{:S(2)}) async-start(), calls=%async_computation.10 | async-start | bytes 2359296 | tf_op jit(solution)/shard_map/all_gather | solution.py:12
  10.3 39.2 %copy-start.13 = (bf16[16,16,8,128]{3,2,1,0:T(8,128)(2,1)}, bf16[16,16,8,128]{3,2,1,0:T(8,128)(2,1)S(1)}, u32[]{:S(2)}) copy-start(bf16[16,16,8,128]{3,2,1,0:T(8,128)(2,1)S(1)} %get-tuple-element.351) | copy-start | bytes 1572868
  10.9 32.2 %copy-start.7 = (bf16[128,16,128]{0,2,1:T(8,128)(2,1)}, bf16[128,16,128]{0,2,1:T(8,128)(2,1)S(1)}, u32[]{:S(2)}) copy-start(bf16[128,16,128]{0,2,1:T(8,128)(2,1)S(1)} %copy.41) | copy-start | bytes 1572868
  43.8 11.6 %all-to-all-start.2 = ((f32[4,4,128]{2,1,0:T(4,128)}), f32[4,4,128]{2,1,0:T(4,128)S(1)}, u32[]{:S(2)}, u32[]{:S(2)}) async-start(f32[4,4,128]{2,1,0:T(4,128)} %bitcast.4), calls=%async_computation.2 | async-start | bytes 16384 | tf_op jit(solution)/shard_map/all_to_all | solution.py:50
  49.5 42.7 %copy-start.5 = (bf16[16,16,8,128]{3,2,1,0:T(8,128)(2,1)}, bf16[16,16,8,128]{3,2,1,0:T(8,128)(2,1)S(1)}, u32[]{:S(2)}) copy-start(bf16[16,16,8,128]{3,2,1,0:T(8,128)(2,1)S(1)} %get-tuple-element.354) | copy-start | bytes 1572868
  55.4 38.1 %copy-start.3 = (bf16[128,16,128]{0,2,1:T(8,128)(2,1)}, bf16[128,16,128]{0,2,1:T(8,128)(2,1)S(1)}, u32[]{:S(2)}) copy-start(bf16[128,16,128]{0,2,1:T(8,128)(2,1)S(1)} %copy.53) | copy-start | bytes 1572868
  56.1 35.5 %all-to-all-start.3 = ((f32[4,4,128]{2,1,0:T(4,128)}), f32[4,4,128]{2,1,0:T(4,128)S(1)}, u32[]{:S(2)}, u32[]{:S(2)}) async-start(f32[4,4,128]{2,1,0:T(4,128)} %reduce-window_subtract_fusion.2), calls=%async_computation.3 | async-start | bytes 16384 | tf_op jit(solution)/shard_map/all_to_all | solution.py:66
  79.7 15.3 %copy-start.2 = (f32[4,128,128]{2,1,0:T(8,128)}, f32[4,128,128]{2,1,0:T(8,128)S(1)}, u32[]{:S(2)}) copy-start(f32[4,128,128]{2,1,0:T(8,128)S(1)} %get-tuple-element.269) | copy-start | bytes 786436
  95.0 42.4 %all-to-all-start.4 = ((f32[16,128,128]{2,1,0:T(8,128)}), f32[16,128,128]{2,1,0:T(8,128)S(1)}, u32[]{:S(2)}, u32[]{:S(2)}) async-start(f32[16,128,128]{2,1,0:T(8,128)} %fusion.53), calls=%async_computation.4 | async-start | bytes 2097152 | tf_op jit(solution)/shard_map/all_to_all | solution.py:49
  98.5 68.2 %all-gather.13.cloned.1.call-start = ((), (), s32[]{:S(2)}) async-start(), calls=%async_computation.8 | async-start | bytes 1310720 | tf_op jit(solution)/shard_map/all_gather | solution.py:68
  99.3 96.1 %all-gather.19.cloned.1.call-start = ((), (), s32[]{:S(2)}) async-start(), calls=%async_computation.11 | async-start | bytes 2359296 | tf_op jit(solution)/shard_map/all_gather | solution.py:12
  140.6 26.1 %all-to-all-start.1 = ((f32[16,128,128]{2,1,0:T(8,128)}), f32[16,128,128]{2,1,0:T(8,128)}, u32[]{:S(2)}, u32[]{:S(2)}) async-start(f32[16,128,128]{2,1,0:T(8,128)} %bitcast_subtract_fusion), calls=%async_computation.1 | async-start | bytes 2097152 | tf_op jit(solution)/shard_map/all_to_all | solution.py:65
  169.9 2.7 copy-start.6
  169.9 7.1 %copy-start.12 = (f32[4,128,128]{2,1,0:T(8,128)S(1)}, f32[4,128,128]{2,1,0:T(8,128)}, u32[]{:S(2)}) copy-start(f32[4,128,128]{2,1,0:T(8,128)} %reduce_sum.68) | copy-start | bytes 786436
  173.8 8.8 %all-to-all-start.6 = ((f32[4,4,128]{2,1,0:T(4,128)}), f32[4,4,128]{2,1,0:T(4,128)S(1)}, u32[]{:S(2)}, u32[]{:S(2)}) async-start(f32[4,4,128]{2,1,0:T(4,128)} %bitcast.27), calls=%async_computation.6 | async-start | bytes 16384 | tf_op jit(solution)/shard_map/all_to_all | solution.py:50
  183.2 21.6 %all-to-all-start.7 = ((f32[4,4,128]{2,1,0:T(4,128)}), f32[4,4,128]{2,1,0:T(4,128)S(1)}, u32[]{:S(2)}, u32[]{:S(2)}) async-start(f32[4,4,128]{2,1,0:T(4,128)} %reduce-window_subtract_fusion.1), calls=%async_computation.7 | async-start | bytes 16384 | tf_op jit(solution)/shard_map/all_to_all | solution.py:66
  186.4 72.0 %all-gather.15.cloned.1.call-start = ((), (), s32[]{:S(2)}) async-start(), calls=%async_computation.9 | async-start | bytes 1310720 | tf_op jit(solution)/shard_map/all_gather | solution.py:68
  204.1 0.7 copy-start.1
  204.1 5.9 %copy-start.15 = (bf16[16,128,128]{1,2,0:T(8,128)(2,1)S(1)}, bf16[16,128,128]{1,2,0:T(8,128)(2,1)}, u32[]{:S(2)}) copy-start(bf16[16,128,128]{1,2,0:T(8,128)(2,1)} %get-tuple-element.357) | copy-start | bytes 1572868
  204.8 6.7 %copy-start.14 = (bf16[128,16,128]{0,2,1:T(8,128)(2,1)S(1)}, bf16[128,16,128]{0,2,1:T(8,128)(2,1)}, u32[]{:S(2)}) copy-start(bf16[128,16,128]{0,2,1:T(8,128)(2,1)} %get-tuple-element.348) | copy-start | bytes 1572868
  204.9 53.6 %all-to-all-start.5 = ((f32[16,128,128]{2,1,0:T(8,128)}), f32[16,128,128]{2,1,0:T(8,128)}, u32[]{:S(2)}, u32[]{:S(2)}) async-start(f32[16,128,128]{2,1,0:T(8,128)} %bitcast.21), calls=%async_computation.5 | async-start | bytes 2097152 | tf_op jit(solution)/shard_map/all_to_all | solution.py:65
  210.0 2.8 %copy-start.8 = (bf16[128,16,128]{0,2,1:T(8,128)(2,1)S(1)}, bf16[128,16,128]{0,2,1:T(8,128)(2,1)}, u32[]{:S(2)}) copy-start(bf16[128,16,128]{0,2,1:T(8,128)(2,1)} %copy-done.7) | copy-start | bytes 1572868
  212.5 1.2 copy-start.10
  213.7 1.4 copy-start.4
  215.2 45.0 %copy-start.9 = (f32[128,2048]{0,1:T(8,128)S(1)}, f32[128,2048]{0,1:T(8,128)}, u32[]{:S(2)}) copy-start(f32[128,2048]{0,1:T(8,128)} %copy.58) | copy-start | bytes 3145732
  216.7 43.5 %copy-start.11 = (f32[16,128,128]{2,1,0:T(8,128)S(1)}, f32[16,128,128]{2,1,0:T(8,128)}, u32[]{:S(2)}) copy-start(f32[16,128,128]{2,1,0:T(8,128)} %fusion.52) | copy-start | bytes 3145732
Sparse Core Ops, SparseCore 0:
  43.9 27.0 all-gather.16
  101.5 38.0 all-gather.12
  142.0 25.9 all-gather.18
  205.0 46.7 all-gather.14
where the time goes:
time: 275 us; the launch traced here: 273 us
  blocking collectives  103 us (37%)
  waiting for transfers between devices  59.7 us (22%)
  other arithmetic  34.5 us (13%)
  starting transfers between devices  28.1 us (10%)
  local copies, waits for them, and re-layouts  16.8 us (6%)
  matrix products  16.1 us (6%)
  between operations  14.1 us (5%)
    all_gather x2, blocking collectives, carry_states(): spread = lax.all_gather(before, 'inner', axis=0, tiled=True)  53.7 us
    all_to_all x1, waiting for transfers between devices, carry_states(): lax.all_to_all(parts[0], 'inner', split_axis=0, concat_axis=0, tiled=True)  37 us
    all_to_all x1, blocking collectives, carry_states(): lax.all_to_all(parts[0], 'inner', split_axis=0, concat_axis=0, tiled=True)  31.8 us
    all_gather x2, blocking collectives, entering(): everything = jax.tree.map(lambda part: lax.all_gather(part, axis), shard)  17.8 us
    select_n x32, other arithmetic, lap(): return jax.tree.map(lambda a, b: jnp.where(reached, a, b), new, before)  16.9 us
    all_to_all x2, waiting for transfers between devices, carry_states(): lax.all_to_all(flat_within[0], 'inner', split_axis=0, concat_axis=0, tile...  16.4 us
    all_to_all x2, starting transfers between devices, carry_states(): lax.all_to_all(flat_within[0], 'inner', split_axis=0, concat_axis=0, tile...  9.66 us
    all_to_all x2, starting transfers between devices, carry_states(): lax.all_to_all(flat_within[1], 'inner', split_axis=0, concat_axis=0, tile...  8.29 us
  transfers between devices with their start and end apart: 11, of which 4 were waited for; matrix products, arithmetic and copies ran while one was open for 18% of the time, Pallas kernels for 0%

commit v1 on v0

v1 whole, which is shorter than its diff:
```python
import functools

import jax
import jax.numpy as jnp
from jax import lax
from jax.experimental import pallas as pl
from jax.experimental.pallas import tpu as pltpu
from jax.sharding import PartitionSpec as P

HD = 128
F32 = jnp.float32
BF16 = jnp.bfloat16


def features(wide):
    return jnp.where(wide > 0, wide + 1.0, jnp.exp(jnp.minimum(wide, 0.0))).astype(BF16)


def slope(wide):
    return jnp.where(wide > 0, 1.0, jnp.exp(jnp.minimum(wide, 0.0)))


def dot(a, b, contract):
    return lax.dot_general(a, b, (contract, ((), ())), preferred_element_type=F32)


NN = ((1,), (0,))
NT = ((1,), (1,))
TN = ((0,), (0,))


def columns(head):
    return slice(head * HD, (head + 1) * HD)


def causal(count):
    rows = lax.broadcasted_iota(jnp.int32, (count, count), 0)
    cols = lax.broadcasted_iota(jnp.int32, (count, count), 1)
    return cols <= rows


def state_kernel(k_ref, v_ref, state_ref, norm_ref):
    for h in range(k_ref.shape[1] // HD):
        at = columns(h)
        k_feat = features(k_ref[:, at].astype(F32))
        state_ref[at, :] = dot(k_feat, v_ref[:, at], TN)
        norm_ref[h : h + 1, :] = jnp.sum(k_feat.astype(F32), axis=0, keepdims=True)


def later_kernel(q_ref, k_ref, c_ref, norm_ref, later_ref, scaled_ref, den_ref):
    mask = causal(q_ref.shape[0])
    for h in range(q_ref.shape[1] // HD):
        at = columns(h)
        q_feat = features(q_ref[:, at].astype(F32))
        k_feat = features(k_ref[:, at].astype(F32))
        scores = jnp.where(mask, dot(q_feat, k_feat, NT), 0.0)
        den = jnp.sum(scores + q_feat.astype(F32) * norm_ref[h : h + 1, :], axis=1, keepdims=True)
        scaled = (c_ref[:, at].astype(F32) / den).astype(BF16)
        den_ref[:, h : h + 1] = den
        scaled_ref[:, at] = scaled
        later_ref[at, :] = dot(q_feat, scaled, TN)


def query_kernel(
    q_ref, k_ref, v_ref, c_ref, scaled_ref, den_ref, norm_ref, state_ref,
    att_ref, qg_ref, ki_ref, vi_ref, lnorm_ref,
):
    mask = causal(q_ref.shape[0])
    for h in range(q_ref.shape[1] // HD):
        at = columns(h)
        q_wide = q_ref[:, at].astype(F32)
        q_feat = features(q_wide)
        k_feat = features(k_ref[:, at].astype(F32))
        value = v_ref[:, at]
        scaled = scaled_ref[:, at]
        den = den_ref[:, h : h + 1]
        state_low = state_ref[at, :].astype(BF16)
        scores = jnp.where(mask, dot(q_feat, k_feat, NT), 0.0)
        weights = scores.astype(BF16)
        num = dot(weights, value, NN) + dot(q_feat, state_low, NN)
        ratio = num / den
        att_ref[:, at] = ratio.astype(BF16)
        grad_den = -jnp.sum(c_ref[:, at].astype(F32) * ratio, axis=1, keepdims=True) / den
        grad_scores = dot(scaled, value, NT) + grad_den
        grad_scores = jnp.where(mask, grad_scores, 0.0).astype(BF16)
        q_lin = dot(grad_scores, k_feat, NN) + dot(scaled, state_low, NT)
        q_lin = q_lin + grad_den * norm_ref[h : h + 1, :]
        qg_ref[:, at] = (q_lin * slope(q_wide)).astype(BF16)
        lnorm_ref[h : h + 1, :] = jnp.sum(grad_den * q_feat.astype(F32), axis=0, keepdims=True)
        ki_ref[:, at] = dot(grad_scores, q_feat, TN)
        vi_ref[:, at] = dot(weights, scaled, TN)


def key_kernel(k_ref, v_ref, ki_ref, vi_ref, lnorm_ref, later_ref, kg_ref, vg_ref):
    for h in range(k_ref.shape[1] // HD):
        at = columns(h)
        k_wide = k_ref[:, at].astype(F32)
        later_low = later_ref[at, :].astype(BF16)
        k_lin = ki_ref[:, at] + dot(v_ref[:, at], later_low, NT) + lnorm_ref[h : h + 1, :]
        kg_ref[:, at] = (k_lin * slope(k_wide)).astype(BF16)
        vg_ref[:, at] = (vi_ref[:, at] + dot(features(k_wide), later_low, NN)).astype(BF16)


def call(kernel, outs, *args):
    flops = 2 * HD * HD * HD * 16
    return pl.pallas_call(
        kernel,
        out_shape=[jax.ShapeDtypeStruct(shape, kind) for shape, kind in outs],
        compiler_params=pltpu.CompilerParams(vmem_limit_bytes=48 * 1024 * 1024),
        cost_estimate=pl.CostEstimate(flops=flops, bytes_accessed=4 << 20, transcendentals=0),
    )(*args)


def bits(axis):
    return (lax.axis_size(axis) - 1).bit_length()


def swap(part, axis, bit):
    return lax.ppermute(part, axis, [(i, i ^ (1 << bit)) for i in range(lax.axis_size(axis))])


def is_late(axis, bit, backward):
    set_bit = (lax.axis_index(axis) >> bit) & 1
    return set_bit == (0 if backward else 1)


def scan_small(part, backward):
    before = jnp.zeros_like(part)
    levels = [("inner", b) for b in range(bits("inner"))] + [("outer", b) for b in range(bits("outer"))]
    for axis, bit in levels:
        got = swap(part, axis, bit)
        before = before + jnp.where(is_late(axis, bit, backward), got, 0.0)
        part = part + got
    return before


def scan_large(part, backward):
    halving = [("inner", b) for b in range(bits("inner"))] + [("outer", 0)]
    doubling = [("outer", b) for b in range(1, bits("outer"))]
    lows = []
    for axis, bit in halving:
        late = is_late(axis, bit, backward)
        half = part.shape[0] // 2
        first, second = part[:half], part[half:]
        mine = jnp.where(late, second, first)
        got = swap(jnp.where(late, first, second), axis, bit)
        lows.append(jnp.where(late, got, mine))
        part = mine + got
    before = jnp.zeros_like(part)
    for axis, bit in doubling:
        got = swap(part, axis, bit)
        before = before + jnp.where(is_late(axis, bit, backward), got, 0.0)
        part = part + got
    for (axis, bit), low in zip(reversed(halving), reversed(lows)):
        late = is_late(axis, bit, backward)
        both = before + low
        mine = jnp.where(late, both, before)
        got = swap(jnp.where(late, before, both), axis, bit)
        first = jnp.where(late, got, mine)
        second = jnp.where(late, mine, got)
        before = jnp.concatenate([first, second])
    return before


def scan_chunks(part, backward, chunks):
    size = part.shape[0] // chunks
    return jnp.concatenate([scan_large(part[i * size : (i + 1) * size], backward) for i in range(chunks)])


def per_device(queries, keys, values, cotangent):
    tokens, width = queries.shape
    heads = width // HD
    flat, square, small = (tokens, width), (width, HD), (heads, HD)
    local_state, local_norm = call(state_kernel, [(square, F32), (small, F32)], keys, values)
    normal = scan_small(local_norm, False)
    state = scan_chunks(local_state, False, 2)
    later_local, scaled, den = call(
        later_kernel, [(square, F32), (flat, BF16), ((tokens, HD), F32)], queries, keys, cotangent, normal
    )
    later = scan_chunks(later_local, True, 2)
    attended, query_grad, k_intra, v_intra, local_lnorm = call(
        query_kernel,
        [(flat, BF16), (flat, BF16), (flat, F32), (flat, F32), (small, F32)],
        queries, keys, values, cotangent, scaled, den, normal, state,
    )
    later_norm = scan_small(local_lnorm, True)
    key_grad, value_grad = call(
        key_kernel, [(flat, BF16), (flat, BF16)], keys, values, k_intra, v_intra, later_norm, later
    )
    return attended, query_grad, key_grad, value_grad


def solution(mesh):
    rows = P(("outer", "inner"), None)
    return jax.shard_map(
        per_device, mesh=mesh, in_specs=(rows,) * 4, out_specs=(rows,) * 4, check_vma=False
    )
```

time: 275 us -> 147 us (0.53)
  blocking collectives: 103 us -> 0 us
  other arithmetic: 34.5 us -> 10.9 us
  starting transfers between devices: 28.1 us -> 44.4 us
  matrix products: 16.1 us -> 0 us
  Pallas kernels: 0 us -> 14.4 us
  between operations: 14.1 us -> 1.16 us
  local copies, waits for them, and re-layouts: 16.8 us -> 8.65 us
  waiting for transfers between devices: 59.7 us -> 66.6 us
    all_gather x4 -> x0, blocking collectives: 71.5 us -> none  [the longest x2 53.7 us: carry_states(): spread = lax.all_gather(before, 'inner', axis=0, tiled=True)]
    ppermute x0 -> x42, waiting for transfers between devices: none -> 66.6 us  [swap(): lax.ppermute(part, axis, [(i, i ^ 1 << bit) for i in range(lax.axis_size(...]
    all_to_all x7 -> x0, waiting for transfers between devices: 57.9 us -> none  [the longest x1 37 us: carry_states(): lax.all_to_all(parts[0], 'inner', split_axis=0, concat_axis=0, tiled=True)]
    ppermute x0 -> x42, starting transfers between devices: none -> 44.4 us  [swap(): lax.ppermute(part, axis, [(i, i ^ 1 << bit) for i in range(lax.axis_size(...]
    all_to_all x1 -> x0, blocking collectives: 31.8 us -> none  [carry_states(): lax.all_to_all(parts[0], 'inner', split_axis=0, concat_axis=0, tiled=True)]
    all_to_all x7 -> x0, starting transfers between devices: 28 us -> none  [the longest x2 9.66 us: carry_states(): lax.all_to_all(flat_within[0], 'inner', split_axis=0, concat_axis=0, tile...]
    select_n x34 -> x38, other arithmetic: 22.4 us -> 2.02 us  [the longest x10 0.99 us: scan_large(): got = swap(jnp.where(late, first, second), axis, bit)]
    dot_general x14 -> x0, matrix products: 16.1 us -> none  [the longest x1 2.66 us: per_device(): jnp.einsum('hts,she->the', weights, value_rows, preferred_element_type=f32)]
  transfers between devices with their start and end apart: 11 -> 42, of which waited for: 4 -> 21; matrix products, arithmetic and copies ran while one was open for 18% -> 7% of each run, Pallas kernels for 0% -> 8%
where the time goes in v1:
time: 147 us; the launch traced here: 146 us
  waiting for transfers between devices  66.6 us (45%)
  starting transfers between devices  44.4 us (30%)
  Pallas kernels  14.4 us (10%)
  other arithmetic  10.9 us (7%)
  local copies, waits for them, and re-layouts  8.65 us (6%)
    ppermute x42, waiting for transfers between devices, swap(): lax.ppermute(part, axis, [(i, i ^ 1 << bit) for i in range(lax.axis_size(...  66.6 us
    ppermute x42, starting transfers between devices, swap(): lax.ppermute(part, axis, [(i, i ^ 1 << bit) for i in range(lax.axis_size(...  44.4 us
    pallas_call x4, Pallas kernels, call(): pl.pallas_call(kernel, out_shape=[jax.ShapeDtypeStruct(shape, kind) for s...  14.4 us
    unnamed x70, local copies, waits for them, and re-layouts  8.65 us
    add x10, other arithmetic, scan_large(): part = mine + got  6.3 us
  transfers between devices with their start and end apart: 42, of which 21 were waited for; matrix products, arithmetic and copies ran while one was open for 7% of the time, Pallas kernels for 8%

profile of v1, /device:TPU:0, one launch (start us, length us, event | category | flops | bytes accessed | tf_op | source)
XLA Modules:
  0.0 146.1 jit_solution(16009328020737560882)
XLA Ops:
  3.3 3.1 %collective-permute-start = (f32[16,128]{1,0:T(8,128)S(1)}, f32[16,128]{1,0:T(8,128)S(1)}, u32[]{:S(2)}, u32[]{:S(2)}) collective-permute-start(f32[16,128]{1,0:T(8,128)S(1)} %get-tuple-element.16), channel_id=1, source_target_pairs={{0,1},{1,0},{2,3},{3,2},{4,5},{5,4},{6,7},{7,6},{8,9},{9,8},{10,11... | collective-permute-start | bytes 24584 | tf_op jit(solution)/shard_map/ppermute | solution.py:119
  6.4 1.6 %collective-permute-done = f32[16,128]{1,0:T(8,128)S(1)} collective-permute-done((f32[16,128]{1,0:T(8,128)S(1)}, f32[16,128]{1,0:T(8,128)S(1)}, u32[]{:S(2)}, u32[]{:S(2)}) %collective-permute-start) | collective-permute-done | bytes 8224 | tf_op jit(solution)/shard_map/ppermute | solution.py:119
  8.0 3.0 %collective-permute-start.1 = (f32[16,128]{1,0:T(8,128)S(1)}, f32[16,128]{1,0:T(8,128)S(1)}, u32[]{:S(2)}, u32[]{:S(2)}) collective-permute-start(f32[16,128]{1,0:T(8,128)S(1)} %add.144), channel_id=1, source_target_pairs={{0,2},{1,3},{2,0},{3,1},{4,6},{5,7},{6,4},{7,5},{8,10},{9,11},{10,... | collective-permute-start | bytes 24584 | tf_op jit(solution)/shard_map/ppermute | solution.py:119
  11.1 1.6 %collective-permute-done.1 = f32[16,128]{1,0:T(8,128)S(1)} collective-permute-done((f32[16,128]{1,0:T(8,128)S(1)}, f32[16,128]{1,0:T(8,128)S(1)}, u32[]{:S(2)}, u32[]{:S(2)}) %collective-permute-start.1) | collective-permute-done | bytes 8224 | tf_op jit(solution)/shard_map/ppermute | solution.py:119
  13.9 1.8 %collective-permute-start.3 = (f32[16,128]{1,0:T(8,128)S(1)}, f32[16,128]{1,0:T(8,128)S(1)}, u32[]{:S(2)}, u32[]{:S(2)}) collective-permute-start(f32[16,128]{1,0:T(8,128)S(1)} %add.148), channel_id=1, source_target_pairs={{0,8},{4,12},{8,0},{12,4},{16,24},{20,28},{24,16},{28,20},{1,9},{5... | collective-permute-start | bytes 24584 | tf_op jit(solution)/shard_map/ppermute | solution.py:119
  15.7 1.8 %collective-permute-done.3 = f32[16,128]{1,0:T(8,128)S(1)} collective-permute-done((f32[16,128]{1,0:T(8,128)S(1)}, f32[16,128]{1,0:T(8,128)S(1)}, u32[]{:S(2)}, u32[]{:S(2)}) %collective-permute-start.3) | collective-permute-done | bytes 8224 | tf_op jit(solution)/shard_map/ppermute | solution.py:119
  17.5 1.9 %collective-permute-start.4 = (f32[16,128]{1,0:T(8,128)S(1)}, f32[16,128]{1,0:T(8,128)S(1)}, u32[]{:S(2)}, u32[]{:S(2)}) collective-permute-start(f32[16,128]{1,0:T(8,128)S(1)} %add.150), channel_id=1, source_target_pairs={{0,16},{4,20},{8,24},{12,28},{16,0},{20,4},{24,8},{28,12},{1,17},{... | collective-permute-start | bytes 24584 | tf_op jit(solution)/shard_map/ppermute | solution.py:119
  20.2 1.6 %collective-permute-start.5 = (f32[512,128]{1,0:T(8,128)}, f32[512,128]{1,0:T(8,128)}, u32[]{:S(2)}, u32[]{:S(2)}) collective-permute-start(f32[512,128]{1,0:T(8,128)} %get-tuple-element.64), channel_id=1, source_target_pairs={{0,1},{1,0},{2,3},{3,2},{4,5},{5,4},{6,7},{7,6},{8,9},{9,8},{10,11... | collective-permute-start | bytes 786440 | tf_op jit(solution)/shard_map/ppermute | solution.py:119
  22.3 4.5 %shard_map.76 = (f32[2048,128]{1,0:T(8,128)S(1)}, bf16[128,2048]{1,0:T(8,128)(2,1)S(1)}, f32[128,128]{1,0:T(8,128)S(1)}) custom-call(bf16[128,2048]{1,0:T(8,128)(2,1)S(1)} %copy-done.4, bf16[128,2048]{1,0:T(8,128)(2,1)S(1)} %copy-done.1, bf16[128,2048]{1,0:T(8,128)(2,1)S(1)} %copy-done.5, f32[16,128]{1,0:T(8,128)S(1)} %select_add_fusion.5.norm_ref), custom_call_target="tpu_custom_call" | custom-call | flops 67108864 | bytes 4194304 | tf_op jit(solution)/shard_map/pallas_call | solution.py:106
  26.8 1.6 %collective-permute-start.26 = (f32[512,128]{1,0:T(8,128)S(1)}, f32[512,128]{1,0:T(8,128)S(1)}, u32[]{:S(2)}, u32[]{:S(2)}) collective-permute-start(f32[512,128]{1,0:T(8,128)S(1)} %get-tuple-element.56), channel_id=1, source_target_pairs={{0,1},{1,0},{2,3},{3,2},{4,5},{5,4},{6,7},{7,6},{8,9},{9,8},{10,11... | collective-permute-start | bytes 786440 | tf_op jit(solution)/shard_map/ppermute | solution.py:119
  29.8 5.6 %collective-permute-done.13 = f32[512,128]{1,0:T(8,128)} collective-permute-done((f32[512,128]{1,0:T(8,128)}, f32[512,128]{1,0:T(8,128)}, u32[]{:S(2)}, u32[]{:S(2)}) %collective-permute-start.13) | collective-permute-done | bytes 262176 | tf_op jit(solution)/shard_map/ppermute | solution.py:119
  35.4 1.9 %fusion.9 = (f32[512,128]{1,0:T(8,128)S(1)}, f32[512,128]{1,0:T(8,128)}, f32[512,128]{1,0:T(8,128)S(1)}, f32[512,128]{1,0:T(8,128)}) fusion(f32[512,128]{1,0:T(8,128)} %collective-permute-done.5, f32[2048,128]{1,0:T(8,128)S(1)} %get-tuple-element.19, pred[]{:T(512)S(6)} %eq.20, f32[512,128]{1,0:T(8,128)} %collective-permute-done.13), kind=kLoop, calls=%fused_computation.109 | loop fusion | flops 262144 | bytes 2621441 | tf_op jit(solution)/shard_map/add | solution.py:148
  37.3 2.7 %collective-permute-start.14 = (f32[256,128]{1,0:T(8,128)S(1)}, f32[256,128]{1,0:T(8,128)S(1)}, u32[]{:S(2)}, u32[]{:S(2)}) collective-permute-start(f32[256,128]{1,0:T(8,128)S(1)} %slice_select_fusion.12), channel_id=1, source_target_pairs={{0,2},{1,3},{2,0},{3,1},{4,6},{5,7},{6,4},{7,5},{8,10},{9,11},{10,... | collective-permute-start | bytes 393224 | tf_op jit(solution)/shard_map/ppermute | solution.py:119
  40.4 5.3 %collective-permute-done.26 = f32[512,128]{1,0:T(8,128)S(1)} collective-permute-done((f32[512,128]{1,0:T(8,128)S(1)}, f32[512,128]{1,0:T(8,128)S(1)}, u32[]{:S(2)}, u32[]{:S(2)}) %collective-permute-start.26) | collective-permute-done | bytes 262176 | tf_op jit(solution)/shard_map/ppermute | solution.py:119
  45.7 4.1 %collective-permute-done.34 = f32[512,128]{1,0:T(8,128)S(1)} collective-permute-done((f32[512,128]{1,0:T(8,128)S(1)}, f32[512,128]{1,0:T(8,128)S(1)}, u32[]{:S(2)}, u32[]{:S(2)}) %collective-permute-start.34) | collective-permute-done | bytes 262176 | tf_op jit(solution)/shard_map/ppermute | solution.py:119
  52.1 1.8 %collective-permute-start.27 = (f32[256,128]{1,0:T(8,128)S(1)}, f32[256,128]{1,0:T(8,128)S(1)}, u32[]{:S(2)}, u32[]{:S(2)}) collective-permute-start(f32[256,128]{1,0:T(8,128)S(1)} %slice_select_fusion.10), channel_id=1, source_target_pairs={{0,2},{1,3},{2,0},{3,1},{4,6},{5,7},{6,4},{7,5},{8,10},{9,11},{10,... | collective-permute-start | bytes 393224 | tf_op jit(solution)/shard_map/ppermute | solution.py:119
  56.0 6.0 %collective-permute-done.35 = f32[256,128]{1,0:T(8,128)S(1)} collective-permute-done((f32[256,128]{1,0:T(8,128)S(1)}, f32[256,128]{1,0:T(8,128)S(1)}, u32[]{:S(2)}, u32[]{:S(2)}) %collective-permute-start.35) | collective-permute-done | bytes 131104 | tf_op jit(solution)/shard_map/ppermute | solution.py:119
  72.5 1.6 %collective-permute-start.9 = (f32[128,128]{1,0:T(8,128)S(1)}, f32[128,128]{1,0:T(8,128)S(1)}, u32[]{:S(2)}, u32[]{:S(2)}) collective-permute-start(f32[128,128]{1,0:T(8,128)S(1)} %add.155), channel_id=1, source_target_pairs={{0,16},{4,20},{8,24},{12,28},{16,0},{20,4},{24,8},{28,12},{1,17},{... | collective-permute-start | bytes 196616 | tf_op jit(solution)/shard_map/ppermute | solution.py:119
  76.4 1.6 %collective-permute-start.30 = (f32[128,128]{1,0:T(8,128)S(1)}, f32[128,128]{1,0:T(8,128)S(1)}, u32[]{:S(2)}, u32[]{:S(2)}) collective-permute-start(f32[128,128]{1,0:T(8,128)S(1)} %add.179), channel_id=1, source_target_pairs={{0,16},{4,20},{8,24},{12,28},{16,0},{20,4},{24,8},{28,12},{1,17},{... | collective-permute-start | bytes 196616 | tf_op jit(solution)/shard_map/ppermute | solution.py:119
  83.0 3.0 %collective-permute-start.11 = (f32[256,128]{1,0:T(8,128)S(1)}, f32[256,128]{1,0:T(8,128)S(1)}, u32[]{:S(2)}, u32[]{:S(2)}) collective-permute-start(f32[256,128]{1,0:T(8,128)S(1)} %add_select_fusion.15), channel_id=1, source_target_pairs={{0,2},{1,3},{2,0},{3,1},{4,6},{5,7},{6,4},{7,5},{8,10},{9,11},{10,... | collective-permute-start | bytes 393224 | tf_op jit(solution)/shard_map/ppermute | solution.py:119
  87.9 8.7 %collective-permute-done.19 = f32[256,128]{1,0:T(8,128)S(1)} collective-permute-done((f32[256,128]{1,0:T(8,128)S(1)}, f32[256,128]{1,0:T(8,128)S(1)}, u32[]{:S(2)}, u32[]{:S(2)}) %collective-permute-start.19) | collective-permute-done | bytes 131104 | tf_op jit(solution)/shard_map/ppermute | solution.py:119
  96.8 2.6 %collective-permute-done.11 = f32[256,128]{1,0:T(8,128)S(1)} collective-permute-done((f32[256,128]{1,0:T(8,128)S(1)}, f32[256,128]{1,0:T(8,128)S(1)}, u32[]{:S(2)}, u32[]{:S(2)}) %collective-permute-start.11) | collective-permute-done | bytes 131104 | tf_op jit(solution)/shard_map/ppermute | solution.py:119
  100.3 2.7 %collective-permute-start.32 = (f32[256,128]{1,0:T(8,128)S(1)}, f32[256,128]{1,0:T(8,128)S(1)}, u32[]{:S(2)}, u32[]{:S(2)}) collective-permute-start(f32[256,128]{1,0:T(8,128)S(1)} %add_select_fusion.11), channel_id=1, source_target_pairs={{0,2},{1,3},{2,0},{3,1},{4,6},{5,7},{6,4},{7,5},{8,10},{9,11},{10,... | collective-permute-start | bytes 393224 | tf_op jit(solution)/shard_map/ppermute | solution.py:119
  103.1 7.6 %collective-permute-done.20 = f32[512,128]{1,0:T(8,128)S(1)} collective-permute-done((f32[512,128]{1,0:T(8,128)S(1)}, f32[512,128]{1,0:T(8,128)S(1)}, u32[]{:S(2)}, u32[]{:S(2)}) %collective-permute-start.20) | collective-permute-done | bytes 262176 | tf_op jit(solution)/shard_map/ppermute | solution.py:119
  110.7 5.4 %collective-permute-done.12 = f32[512,128]{1,0:T(8,128)S(1)} collective-permute-done((f32[512,128]{1,0:T(8,128)S(1)}, f32[512,128]{1,0:T(8,128)S(1)}, u32[]{:S(2)}, u32[]{:S(2)}) %collective-permute-start.12) | collective-permute-done | bytes 262176 | tf_op jit(solution)/shard_map/ppermute | solution.py:119
  117.3 7.7 %shard_map.77 = (bf16[128,2048]{1,0:T(8,128)(2,1)}, bf16[128,2048]{1,0:T(8,128)(2,1)}, f32[128,2048]{1,0:T(8,128)S(1)}, f32[128,2048]{1,0:T(8,128)S(1)}, f32[16,128]{1,0:T(8,128)S(1)}) custom-call(bf16[128,2048]{1,0:T(8,128)(2,1)S(1)} %copy-done.4, bf16[128,2048]{1,0:T(8,128)(2,1)S(1)} %copy-done.1, bf16[128,2048]{1,0:T(8,128)(2,1)S(1)} %copy-done.3, ...), custom_call_target="tpu_custom_call" | custom-call | flops 67108864 | bytes 4194304 | tf_op jit(solution)/shard_map/pallas_call | solution.py:106
  125.5 3.1 %collective-permute-done.21 = f32[16,128]{1,0:T(8,128)S(1)} collective-permute-done((f32[16,128]{1,0:T(8,128)S(1)}, f32[16,128]{1,0:T(8,128)S(1)}, u32[]{:S(2)}, u32[]{:S(2)}) %collective-permute-start.21) | collective-permute-done | bytes 8224 | tf_op jit(solution)/shard_map/ppermute | solution.py:119
  130.0 2.1 %collective-permute-start.41 = (f32[512,128]{1,0:T(8,128)S(1)}, f32[512,128]{1,0:T(8,128)S(1)}, u32[]{:S(2)}, u32[]{:S(2)}) collective-permute-start(f32[512,128]{1,0:T(8,128)S(1)} %add_select_fusion.1), channel_id=1, source_target_pairs={{0,1},{1,0},{2,3},{3,2},{4,5},{5,4},{6,7},{7,6},{8,9},{9,8},{10,11... | collective-permute-start | bytes 786440 | tf_op jit(solution)/shard_map/ppermute | solution.py:119
  136.5 1.6 %collective-permute-done.24 = f32[16,128]{1,0:T(8,128)S(1)} collective-permute-done((f32[16,128]{1,0:T(8,128)S(1)}, f32[16,128]{1,0:T(8,128)S(1)}, u32[]{:S(2)}, u32[]{:S(2)}) %collective-permute-start.24) | collective-permute-done | bytes 8224 | tf_op jit(solution)/shard_map/ppermute | solution.py:119
  138.2 1.5 %collective-permute-start.25 = (f32[16,128]{1,0:T(8,128)S(1)}, f32[16,128]{1,0:T(8,128)S(1)}, u32[]{:S(2)}, u32[]{:S(2)}) collective-permute-start(f32[16,128]{1,0:T(8,128)S(1)} %add.174), channel_id=1, source_target_pairs={{0,16},{4,20},{8,24},{12,28},{16,0},{20,4},{24,8},{28,12},{1,17},{... | collective-permute-start | bytes 24584 | tf_op jit(solution)/shard_map/ppermute | solution.py:119
  139.7 4.5 %collective-permute-done.33 = f32[512,128]{1,0:T(8,128)S(1)} collective-permute-done((f32[512,128]{1,0:T(8,128)S(1)}, f32[512,128]{1,0:T(8,128)S(1)}, u32[]{:S(2)}, u32[]{:S(2)}) %collective-permute-start.33) | collective-permute-done | bytes 262176 | tf_op jit(solution)/shard_map/ppermute | solution.py:119
  144.4 1.7 %shard_map.78 = (bf16[128,2048]{1,0:T(8,128)(2,1)}, bf16[128,2048]{1,0:T(8,128)(2,1)}) custom-call(bf16[128,2048]{1,0:T(8,128)(2,1)S(1)} %copy-done.1, bf16[128,2048]{1,0:T(8,128)(2,1)S(1)} %copy-done.3, f32[128,2048]{1,0:T(8,128)S(1)} %get-tuple-element.22.ki_ref, f32[128,2048]{1,0:T(8,128)S(1)} %get-tuple-element.23.vi_ref, ...), custom_call_target="tpu_custom_call" | custom-call | flops 67108864 | bytes 4194304 | tf_op jit(solution)/shard_map/pallas_call | solution.py:106
  (190 shorter events, 39.5 us)
Async XLA Ops:
  3.3 4.7 %collective-permute-start = (f32[16,128]{1,0:T(8,128)S(1)}, f32[16,128]{1,0:T(8,128)S(1)}, u32[]{:S(2)}, u32[]{:S(2)}) collective-permute-start(f32[16,128]{1,0:T(8,128)S(1)} %get-tuple-element.16), channel_id=1, source_target_pairs={{0,1},{1,0},{2,3},{3,2},{4,5},{5,4},{6,7},{7,6},{8,9},{9,8},{10,11... | collective-permute-start | bytes 24584 | tf_op jit(solution)/shard_map/ppermute | solution.py:119
  17.5 4.7 %collective-permute-start.4 = (f32[16,128]{1,0:T(8,128)S(1)}, f32[16,128]{1,0:T(8,128)S(1)}, u32[]{:S(2)}, u32[]{:S(2)}) collective-permute-start(f32[16,128]{1,0:T(8,128)S(1)} %add.150), channel_id=1, source_target_pairs={{0,16},{4,20},{8,24},{12,28},{16,0},{20,4},{24,8},{28,12},{1,17},{... | collective-permute-start | bytes 24584 | tf_op jit(solution)/shard_map/ppermute | solution.py:119
  20.2 9.6 %collective-permute-start.5 = (f32[512,128]{1,0:T(8,128)}, f32[512,128]{1,0:T(8,128)}, u32[]{:S(2)}, u32[]{:S(2)}) collective-permute-start(f32[512,128]{1,0:T(8,128)} %get-tuple-element.64), channel_id=1, source_target_pairs={{0,1},{1,0},{2,3},{3,2},{4,5},{5,4},{6,7},{7,6},{8,9},{9,8},{10,11... | collective-permute-start | bytes 786440 | tf_op jit(solution)/shard_map/ppermute | solution.py:119
  21.8 13.6 %collective-permute-start.13 = (f32[512,128]{1,0:T(8,128)}, f32[512,128]{1,0:T(8,128)}, u32[]{:S(2)}, u32[]{:S(2)}) collective-permute-start(f32[512,128]{1,0:T(8,128)} %get-tuple-element.65), channel_id=1, source_target_pairs={{0,1},{1,0},{2,3},{3,2},{4,5},{5,4},{6,7},{7,6},{8,9},{9,8},{10,11... | collective-permute-start | bytes 786440 | tf_op jit(solution)/shard_map/ppermute | solution.py:119
  26.8 18.9 %collective-permute-start.26 = (f32[512,128]{1,0:T(8,128)S(1)}, f32[512,128]{1,0:T(8,128)S(1)}, u32[]{:S(2)}, u32[]{:S(2)}) collective-permute-start(f32[512,128]{1,0:T(8,128)S(1)} %get-tuple-element.56), channel_id=1, source_target_pairs={{0,1},{1,0},{2,3},{3,2},{4,5},{5,4},{6,7},{7,6},{8,9},{9,8},{10,11... | collective-permute-start | bytes 786440 | tf_op jit(solution)/shard_map/ppermute | solution.py:119
  28.5 21.4 %collective-permute-start.34 = (f32[512,128]{1,0:T(8,128)S(1)}, f32[512,128]{1,0:T(8,128)S(1)}, u32[]{:S(2)}, u32[]{:S(2)}) collective-permute-start(f32[512,128]{1,0:T(8,128)S(1)} %get-tuple-element.57), channel_id=1, source_target_pairs={{0,1},{1,0},{2,3},{3,2},{4,5},{5,4},{6,7},{7,6},{8,9},{9,8},{10,11... | collective-permute-start | bytes 786440 | tf_op jit(solution)/shard_map/ppermute | solution.py:119
  37.3 16.5 %collective-permute-start.14 = (f32[256,128]{1,0:T(8,128)S(1)}, f32[256,128]{1,0:T(8,128)S(1)}, u32[]{:S(2)}, u32[]{:S(2)}) collective-permute-start(f32[256,128]{1,0:T(8,128)S(1)} %slice_select_fusion.12), channel_id=1, source_target_pairs={{0,2},{1,3},{2,0},{3,1},{4,6},{5,7},{6,4},{7,5},{8,10},{9,11},{10,... | collective-permute-start | bytes 393224 | tf_op jit(solution)/shard_map/ppermute | solution.py:119
  40.0 14.7 %collective-permute-start.6 = (f32[256,128]{1,0:T(8,128)S(1)}, f32[256,128]{1,0:T(8,128)S(1)}, u32[]{:S(2)}, u32[]{:S(2)}) collective-permute-start(f32[256,128]{1,0:T(8,128)S(1)} %slice_select_fusion.14), channel_id=1, source_target_pairs={{0,2},{1,3},{2,0},{3,1},{4,6},{5,7},{6,4},{7,5},{8,10},{9,11},{10,... | collective-permute-start | bytes 393224 | tf_op jit(solution)/shard_map/ppermute | solution.py:119
  50.8 11.2 %collective-permute-start.35 = (f32[256,128]{1,0:T(8,128)S(1)}, f32[256,128]{1,0:T(8,128)S(1)}, u32[]{:S(2)}, u32[]{:S(2)}) collective-permute-start(f32[256,128]{1,0:T(8,128)S(1)} %slice_select_fusion.8), channel_id=1, source_target_pairs={{0,2},{1,3},{2,0},{3,1},{4,6},{5,7},{6,4},{7,5},{8,10},{9,11},{10,... | collective-permute-start | bytes 393224 | tf_op jit(solution)/shard_map/ppermute | solution.py:119
  52.1 11.3 %collective-permute-start.27 = (f32[256,128]{1,0:T(8,128)S(1)}, f32[256,128]{1,0:T(8,128)S(1)}, u32[]{:S(2)}, u32[]{:S(2)}) collective-permute-start(f32[256,128]{1,0:T(8,128)S(1)} %slice_select_fusion.10), channel_id=1, source_target_pairs={{0,2},{1,3},{2,0},{3,1},{4,6},{5,7},{6,4},{7,5},{8,10},{9,11},{10,... | collective-permute-start | bytes 393224 | tf_op jit(solution)/shard_map/ppermute | solution.py:119
  54.6 9.6 %collective-permute-start.15 = (f32[128,128]{1,0:T(8,128)S(1)}, f32[128,128]{1,0:T(8,128)S(1)}, u32[]{:S(2)}, u32[]{:S(2)}) collective-permute-start(f32[128,128]{1,0:T(8,128)S(1)} %slice_select_fusion.20), channel_id=1, source_target_pairs={{0,4},{4,0},{8,12},{12,8},{16,20},{20,16},{24,28},{28,24},{1,5},{5... | collective-permute-start | bytes 196616 | tf_op jit(solution)/shard_map/ppermute | solution.py:119
  55.4 10.9 %collective-permute-start.7 = (f32[128,128]{1,0:T(8,128)S(1)}, f32[128,128]{1,0:T(8,128)S(1)}, u32[]{:S(2)}, u32[]{:S(2)}) collective-permute-start(f32[128,128]{1,0:T(8,128)S(1)} %slice_select_fusion.22), channel_id=1, source_target_pairs={{0,4},{4,0},{8,12},{12,8},{16,20},{20,16},{24,28},{28,24},{1,5},{5... | collective-permute-start | bytes 196616 | tf_op jit(solution)/shard_map/ppermute | solution.py:119
  62.7 4.7 %collective-permute-start.36 = (f32[128,128]{1,0:T(8,128)S(1)}, f32[128,128]{1,0:T(8,128)S(1)}, u32[]{:S(2)}, u32[]{:S(2)}) collective-permute-start(f32[128,128]{1,0:T(8,128)S(1)} %slice_select_fusion.16), channel_id=1, source_target_pairs={{0,4},{4,0},{8,12},{12,8},{16,20},{20,16},{24,28},{28,24},{1,5},{5... | collective-permute-start | bytes 196616 | tf_op jit(solution)/shard_map/ppermute | solution.py:119
  64.1 6.1 %collective-permute-start.28 = (f32[128,128]{1,0:T(8,128)S(1)}, f32[128,128]{1,0:T(8,128)S(1)}, u32[]{:S(2)}, u32[]{:S(2)}) collective-permute-start(f32[128,128]{1,0:T(8,128)S(1)} %slice_select_fusion.18), channel_id=1, source_target_pairs={{0,4},{4,0},{8,12},{12,8},{16,20},{20,16},{24,28},{28,24},{1,5},{5... | collective-permute-start | bytes 196616 | tf_op jit(solution)/shard_map/ppermute | solution.py:119
  64.8 6.6 %collective-permute-start.16 = (f32[128,128]{1,0:T(8,128)S(1)}, f32[128,128]{1,0:T(8,128)S(1)}, u32[]{:S(2)}, u32[]{:S(2)}) collective-permute-start(f32[128,128]{1,0:T(8,128)S(1)} %fusion.1), channel_id=1, source_target_pairs={{0,8},{4,12},{8,0},{12,4},{16,24},{20,28},{24,16},{28,20},{1,9},{5... | collective-permute-start | bytes 196616 | tf_op jit(solution)/shard_map/ppermute | solution.py:119
  66.9 5.6 %collective-permute-start.8 = (f32[128,128]{1,0:T(8,128)S(1)}, f32[128,128]{1,0:T(8,128)S(1)}, u32[]{:S(2)}, u32[]{:S(2)}) collective-permute-start(f32[128,128]{1,0:T(8,128)S(1)} %fusion), channel_id=1, source_target_pairs={{0,8},{4,12},{8,0},{12,4},{16,24},{20,28},{24,16},{28,20},{1,9},{5... | collective-permute-start | bytes 196616 | tf_op jit(solution)/shard_map/ppermute | solution.py:119
  68.7 5.4 %collective-permute-start.37 = (f32[128,128]{1,0:T(8,128)}, f32[128,128]{1,0:T(8,128)S(1)}, u32[]{:S(2)}, u32[]{:S(2)}) collective-permute-start(f32[128,128]{1,0:T(8,128)} %fusion.3), channel_id=1, source_target_pairs={{0,8},{4,12},{8,0},{12,4},{16,24},{20,28},{24,16},{28,20},{1,9},{5... | collective-permute-start | bytes 196616 | tf_op jit(solution)/shard_map/ppermute | solution.py:119
  70.9 4.7 %collective-permute-start.29 = (f32[128,128]{1,0:T(8,128)}, f32[128,128]{1,0:T(8,128)S(1)}, u32[]{:S(2)}, u32[]{:S(2)}) collective-permute-start(f32[128,128]{1,0:T(8,128)} %fusion.2), channel_id=1, source_target_pairs={{0,8},{4,12},{8,0},{12,4},{16,24},{20,28},{24,16},{28,20},{1,9},{5... | collective-permute-start | bytes 196616 | tf_op jit(solution)/shard_map/ppermute | solution.py:119
  72.0 6.0 %collective-permute-start.17 = (f32[128,128]{1,0:T(8,128)}, f32[128,128]{1,0:T(8,128)S(1)}, u32[]{:S(2)}, u32[]{:S(2)}) collective-permute-start(f32[128,128]{1,0:T(8,128)} %add.163), channel_id=1, source_target_pairs={{0,16},{4,20},{8,24},{12,28},{16,0},{20,4},{24,8},{28,12},{1,17},{... | collective-permute-start | bytes 196616 | tf_op jit(solution)/shard_map/ppermute | solution.py:119
  72.5 5.6 %collective-permute-start.9 = (f32[128,128]{1,0:T(8,128)S(1)}, f32[128,128]{1,0:T(8,128)S(1)}, u32[]{:S(2)}, u32[]{:S(2)}) collective-permute-start(f32[128,128]{1,0:T(8,128)S(1)} %add.155), channel_id=1, source_target_pairs={{0,16},{4,20},{8,24},{12,28},{16,0},{20,4},{24,8},{28,12},{1,17},{... | collective-permute-start | bytes 196616 | tf_op jit(solution)/shard_map/ppermute | solution.py:119
  79.4 6.6 %collective-permute-start.39 = (f32[128,128]{1,0:T(8,128)S(1)}, f32[128,128]{1,0:T(8,128)S(1)}, u32[]{:S(2)}, u32[]{:S(2)}) collective-permute-start(f32[128,128]{1,0:T(8,128)S(1)} %add_select_fusion.17), channel_id=1, source_target_pairs={{0,4},{4,0},{8,12},{12,8},{16,20},{20,16},{24,28},{28,24},{1,5},{5... | collective-permute-start | bytes 196616 | tf_op jit(solution)/shard_map/ppermute | solution.py:119
  80.8 7.0 %collective-permute-start.31 = (f32[128,128]{1,0:T(8,128)S(1)}, f32[128,128]{1,0:T(8,128)S(1)}, u32[]{:S(2)}, u32[]{:S(2)}) collective-permute-start(f32[128,128]{1,0:T(8,128)S(1)} %add_select_fusion.19), channel_id=1, source_target_pairs={{0,4},{4,0},{8,12},{12,8},{16,20},{20,16},{24,28},{28,24},{1,5},{5... | collective-permute-start | bytes 196616 | tf_op jit(solution)/shard_map/ppermute | solution.py:119
  81.9 14.6 %collective-permute-start.19 = (f32[256,128]{1,0:T(8,128)S(1)}, f32[256,128]{1,0:T(8,128)S(1)}, u32[]{:S(2)}, u32[]{:S(2)}) collective-permute-start(f32[256,128]{1,0:T(8,128)S(1)} %add_select_fusion.13), channel_id=1, source_target_pairs={{0,2},{1,3},{2,0},{3,1},{4,6},{5,7},{6,4},{7,5},{8,10},{9,11},{10,... | collective-permute-start | bytes 393224 | tf_op jit(solution)/shard_map/ppermute | solution.py:119
  83.0 16.4 %collective-permute-start.11 = (f32[256,128]{1,0:T(8,128)S(1)}, f32[256,128]{1,0:T(8,128)S(1)}, u32[]{:S(2)}, u32[]{:S(2)}) collective-permute-start(f32[256,128]{1,0:T(8,128)S(1)} %add_select_fusion.15), channel_id=1, source_target_pairs={{0,2},{1,3},{2,0},{3,1},{4,6},{5,7},{6,4},{7,5},{8,10},{9,11},{10,... | collective-permute-start | bytes 393224 | tf_op jit(solution)/shard_map/ppermute | solution.py:119
  87.0 38.5 %collective-permute-start.40 = (f32[256,128]{1,0:T(8,128)S(1)}, f32[256,128]{1,0:T(8,128)S(1)}, u32[]{:S(2)}, u32[]{:S(2)}) collective-permute-start(f32[256,128]{1,0:T(8,128)S(1)} %add_select_fusion.9), channel_id=1, source_target_pairs={{0,2},{1,3},{2,0},{3,1},{4,6},{5,7},{6,4},{7,5},{8,10},{9,11},{10,... | collective-permute-start | bytes 393224 | tf_op jit(solution)/shard_map/ppermute | solution.py:119
  96.7 14.0 %collective-permute-start.20 = (f32[512,128]{1,0:T(8,128)S(1)}, f32[512,128]{1,0:T(8,128)S(1)}, u32[]{:S(2)}, u32[]{:S(2)}) collective-permute-start(f32[512,128]{1,0:T(8,128)S(1)} %add_select_fusion.5), channel_id=1, source_target_pairs={{0,1},{1,0},{2,3},{3,2},{4,5},{5,4},{6,7},{7,6},{8,9},{9,8},{10,11... | collective-permute-start | bytes 786440 | tf_op jit(solution)/shard_map/ppermute | solution.py:119
  99.5 16.7 %collective-permute-start.12 = (f32[512,128]{1,0:T(8,128)S(1)}, f32[512,128]{1,0:T(8,128)S(1)}, u32[]{:S(2)}, u32[]{:S(2)}) collective-permute-start(f32[512,128]{1,0:T(8,128)S(1)} %add_select_fusion.7), channel_id=1, source_target_pairs={{0,1},{1,0},{2,3},{3,2},{4,5},{5,4},{6,7},{7,6},{8,9},{9,8},{10,11... | collective-permute-start | bytes 786440 | tf_op jit(solution)/shard_map/ppermute | solution.py:119
  100.3 33.0 %collective-permute-start.32 = (f32[256,128]{1,0:T(8,128)S(1)}, f32[256,128]{1,0:T(8,128)S(1)}, u32[]{:S(2)}, u32[]{:S(2)}) collective-permute-start(f32[256,128]{1,0:T(8,128)S(1)} %add_select_fusion.11), channel_id=1, source_target_pairs={{0,2},{1,3},{2,0},{3,1},{4,6},{5,7},{6,4},{7,5},{8,10},{9,11},{10,... | collective-permute-start | bytes 393224 | tf_op jit(solution)/shard_map/ppermute | solution.py:119
  128.6 4.7 %collective-permute-start.22 = (f32[16,128]{1,0:T(8,128)S(1)}, f32[16,128]{1,0:T(8,128)S(1)}, u32[]{:S(2)}, u32[]{:S(2)}) collective-permute-start(f32[16,128]{1,0:T(8,128)S(1)} %add.168), channel_id=1, source_target_pairs={{0,2},{1,3},{2,0},{3,1},{4,6},{5,7},{6,4},{7,5},{8,10},{9,11},{10,... | collective-permute-start | bytes 24584 | tf_op jit(solution)/shard_map/ppermute | solution.py:119
  130.0 9.7 %collective-permute-start.41 = (f32[512,128]{1,0:T(8,128)S(1)}, f32[512,128]{1,0:T(8,128)S(1)}, u32[]{:S(2)}, u32[]{:S(2)}) collective-permute-start(f32[512,128]{1,0:T(8,128)S(1)} %add_select_fusion.1), channel_id=1, source_target_pairs={{0,1},{1,0},{2,3},{3,2},{4,5},{5,4},{6,7},{7,6},{8,9},{9,8},{10,11... | collective-permute-start | bytes 786440 | tf_op jit(solution)/shard_map/ppermute | solution.py:119
  136.0 8.2 %collective-permute-start.33 = (f32[512,128]{1,0:T(8,128)S(1)}, f32[512,128]{1,0:T(8,128)S(1)}, u32[]{:S(2)}, u32[]{:S(2)}) collective-permute-start(f32[512,128]{1,0:T(8,128)S(1)} %add_select_fusion.3), channel_id=1, source_target_pairs={{0,1},{1,0},{2,3},{3,2},{4,5},{5,4},{6,7},{7,6},{8,9},{9,8},{10,11... | collective-permute-start | bytes 786440 | tf_op jit(solution)/shard_map/ppermute | solution.py:119
  138.2 6.2 %collective-permute-start.25 = (f32[16,128]{1,0:T(8,128)S(1)}, f32[16,128]{1,0:T(8,128)S(1)}, u32[]{:S(2)}, u32[]{:S(2)}) collective-permute-start(f32[16,128]{1,0:T(8,128)S(1)} %add.174), channel_id=1, source_target_pairs={{0,16},{4,20},{8,24},{12,28},{16,0},{20,4},{24,8},{28,12},{1,17},{... | collective-permute-start | bytes 24584 | tf_op jit(solution)/shard_map/ppermute | solution.py:119
  (45 other events, 146.1 us)

commit v2 on v1

v2 whole, which is shorter than its diff:
```python
import functools

import jax
import jax.numpy as jnp
from jax import lax
from jax.experimental import pallas as pl
from jax.experimental.pallas import tpu as pltpu
from jax.sharding import PartitionSpec as P

HD = 128
F32 = jnp.float32
BF16 = jnp.bfloat16


def features(wide):
    return jnp.where(wide > 0, wide + 1.0, jnp.exp(jnp.minimum(wide, 0.0))).astype(BF16)


def slope(wide):
    return jnp.where(wide > 0, 1.0, jnp.exp(jnp.minimum(wide, 0.0)))


def dot(a, b, contract):
    return lax.dot_general(a, b, (contract, ((), ())), preferred_element_type=F32)


NN = ((1,), (0,))
NT = ((1,), (1,))
TN = ((0,), (0,))


def columns(head):
    return slice(head * HD, (head + 1) * HD)


def causal(count, key_axis):
    keys = lax.broadcasted_iota(jnp.int32, (count, count), key_axis)
    queries = lax.broadcasted_iota(jnp.int32, (count, count), 1 - key_axis)
    return keys <= queries


def parts(row):
    high = row.astype(BF16)
    rest = row - high.astype(F32)
    middle = rest.astype(BF16)
    low = (rest - middle.astype(F32)).astype(BF16)
    return jnp.concatenate([high, middle, low], axis=0)


def row_dot(row, matrix):
    return jnp.sum(dot(parts(row), matrix, NN), axis=0, keepdims=True)


def state_kernel(k_ref, v_ref, state_ref, norm_ref):
    for h in range(k_ref.shape[1] // HD):
        at = columns(h)
        k_feat = features(k_ref[:, at].astype(F32))
        state_ref[at, :] = dot(k_feat, v_ref[:, at], TN)
        norm_ref[h : h + 1, :] = jnp.sum(k_feat.astype(F32), axis=0, keepdims=True)


def weights_kernel(q_ref, k_ref, c_ref, qf_ref, kf_ref, qt_ref, ct_ref, w_ref, part_ref):
    mask = causal(q_ref.shape[0], 0)
    for h in range(q_ref.shape[1] // HD):
        at = columns(h)
        q_feat = features(q_ref[:, at].astype(F32))
        k_feat = features(k_ref[:, at].astype(F32))
        scores = jnp.where(mask, dot(k_feat, q_feat, NT), 0.0)
        qf_ref[:, at] = q_feat
        kf_ref[:, at] = k_feat
        qt_ref[at, :] = q_feat.T
        ct_ref[at, :] = c_ref[:, at].T
        w_ref[:, at] = scores.astype(BF16)
        part_ref[h : h + 1, :] = jnp.sum(scores, axis=0, keepdims=True)


def later_kernel(qt_ref, ct_ref, part_ref, norm_ref, later_ref, scaled_ref, inv_ref):
    for h in range(part_ref.shape[0]):
        at = columns(h)
        row = slice(h, h + 1)
        q_turned = qt_ref[at, :]
        inverse = 1.0 / (part_ref[row, :] + row_dot(norm_ref[row, :], q_turned))
        scaled = (ct_ref[at, :].astype(F32) * inverse).astype(BF16)
        inv_ref[row, :] = inverse
        scaled_ref[at, :] = scaled
        later_ref[at, :] = dot(q_turned, scaled, NT)


def near_kernel(w_ref, scaled_ref, v_ref, num_ref, gs_ref, vi_ref, plain_ref):
    for h in range(w_ref.shape[1] // HD):
        at = columns(h)
        weights, value = w_ref[:, at], v_ref[:, at]
        scaled = scaled_ref[at, :].T
        plain_ref[:, at] = scaled
        num_ref[at, :] = dot(value, weights, TN)
        gs_ref[:, at] = dot(scaled, value, NT)
        vi_ref[:, at] = dot(weights, scaled, NN)


def attend_kernel(qf_ref, qt_ref, ct_ref, inv_ref, num_ref, state_ref, ratio_ref, gden_ref, lnorm_ref):
    for h in range(inv_ref.shape[0]):
        at = columns(h)
        row = slice(h, h + 1)
        inverse = inv_ref[row, :]
        ratio = (num_ref[at, :] + dot(state_ref[at, :].astype(BF16), qt_ref[at, :], TN)) * inverse
        ratio_ref[at, :] = ratio.astype(BF16)
        grad_den = -jnp.sum(ct_ref[at, :].astype(F32) * ratio, axis=0, keepdims=True) * inverse
        gden_ref[row, :] = grad_den
        lnorm_ref[row, :] = row_dot(grad_den, qf_ref[:, at])


def query_kernel(
    q_ref, qf_ref, kf_ref, scaled_ref, ratio_ref, gden_ref, norm_ref, gs_ref, state_ref, att_ref, qg_ref, ki_ref
):
    mask = causal(q_ref.shape[0], 1)
    gden_columns = gden_ref[...].T
    for h in range(gden_ref.shape[0]):
        at = columns(h)
        grad_den = gden_columns[:, h : h + 1]
        grad_scores = jnp.where(mask, gs_ref[:, at] + grad_den, 0.0).astype(BF16)
        q_lin = dot(grad_scores, kf_ref[:, at], NN) + dot(scaled_ref[:, at], state_ref[at, :].astype(BF16), NT)
        q_lin = q_lin + grad_den * norm_ref[h : h + 1, :]
        qg_ref[:, at] = (q_lin * slope(q_ref[:, at].astype(F32))).astype(BF16)
        ki_ref[:, at] = dot(grad_scores, qf_ref[:, at], TN)
        att_ref[:, at] = ratio_ref[at, :].T


def key_kernel(k_ref, kf_ref, v_ref, ki_ref, vi_ref, lnorm_ref, later_ref, kg_ref, vg_ref):
    for h in range(k_ref.shape[1] // HD):
        at = columns(h)
        later_low = later_ref[at, :].astype(BF16)
        k_lin = ki_ref[:, at] + dot(v_ref[:, at], later_low, NT) + lnorm_ref[h : h + 1, :]
        kg_ref[:, at] = (k_lin * slope(k_ref[:, at].astype(F32))).astype(BF16)
        vg_ref[:, at] = (vi_ref[:, at] + dot(kf_ref[:, at], later_low, NN)).astype(BF16)


COST = dict(state=1.0, weights=1.0, later=1.0, near=1.0, attend=1.0, query=1.0, key=1.0)
CHUNKS = (2, 2)
RADIX = 2
EARLY = ("N", "S0<N", "S1<N", "N", "N", "N")
GATE = "S0"
LATE = ()
LAST = ()
VMEM = 16


def call(name, kernel, outs, *args):
    return pl.pallas_call(
        kernel,
        out_shape=[jax.ShapeDtypeStruct(shape, kind) for shape, kind in outs],
        compiler_params=pltpu.CompilerParams(vmem_limit_bytes=VMEM << 20),
        cost_estimate=pl.CostEstimate(flops=0, bytes_accessed=int(COST[name] * 3.5e6), transcendentals=0),
        name=name,
    )(*args)


def bits(axis):
    return (lax.axis_size(axis) - 1).bit_length()


def swap(part, axis, mask):
    return lax.ppermute(part, axis, [(i, i ^ mask) for i in range(lax.axis_size(axis))])


def is_late(axis, mask, backward):
    set_bit = (lax.axis_index(axis) >> (mask.bit_length() - 1)) & 1
    return set_bit == (0 if backward else 1)


def groups(axis, start, radix):
    spans = [(b, min(b + radix, bits(axis))) for b in range(start, bits(axis), radix)]
    return [(axis, [m << low for m in range(1, 1 << (high - low))]) for low, high in spans]


def tie(value, others):
    return lax.optimization_barrier((value, *others))[0] if others else value


def add_up(part, levels, backward):
    before = jnp.zeros_like(part)
    for axis, masks in levels:
        got = yield [(part, axis, mask) for mask in masks]
        for mask, other in zip(masks, got):
            before = before + jnp.where(is_late(axis, mask, backward), other, 0.0)
            part = part + other
    return before


def scan_small(part, backward):
    levels = groups("inner", 0, RADIX) + [("outer", [1])] + groups("outer", 1, RADIX)
    return add_up(part, levels, backward)


def scan_large(part, backward):
    halving = [("inner", 1 << b) for b in range(bits("inner"))] + [("outer", 1)]
    lows = []
    for axis, mask in halving:
        late = is_late(axis, mask, backward)
        half = part.shape[0] // 2
        first, second = part[:half], part[half:]
        mine = jnp.where(late, second, first)
        (got,) = yield [(jnp.where(late, first, second), axis, mask)]
        lows.append(jnp.where(late, got, mine))
        part = mine + got
    before = yield from add_up(part, groups("outer", 1, RADIX), backward)
    for (axis, mask), low in zip(reversed(halving), reversed(lows)):
        late = is_late(axis, mask, backward)
        both = before + low
        mine = jnp.where(late, both, before)
        (got,) = yield [(jnp.where(late, before, both), axis, mask)]
        first = jnp.where(late, got, mine)
        second = jnp.where(late, mine, got)
        before = jnp.concatenate([first, second])
    return before


class Chain:
    def __init__(self, scan):
        self.scan = scan
        self.arrived = []
        self.result = None
        self.ask = next(scan)

    def hop(self, after=()):
        got = [swap(tie(part, after), axis, mask) for part, axis, mask in self.ask]
        self.arrived.append(got)
        try:
            self.ask = self.scan.send(got)
        except StopIteration as end:
            self.ask, self.result = None, end.value


def split(part, chunks, backward):
    size = part.shape[0] // chunks
    return [Chain(scan_large(part[i * size : (i + 1) * size], backward)) for i in range(chunks)]


def last(chains, names):
    found = []
    for name, _, hop in (entry.partition(".") for entry in names.split(",")):
        if name in chains and chains[name].arrived:
            arrived = chains[name].arrived
            found.extend(arrived[min(int(hop), len(arrived) - 1)] if hop else arrived[-1])
    return found


def run(chains, order):
    for entry in order:
        name, _, others = entry.partition("<")
        if name in chains and chains[name].ask:
            chains[name].hop(last(chains, others))


def drain(chains, kind):
    ours = [chains[name] for name in sorted(chains) if name[0] == kind]
    while any(chain.ask for chain in ours):
        for chain in ours:
            if chain.ask:
                chain.hop()
    results = [chain.result for chain in ours]
    return jnp.concatenate(results) if len(results) > 1 else results[0]


def per_device(queries, keys, values, cotangent):
    tokens, width = queries.shape
    heads = width // HD
    flat, turned, square, pairs = (tokens, width), (width, tokens), (width, HD), (tokens, heads * tokens)
    small, column = (heads, HD), (heads, tokens)
    local_state, local_norm = call("state", state_kernel, [(square, F32), (small, F32)], keys, values)
    chains = {"N": Chain(scan_small(local_norm, False))}
    chains.update(("S%d" % i, chain) for i, chain in enumerate(split(local_state, CHUNKS[0], False)))
    run(chains, EARLY)
    normal = tie(drain(chains, "N"), last(chains, GATE))
    q_feat, k_feat, q_turned, c_turned, weights, part = call(
        "weights", weights_kernel,
        [(flat, BF16), (flat, BF16), (turned, BF16), (turned, BF16), (pairs, BF16), (column, F32)],
        queries, keys, cotangent,
    )
    later_local, scaled, inverse = call(
        "later", later_kernel, [(square, F32), (turned, BF16), (column, F32)], q_turned, c_turned, part, normal
    )
    chains.update(("L%d" % i, chain) for i, chain in enumerate(split(later_local, CHUNKS[1], True)))
    run(chains, LATE)
    state = drain(chains, "S")
    near_num, near_scores, near_values, plain = call(
        "near", near_kernel, [(turned, F32), (pairs, F32), (flat, F32), (flat, BF16)], weights, scaled, values
    )
    ratio, grad_den, local_lnorm = call(
        "attend", attend_kernel, [(turned, BF16), (column, F32), (small, F32)],
        q_feat, q_turned, c_turned, inverse, near_num, state,
    )
    chains["M"] = Chain(scan_small(local_lnorm, True))
    run(chains, LAST)
    later_norm = drain(chains, "M")
    later = drain(chains, "L")
    attended, query_grad, near_keys = call(
        "query", query_kernel, [(flat, BF16), (flat, BF16), (flat, F32)],
        queries, q_feat, k_feat, plain, ratio, grad_den, normal, near_scores, state,
    )
    key_grad, value_grad = call(
        "key", key_kernel, [(flat, BF16), (flat, BF16)],
        keys, k_feat, values, near_keys, near_values, later_norm, later,
    )
    return attended, query_grad, key_grad, value_grad


def solution(mesh):
    rows = P(("outer", "inner"), None)
    return jax.shard_map(
        per_device, mesh=mesh, in_specs=(rows,) * 4, out_specs=(rows,) * 4, check_vma=False
    )
```

time: 147 us -> 120 us (0.82)
  waiting for transfers between devices: 66.6 us -> 56.4 us
  other arithmetic: 10.9 us -> 2.47 us
  local copies, waits for them, and re-layouts: 8.65 us -> 2.09 us
  Pallas kernels: 14.4 us -> 8.44 us
  starting transfers between devices: 44.4 us -> 49.4 us
    ppermute x42 -> x50, waiting for transfers between devices: 66.6 us -> 56.4 us  [swap(): lax.ppermute(part, axis, [(i, i ^ mask) for i in range(lax.axis_size(axis...]
    unnamed x70 -> x12, local copies, waits for them, and re-layouts: 8.65 us -> 2.09 us
    pallas_call x4 -> x7, Pallas kernels: 14.4 us -> 8.44 us  [call(): pl.pallas_call(kernel, out_shape=[jax.ShapeDtypeStruct(shape, kind) for s...]
    add x10, other arithmetic: 6.3 us -> 0.37 us  [scan_large(): part = mine + got]
    ppermute x42 -> x50, starting transfers between devices: 44.4 us -> 49.4 us  [swap(): lax.ppermute(part, axis, [(i, i ^ mask) for i in range(lax.axis_size(axis...]
    add x14 -> x6, other arithmetic: 2.4 us -> 0.04 us  [the longest x2 0.02 us: add_up(): before = before + jnp.where(is_late(axis, mask, backward), other, 0.0)]
  transfers between devices with their start and end apart: 42 -> 50, of which waited for: 21 -> 28; matrix products, arithmetic and copies ran while one was open for 7% -> 2% of each run, Pallas kernels for 8% -> 5%
where the time goes in v2:
time: 120 us
  waiting for transfers between devices  56.4 us (47%)
  starting transfers between devices  49.4 us (41%)
  Pallas kernels  8.44 us (7%)
  other arithmetic  2.47 us (2%)
  local copies, waits for them, and re-layouts  2.09 us (2%)
    ppermute x50, waiting for transfers between devices, swap(): lax.ppermute(part, axis, [(i, i ^ mask) for i in range(lax.axis_size(axis...  56.4 us
    ppermute x50, starting transfers between devices, swap(): lax.ppermute(part, axis, [(i, i ^ mask) for i in range(lax.axis_size(axis...  49.4 us
    pallas_call x7, Pallas kernels, call(): pl.pallas_call(kernel, out_shape=[jax.ShapeDtypeStruct(shape, kind) for s...  8.44 us
  transfers between devices with their start and end apart: 50, of which 28 were waited for; matrix products, arithmetic and copies ran while one was open for 2% of the time, Pallas kernels for 5%

profile of v2, /device:TPU:0, one launch (start us, length us, event | category | flops | bytes accessed | tf_op | source)
XLA Modules:
  0.0 119.8 jit_solution(17610525081933207366)
XLA Ops:
  3.3 5.1 %collective-permute-start.2 = (f32[16,128]{1,0:T(8,128)S(1)}, f32[16,128]{1,0:T(8,128)S(1)}, u32[]{:S(2)}, u32[]{:S(2)}) collective-permute-start(f32[16,128]{1,0:T(8,128)S(1)} %get-tuple-element.36), channel_id=1, source_target_pairs={{0,3},{1,2},{2,1},{3,0},{4,7},{5,6},{6,5},{7,4},{8,11},{9,10},{10,... | collective-permute-start | bytes 24584 | tf_op jit(solution)/shard_map/ppermute | solution.py:162
  10.1 2.9 %collective-permute-done.1 = f32[16,128]{1,0:T(8,128)S(1)} collective-permute-done((f32[16,128]{1,0:T(8,128)S(1)}, f32[16,128]{1,0:T(8,128)S(1)}, u32[]{:S(2)}, u32[]{:S(2)}) %collective-permute-start.1) | collective-permute-done | bytes 8224 | tf_op jit(solution)/shard_map/ppermute | solution.py:162
  13.0 2.0 %collective-permute-start.16 = (f32[512,128]{1,0:T(8,128)S(1)}, f32[512,128]{1,0:T(8,128)S(1)}, u32[]{:S(2)}, u32[]{:S(2)}) collective-permute-start(f32[512,128]{1,0:T(8,128)S(1)} %get-tuple-element.44), channel_id=1, source_target_pairs={{0,1},{1,0},{2,3},{3,2},{4,5},{5,4},{6,7},{7,6},{8,9},{9,8},{10,11... | collective-permute-start | bytes 786440 | tf_op jit(solution)/shard_map/ppermute | solution.py:162
  16.2 2.5 %collective-permute-start.6 = (f32[16,128]{1,0:T(8,128)S(1)}, f32[16,128]{1,0:T(8,128)S(1)}, u32[]{:S(2)}, u32[]{:S(2)}) collective-permute-start(f32[16,128]{1,0:T(8,128)S(1)} %add.162), channel_id=1, source_target_pairs={{0,24},{4,28},{8,16},{12,20},{16,8},{20,12},{24,0},{28,4},{1,25},{... | collective-permute-start | bytes 24584 | tf_op jit(solution)/shard_map/ppermute | solution.py:162
  20.7 1.6 %collective-permute-done.5 = f32[16,128]{1,0:T(8,128)S(1)} collective-permute-done((f32[16,128]{1,0:T(8,128)S(1)}, f32[16,128]{1,0:T(8,128)S(1)}, u32[]{:S(2)}, u32[]{:S(2)}) %collective-permute-start.5) | collective-permute-done | bytes 8224 | tf_op jit(solution)/shard_map/ppermute | solution.py:162
  22.8 2.6 %collective-permute-done.16 = f32[512,128]{1,0:T(8,128)S(1)} collective-permute-done((f32[512,128]{1,0:T(8,128)S(1)}, f32[512,128]{1,0:T(8,128)S(1)}, u32[]{:S(2)}, u32[]{:S(2)}) %collective-permute-start.16) | collective-permute-done | bytes 262176 | tf_op jit(solution)/shard_map/ppermute | solution.py:162
  25.6 1.9 %collective-permute-start.17 = (f32[256,128]{1,0:T(8,128)S(1)}, f32[256,128]{1,0:T(8,128)S(1)}, u32[]{:S(2)}, u32[]{:S(2)}) collective-permute-start(f32[256,128]{1,0:T(8,128)S(1)} %slice_select_fusion.12), channel_id=1, source_target_pairs={{0,2},{1,3},{2,0},{3,1},{4,6},{5,7},{6,4},{7,5},{8,10},{9,11},{10,... | collective-permute-start | bytes 393224 | tf_op jit(solution)/shard_map/ppermute | solution.py:162
  28.6 1.7 %later.1 = (f32[2048,128]{1,0:T(8,128)S(1)}, bf16[2048,128]{1,0:T(8,128)(2,1)S(1)}, f32[16,128]{1,0:T(8,128)S(1)}) custom-call(bf16[2048,128]{1,0:T(8,128)(2,1)S(1)} %get-tuple-element.33.qt_ref, bf16[2048,128]{1,0:T(8,128)(2,1)S(1)} %get-tuple-element.34.ct_ref, f32[16,128]{1,0:T(8,128)S(1)} %get-tuple-element.35.part_ref, ...), custom_call_target="tpu_custom_call" | custom-call | bytes 3500000 | tf_op jit(solution)/shard_map/later/pallas_call | solution.py:148
  30.7 1.7 %collective-permute-start.41 = (f32[512,128]{1,0:T(8,128)S(1)}, f32[512,128]{1,0:T(8,128)S(1)}, u32[]{:S(2)}, u32[]{:S(2)}) collective-permute-start(f32[512,128]{1,0:T(8,128)S(1)} %get-tuple-element.93), channel_id=1, source_target_pairs={{0,1},{1,0},{2,3},{3,2},{4,5},{5,4},{6,7},{7,6},{8,9},{9,8},{10,11... | collective-permute-start | bytes 786440 | tf_op jit(solution)/shard_map/ppermute | solution.py:162
  33.2 2.3 %collective-permute-done.17 = f32[256,128]{1,0:T(8,128)S(1)} collective-permute-done((f32[256,128]{1,0:T(8,128)S(1)}, f32[256,128]{1,0:T(8,128)S(1)}, u32[]{:S(2)}, u32[]{:S(2)}) %collective-permute-start.17) | collective-permute-done | bytes 131104 | tf_op jit(solution)/shard_map/ppermute | solution.py:162
  35.7 2.2 %collective-permute-done.8 = f32[256,128]{1,0:T(8,128)S(1)} collective-permute-done((f32[256,128]{1,0:T(8,128)S(1)}, f32[256,128]{1,0:T(8,128)S(1)}, u32[]{:S(2)}, u32[]{:S(2)}) %collective-permute-start.8) | collective-permute-done | bytes 131104 | tf_op jit(solution)/shard_map/ppermute | solution.py:162
  38.1 2.5 %collective-permute-start.21 = (f32[128,128]{1,0:T(8,128)S(1)}, f32[128,128]{1,0:T(8,128)S(1)}, u32[]{:S(2)}, u32[]{:S(2)}) collective-permute-start(f32[128,128]{1,0:T(8,128)S(1)} %get-tuple-element.82), channel_id=1, source_target_pairs={{0,24},{4,28},{8,16},{12,20},{16,8},{20,12},{24,0},{28,4},{1,25},{... | collective-permute-start | bytes 196616 | tf_op jit(solution)/shard_map/ppermute | solution.py:162
  41.7 1.9 %collective-permute-done.21 = f32[128,128]{1,0:T(8,128)S(1)} collective-permute-done((f32[128,128]{1,0:T(8,128)S(1)}, f32[128,128]{1,0:T(8,128)S(1)}, u32[]{:S(2)}, u32[]{:S(2)}) %collective-permute-start.21) | collective-permute-done | bytes 65568 | tf_op jit(solution)/shard_map/ppermute | solution.py:162
  43.5 2.8 %collective-permute-start.12 = (f32[128,128]{1,0:T(8,128)S(1)}, f32[128,128]{1,0:T(8,128)S(1)}, u32[]{:S(2)}, u32[]{:S(2)}) collective-permute-start(f32[128,128]{1,0:T(8,128)S(1)} %get-tuple-element.74), channel_id=1, source_target_pairs={{0,24},{4,28},{8,16},{12,20},{16,8},{20,12},{24,0},{28,4},{1,25},{... | collective-permute-start | bytes 196616 | tf_op jit(solution)/shard_map/ppermute | solution.py:162
  48.8 1.8 %collective-permute-done.11 = f32[128,128]{1,0:T(8,128)S(1)} collective-permute-done((f32[128,128]{1,0:T(8,128)S(1)}, f32[128,128]{1,0:T(8,128)S(1)}, u32[]{:S(2)}, u32[]{:S(2)}) %collective-permute-start.11) | collective-permute-done | bytes 65568 | tf_op jit(solution)/shard_map/ppermute | solution.py:162
  51.2 2.9 %collective-permute-start.33 = (f32[256,128]{1,0:T(8,128)S(1)}, f32[256,128]{1,0:T(8,128)S(1)}, u32[]{:S(2)}, u32[]{:S(2)}) collective-permute-start(f32[256,128]{1,0:T(8,128)S(1)} %slice_select_fusion.10), channel_id=1, source_target_pairs={{0,2},{1,3},{2,0},{3,1},{4,6},{5,7},{6,4},{7,5},{8,10},{9,11},{10,... | collective-permute-start | bytes 393224 | tf_op jit(solution)/shard_map/ppermute | solution.py:162
  54.4 2.9 %collective-permute-start.14 = (f32[256,128]{1,0:T(8,128)S(1)}, f32[256,128]{1,0:T(8,128)S(1)}, u32[]{:S(2)}, u32[]{:S(2)}) collective-permute-start(f32[256,128]{1,0:T(8,128)S(1)} %add_select_fusion.15), channel_id=1, source_target_pairs={{0,2},{1,3},{2,0},{3,1},{4,6},{5,7},{6,4},{7,5},{8,10},{9,11},{10,... | collective-permute-start | bytes 393224 | tf_op jit(solution)/shard_map/ppermute | solution.py:162
  57.3 11.4 %collective-permute-done.42 = f32[256,128]{1,0:T(8,128)S(1)} collective-permute-done((f32[256,128]{1,0:T(8,128)S(1)}, f32[256,128]{1,0:T(8,128)S(1)}, u32[]{:S(2)}, u32[]{:S(2)}) %collective-permute-start.42) | collective-permute-done | bytes 131104 | tf_op jit(solution)/shard_map/ppermute | solution.py:162
  68.8 2.7 %collective-permute-done.33 = f32[256,128]{1,0:T(8,128)S(1)} collective-permute-done((f32[256,128]{1,0:T(8,128)S(1)}, f32[256,128]{1,0:T(8,128)S(1)}, u32[]{:S(2)}, u32[]{:S(2)}) %collective-permute-start.33) | collective-permute-done | bytes 131104 | tf_op jit(solution)/shard_map/ppermute | solution.py:162
  71.6 2.7 %collective-permute-done.23 = f32[256,128]{1,0:T(8,128)S(1)} collective-permute-done((f32[256,128]{1,0:T(8,128)S(1)}, f32[256,128]{1,0:T(8,128)S(1)}, u32[]{:S(2)}, u32[]{:S(2)}) %collective-permute-start.23) | collective-permute-done | bytes 131104 | tf_op jit(solution)/shard_map/ppermute | solution.py:162
  74.5 2.6 %collective-permute-done.14 = f32[256,128]{1,0:T(8,128)S(1)} collective-permute-done((f32[256,128]{1,0:T(8,128)S(1)}, f32[256,128]{1,0:T(8,128)S(1)}, u32[]{:S(2)}, u32[]{:S(2)}) %collective-permute-start.14) | collective-permute-done | bytes 131104 | tf_op jit(solution)/shard_map/ppermute | solution.py:162
  77.3 1.6 %collective-permute-start.46 = (f32[128,128]{1,0:T(8,128)S(1)}, f32[128,128]{1,0:T(8,128)S(1)}, u32[]{:S(2)}, u32[]{:S(2)}) collective-permute-start(f32[128,128]{1,0:T(8,128)S(1)} %get-tuple-element.66), channel_id=1, source_target_pairs={{0,24},{4,28},{8,16},{12,20},{16,8},{20,12},{24,0},{28,4},{1,25},{... | collective-permute-start | bytes 196616 | tf_op jit(solution)/shard_map/ppermute | solution.py:162
  80.8 1.8 %collective-permute-done.46 = f32[128,128]{1,0:T(8,128)S(1)} collective-permute-done((f32[128,128]{1,0:T(8,128)S(1)}, f32[128,128]{1,0:T(8,128)S(1)}, u32[]{:S(2)}, u32[]{:S(2)}) %collective-permute-start.46) | collective-permute-done | bytes 65568 | tf_op jit(solution)/shard_map/ppermute | solution.py:162
  86.4 1.8 %collective-permute-done.37 = f32[128,128]{1,0:T(8,128)S(1)} collective-permute-done((f32[128,128]{1,0:T(8,128)S(1)}, f32[128,128]{1,0:T(8,128)S(1)}, u32[]{:S(2)}, u32[]{:S(2)}) %collective-permute-start.37) | collective-permute-done | bytes 65568 | tf_op jit(solution)/shard_map/ppermute | solution.py:162
  89.5 2.3 %collective-permute-start.48 = (f32[256,128]{1,0:T(8,128)S(1)}, f32[256,128]{1,0:T(8,128)S(1)}, u32[]{:S(2)}, u32[]{:S(2)}) collective-permute-start(f32[256,128]{1,0:T(8,128)S(1)} %add_select_fusion.9), channel_id=1, source_target_pairs={{0,2},{1,3},{2,0},{3,1},{4,6},{5,7},{6,4},{7,5},{8,10},{9,11},{10,... | collective-permute-start | bytes 393224 | tf_op jit(solution)/shard_map/ppermute | solution.py:162
  93.6 2.1 %collective-permute-start.27 = (f32[16,128]{1,0:T(8,128)S(1)}, f32[16,128]{1,0:T(8,128)S(1)}, u32[]{:S(2)}, u32[]{:S(2)}) collective-permute-start(f32[16,128]{1,0:T(8,128)S(1)} %get-tuple-element.52), channel_id=1, source_target_pairs={{0,3},{1,2},{2,1},{3,0},{4,7},{5,6},{6,5},{7,4},{8,11},{9,10},{10,... | collective-permute-start | bytes 24584 | tf_op jit(solution)/shard_map/ppermute | solution.py:162
  98.0 4.7 %collective-permute-done.48 = f32[256,128]{1,0:T(8,128)S(1)} collective-permute-done((f32[256,128]{1,0:T(8,128)S(1)}, f32[256,128]{1,0:T(8,128)S(1)}, u32[]{:S(2)}, u32[]{:S(2)}) %collective-permute-start.48) | collective-permute-done | bytes 131104 | tf_op jit(solution)/shard_map/ppermute | solution.py:162
  102.9 2.5 %collective-permute-done.26 = f32[16,128]{1,0:T(8,128)S(1)} collective-permute-done((f32[16,128]{1,0:T(8,128)S(1)}, f32[16,128]{1,0:T(8,128)S(1)}, u32[]{:S(2)}, u32[]{:S(2)}) %collective-permute-start.26) | collective-permute-done | bytes 8224 | tf_op jit(solution)/shard_map/ppermute | solution.py:162
  106.7 2.8 %collective-permute-start.31 = (f32[16,128]{1,0:T(8,128)S(1)}, f32[16,128]{1,0:T(8,128)S(1)}, u32[]{:S(2)}, u32[]{:S(2)}) collective-permute-start(f32[16,128]{1,0:T(8,128)S(1)} %add.188), channel_id=1, source_target_pairs={{0,24},{4,28},{8,16},{12,20},{16,8},{20,12},{24,0},{28,4},{1,25},{... | collective-permute-start | bytes 24584 | tf_op jit(solution)/shard_map/ppermute | solution.py:162
  110.8 2.3 %query.1 = (bf16[128,2048]{1,0:T(8,128)(2,1)}, bf16[128,2048]{1,0:T(8,128)(2,1)}, f32[128,2048]{1,0:T(8,128)S(1)}) custom-call(bf16[128,2048]{1,0:T(8,128)(2,1)S(1)} %copy-done.4, bf16[128,2048]{1,0:T(8,128)(2,1)S(1)} %get-tuple-element.30.qf_ref, bf16[128,2048]{1,0:T(8,128)(2,1)S(1)} %get-tuple-element.31.kf_ref, ...), custom_call_target="tpu_custom_call" | custom-call | bytes 3500000 | tf_op jit(solution)/shard_map/query/pallas_call | solution.py:148
  113.3 4.7 %collective-permute-done.40 = f32[512,128]{1,0:T(8,128)S(1)} collective-permute-done((f32[512,128]{1,0:T(8,128)S(1)}, f32[512,128]{1,0:T(8,128)S(1)}, u32[]{:S(2)}, u32[]{:S(2)}) %collective-permute-start.40) | collective-permute-done | bytes 262176 | tf_op jit(solution)/shard_map/ppermute | solution.py:162
  118.1 1.7 %key.1 = (bf16[128,2048]{1,0:T(8,128)(2,1)}, bf16[128,2048]{1,0:T(8,128)(2,1)}) custom-call(bf16[128,2048]{1,0:T(8,128)(2,1)S(1)} %copy-done.1, bf16[128,2048]{1,0:T(8,128)(2,1)S(1)} %get-tuple-element.31.kf_ref, bf16[128,2048]{1,0:T(8,128)(2,1)S(1)} %copy-done.3, f32[128,2048]{1,0:T(8,128)S(1)} %get-tuple-element.50.ki_ref, ...), custom_call_target="tpu_custom_call" | custom-call | bytes 3500000 | tf_op jit(solution)/shard_map/key/pallas_call | solution.py:148
  (139 shorter events, 29.9 us)
Async XLA Ops:
  3.3 6.7 %collective-permute-start.2 = (f32[16,128]{1,0:T(8,128)S(1)}, f32[16,128]{1,0:T(8,128)S(1)}, u32[]{:S(2)}, u32[]{:S(2)}) collective-permute-start(f32[16,128]{1,0:T(8,128)S(1)} %get-tuple-element.36), channel_id=1, source_target_pairs={{0,3},{1,2},{2,1},{3,0},{4,7},{5,6},{6,5},{7,4},{8,11},{9,10},{10,... | collective-permute-start | bytes 24584 | tf_op jit(solution)/shard_map/ppermute | solution.py:162
  13.0 9.8 %collective-permute-start.7 = (f32[512,128]{1,0:T(8,128)}, f32[512,128]{1,0:T(8,128)S(1)}, u32[]{:S(2)}, u32[]{:S(2)}) collective-permute-start(f32[512,128]{1,0:T(8,128)} %get-tuple-element.38), channel_id=1, source_target_pairs={{0,1},{1,0},{2,3},{3,2},{4,5},{5,4},{6,7},{7,6},{8,9},{9,8},{10,11... | collective-permute-start | bytes 786440 | tf_op jit(solution)/shard_map/ppermute | solution.py:162
  13.0 12.4 %collective-permute-start.16 = (f32[512,128]{1,0:T(8,128)S(1)}, f32[512,128]{1,0:T(8,128)S(1)}, u32[]{:S(2)}, u32[]{:S(2)}) collective-permute-start(f32[512,128]{1,0:T(8,128)S(1)} %get-tuple-element.44), channel_id=1, source_target_pairs={{0,1},{1,0},{2,3},{3,2},{4,5},{5,4},{6,7},{7,6},{8,9},{9,8},{10,11... | collective-permute-start | bytes 786440 | tf_op jit(solution)/shard_map/ppermute | solution.py:162
  25.6 10.0 %collective-permute-start.17 = (f32[256,128]{1,0:T(8,128)S(1)}, f32[256,128]{1,0:T(8,128)S(1)}, u32[]{:S(2)}, u32[]{:S(2)}) collective-permute-start(f32[256,128]{1,0:T(8,128)S(1)} %slice_select_fusion.12), channel_id=1, source_target_pairs={{0,2},{1,3},{2,0},{3,1},{4,6},{5,7},{6,4},{7,5},{8,10},{9,11},{10,... | collective-permute-start | bytes 393224 | tf_op jit(solution)/shard_map/ppermute | solution.py:162
  27.4 10.5 %collective-permute-start.8 = (f32[256,128]{1,0:T(8,128)S(1)}, f32[256,128]{1,0:T(8,128)S(1)}, u32[]{:S(2)}, u32[]{:S(2)}) collective-permute-start(f32[256,128]{1,0:T(8,128)S(1)} %slice_select_fusion.14), channel_id=1, source_target_pairs={{0,2},{1,3},{2,0},{3,1},{4,6},{5,7},{6,4},{7,5},{8,10},{9,11},{10,... | collective-permute-start | bytes 393224 | tf_op jit(solution)/shard_map/ppermute | solution.py:162
  30.3 20.7 %collective-permute-start.32 = (f32[512,128]{1,0:T(8,128)S(1)}, f32[512,128]{1,0:T(8,128)S(1)}, u32[]{:S(2)}, u32[]{:S(2)}) collective-permute-start(f32[512,128]{1,0:T(8,128)S(1)} %get-tuple-element.92), channel_id=1, source_target_pairs={{0,1},{1,0},{2,3},{3,2},{4,5},{5,4},{6,7},{7,6},{8,9},{9,8},{10,11... | collective-permute-start | bytes 786440 | tf_op jit(solution)/shard_map/ppermute | solution.py:162
  30.7 20.3 %collective-permute-start.41 = (f32[512,128]{1,0:T(8,128)S(1)}, f32[512,128]{1,0:T(8,128)S(1)}, u32[]{:S(2)}, u32[]{:S(2)}) collective-permute-start(f32[512,128]{1,0:T(8,128)S(1)} %get-tuple-element.93), channel_id=1, source_target_pairs={{0,1},{1,0},{2,3},{3,2},{4,5},{5,4},{6,7},{7,6},{8,9},{9,8},{10,11... | collective-permute-start | bytes 786440 | tf_op jit(solution)/shard_map/ppermute | solution.py:162
  38.1 5.5 %collective-permute-start.21 = (f32[128,128]{1,0:T(8,128)S(1)}, f32[128,128]{1,0:T(8,128)S(1)}, u32[]{:S(2)}, u32[]{:S(2)}) collective-permute-start(f32[128,128]{1,0:T(8,128)S(1)} %get-tuple-element.82), channel_id=1, source_target_pairs={{0,24},{4,28},{8,16},{12,20},{16,8},{20,12},{24,0},{28,4},{1,25},{... | collective-permute-start | bytes 196616 | tf_op jit(solution)/shard_map/ppermute | solution.py:162
  40.6 5.8 %collective-permute-start.20 = (f32[128,128]{1,0:T(8,128)S(1)}, f32[128,128]{1,0:T(8,128)S(1)}, u32[]{:S(2)}, u32[]{:S(2)}) collective-permute-start(f32[128,128]{1,0:T(8,128)S(1)} %get-tuple-element.82), channel_id=1, source_target_pairs={{0,16},{4,20},{8,24},{12,28},{16,0},{20,4},{24,8},{28,12},{1,17},{... | collective-permute-start | bytes 196616 | tf_op jit(solution)/shard_map/ppermute | solution.py:162
  41.1 5.5 %collective-permute-start.19 = (f32[128,128]{1,0:T(8,128)S(1)}, f32[128,128]{1,0:T(8,128)S(1)}, u32[]{:S(2)}, u32[]{:S(2)}) collective-permute-start(f32[128,128]{1,0:T(8,128)S(1)} %get-tuple-element.82), channel_id=1, source_target_pairs={{0,8},{4,12},{8,0},{12,4},{16,24},{20,28},{24,16},{28,20},{1,9},{5... | collective-permute-start | bytes 196616 | tf_op jit(solution)/shard_map/ppermute | solution.py:162
  43.5 5.3 %collective-permute-start.12 = (f32[128,128]{1,0:T(8,128)S(1)}, f32[128,128]{1,0:T(8,128)S(1)}, u32[]{:S(2)}, u32[]{:S(2)}) collective-permute-start(f32[128,128]{1,0:T(8,128)S(1)} %get-tuple-element.74), channel_id=1, source_target_pairs={{0,24},{4,28},{8,16},{12,20},{16,8},{20,12},{24,0},{28,4},{1,25},{... | collective-permute-start | bytes 196616 | tf_op jit(solution)/shard_map/ppermute | solution.py:162
  48.8 5.3 %collective-permute-start.22 = (f32[128,128]{1,0:T(8,128)S(1)}, f32[128,128]{1,0:T(8,128)S(1)}, u32[]{:S(2)}, u32[]{:S(2)}) collective-permute-start(f32[128,128]{1,0:T(8,128)S(1)} %get-tuple-element.80), channel_id=1, source_target_pairs={{0,4},{4,0},{8,12},{12,8},{16,20},{20,16},{24,28},{28,24},{1,5},{5... | collective-permute-start | bytes 196616 | tf_op jit(solution)/shard_map/ppermute | solution.py:162
  51.1 17.5 %collective-permute-start.42 = (f32[256,128]{1,0:T(8,128)S(1)}, f32[256,128]{1,0:T(8,128)S(1)}, u32[]{:S(2)}, u32[]{:S(2)}) collective-permute-start(f32[256,128]{1,0:T(8,128)S(1)} %slice_select_fusion.8), channel_id=1, source_target_pairs={{0,2},{1,3},{2,0},{3,1},{4,6},{5,7},{6,4},{7,5},{8,10},{9,11},{10,... | collective-permute-start | bytes 393224 | tf_op jit(solution)/shard_map/ppermute | solution.py:162
  51.2 20.3 %collective-permute-start.33 = (f32[256,128]{1,0:T(8,128)S(1)}, f32[256,128]{1,0:T(8,128)S(1)}, u32[]{:S(2)}, u32[]{:S(2)}) collective-permute-start(f32[256,128]{1,0:T(8,128)S(1)} %slice_select_fusion.10), channel_id=1, source_target_pairs={{0,2},{1,3},{2,0},{3,1},{4,6},{5,7},{6,4},{7,5},{8,10},{9,11},{10,... | collective-permute-start | bytes 393224 | tf_op jit(solution)/shard_map/ppermute | solution.py:162
  54.2 20.1 %collective-permute-start.23 = (f32[256,128]{1,0:T(8,128)S(1)}, f32[256,128]{1,0:T(8,128)S(1)}, u32[]{:S(2)}, u32[]{:S(2)}) collective-permute-start(f32[256,128]{1,0:T(8,128)S(1)} %add_select_fusion.13), channel_id=1, source_target_pairs={{0,2},{1,3},{2,0},{3,1},{4,6},{5,7},{6,4},{7,5},{8,10},{9,11},{10,... | collective-permute-start | bytes 393224 | tf_op jit(solution)/shard_map/ppermute | solution.py:162
  54.4 22.7 %collective-permute-start.14 = (f32[256,128]{1,0:T(8,128)S(1)}, f32[256,128]{1,0:T(8,128)S(1)}, u32[]{:S(2)}, u32[]{:S(2)}) collective-permute-start(f32[256,128]{1,0:T(8,128)S(1)} %add_select_fusion.15), channel_id=1, source_target_pairs={{0,2},{1,3},{2,0},{3,1},{4,6},{5,7},{6,4},{7,5},{8,10},{9,11},{10,... | collective-permute-start | bytes 393224 | tf_op jit(solution)/shard_map/ppermute | solution.py:162
  68.7 8.5 %collective-permute-start.43 = (f32[128,128]{1,0:T(8,128)S(1)}, f32[128,128]{1,0:T(8,128)S(1)}, u32[]{:S(2)}, u32[]{:S(2)}) collective-permute-start(f32[128,128]{1,0:T(8,128)S(1)} %slice_select_fusion.16), channel_id=1, source_target_pairs={{0,4},{4,0},{8,12},{12,8},{16,20},{20,16},{24,28},{28,24},{1,5},{5... | collective-permute-start | bytes 196616 | tf_op jit(solution)/shard_map/ppermute | solution.py:162
  71.5 8.0 %collective-permute-start.34 = (f32[128,128]{1,0:T(8,128)S(1)}, f32[128,128]{1,0:T(8,128)S(1)}, u32[]{:S(2)}, u32[]{:S(2)}) collective-permute-start(f32[128,128]{1,0:T(8,128)S(1)} %slice_select_fusion.18), channel_id=1, source_target_pairs={{0,4},{4,0},{8,12},{12,8},{16,20},{20,16},{24,28},{28,24},{1,5},{5... | collective-permute-start | bytes 196616 | tf_op jit(solution)/shard_map/ppermute | solution.py:162
  74.4 18.3 %collective-permute-start.24 = (f32[512,128]{1,0:T(8,128)S(1)}, f32[512,128]{1,0:T(8,128)S(1)}, u32[]{:S(2)}, u32[]{:S(2)}) collective-permute-start(f32[512,128]{1,0:T(8,128)S(1)} %add_select_fusion.5), channel_id=1, source_target_pairs={{0,1},{1,0},{2,3},{3,2},{4,5},{5,4},{6,7},{7,6},{8,9},{9,8},{10,11... | collective-permute-start | bytes 786440 | tf_op jit(solution)/shard_map/ppermute | solution.py:162
  77.2 15.7 %collective-permute-start.15 = (f32[512,128]{1,0:T(8,128)S(1)}, f32[512,128]{1,0:T(8,128)S(1)}, u32[]{:S(2)}, u32[]{:S(2)}) collective-permute-start(f32[512,128]{1,0:T(8,128)S(1)} %add_select_fusion.7), channel_id=1, source_target_pairs={{0,1},{1,0},{2,3},{3,2},{4,5},{5,4},{6,7},{7,6},{8,9},{9,8},{10,11... | collective-permute-start | bytes 786440 | tf_op jit(solution)/shard_map/ppermute | solution.py:162
  77.3 5.3 %collective-permute-start.46 = (f32[128,128]{1,0:T(8,128)S(1)}, f32[128,128]{1,0:T(8,128)S(1)}, u32[]{:S(2)}, u32[]{:S(2)}) collective-permute-start(f32[128,128]{1,0:T(8,128)S(1)} %get-tuple-element.66), channel_id=1, source_target_pairs={{0,24},{4,28},{8,16},{12,20},{16,8},{20,12},{24,0},{28,4},{1,25},{... | collective-permute-start | bytes 196616 | tf_op jit(solution)/shard_map/ppermute | solution.py:162
  78.8 5.3 %collective-permute-start.45 = (f32[128,128]{1,0:T(8,128)S(1)}, f32[128,128]{1,0:T(8,128)S(1)}, u32[]{:S(2)}, u32[]{:S(2)}) collective-permute-start(f32[128,128]{1,0:T(8,128)S(1)} %get-tuple-element.66), channel_id=1, source_target_pairs={{0,16},{4,20},{8,24},{12,28},{16,0},{20,4},{24,8},{28,12},{1,17},{... | collective-permute-start | bytes 196616 | tf_op jit(solution)/shard_map/ppermute | solution.py:162
  79.5 5.4 %collective-permute-start.44 = (f32[128,128]{1,0:T(8,128)S(1)}, f32[128,128]{1,0:T(8,128)S(1)}, u32[]{:S(2)}, u32[]{:S(2)}) collective-permute-start(f32[128,128]{1,0:T(8,128)S(1)} %get-tuple-element.66), channel_id=1, source_target_pairs={{0,8},{4,12},{8,0},{12,4},{16,24},{20,28},{24,16},{28,20},{1,9},{5... | collective-permute-start | bytes 196616 | tf_op jit(solution)/shard_map/ppermute | solution.py:162
  82.6 5.6 %collective-permute-start.37 = (f32[128,128]{1,0:T(8,128)S(1)}, f32[128,128]{1,0:T(8,128)S(1)}, u32[]{:S(2)}, u32[]{:S(2)}) collective-permute-start(f32[128,128]{1,0:T(8,128)S(1)} %get-tuple-element.58), channel_id=1, source_target_pairs={{0,24},{4,28},{8,16},{12,20},{16,8},{20,12},{24,0},{28,4},{1,25},{... | collective-permute-start | bytes 196616 | tf_op jit(solution)/shard_map/ppermute | solution.py:162
  89.5 13.2 %collective-permute-start.48 = (f32[256,128]{1,0:T(8,128)S(1)}, f32[256,128]{1,0:T(8,128)S(1)}, u32[]{:S(2)}, u32[]{:S(2)}) collective-permute-start(f32[256,128]{1,0:T(8,128)S(1)} %add_select_fusion.9), channel_id=1, source_target_pairs={{0,2},{1,3},{2,0},{3,1},{4,6},{5,7},{6,4},{7,5},{8,10},{9,11},{10,... | collective-permute-start | bytes 393224 | tf_op jit(solution)/shard_map/ppermute | solution.py:162
  91.8 13.7 %collective-permute-start.39 = (f32[256,128]{1,0:T(8,128)S(1)}, f32[256,128]{1,0:T(8,128)S(1)}, u32[]{:S(2)}, u32[]{:S(2)}) collective-permute-start(f32[256,128]{1,0:T(8,128)S(1)} %add_select_fusion.11), channel_id=1, source_target_pairs={{0,2},{1,3},{2,0},{3,1},{4,6},{5,7},{6,4},{7,5},{8,10},{9,11},{10,... | collective-permute-start | bytes 393224 | tf_op jit(solution)/shard_map/ppermute | solution.py:162
  93.6 9.3 %collective-permute-start.27 = (f32[16,128]{1,0:T(8,128)S(1)}, f32[16,128]{1,0:T(8,128)S(1)}, u32[]{:S(2)}, u32[]{:S(2)}) collective-permute-start(f32[16,128]{1,0:T(8,128)S(1)} %get-tuple-element.52), channel_id=1, source_target_pairs={{0,3},{1,2},{2,1},{3,0},{4,7},{5,6},{6,5},{7,4},{8,11},{9,10},{10,... | collective-permute-start | bytes 24584 | tf_op jit(solution)/shard_map/ppermute | solution.py:162
  95.7 9.7 %collective-permute-start.26 = (f32[16,128]{1,0:T(8,128)S(1)}, f32[16,128]{1,0:T(8,128)S(1)}, u32[]{:S(2)}, u32[]{:S(2)}) collective-permute-start(f32[16,128]{1,0:T(8,128)S(1)} %get-tuple-element.52), channel_id=1, source_target_pairs={{0,2},{1,3},{2,0},{3,1},{4,6},{5,7},{6,4},{7,5},{8,10},{9,11},{10,... | collective-permute-start | bytes 24584 | tf_op jit(solution)/shard_map/ppermute | solution.py:162
  96.9 8.5 %collective-permute-start.25 = (f32[16,128]{1,0:T(8,128)S(1)}, f32[16,128]{1,0:T(8,128)S(1)}, u32[]{:S(2)}, u32[]{:S(2)}) collective-permute-start(f32[16,128]{1,0:T(8,128)S(1)} %get-tuple-element.52), channel_id=1, source_target_pairs={{0,1},{1,0},{2,3},{3,2},{4,5},{5,4},{6,7},{7,6},{8,9},{9,8},{10,11... | collective-permute-start | bytes 24584 | tf_op jit(solution)/shard_map/ppermute | solution.py:162
  102.8 10.4 %collective-permute-start.49 = (f32[512,128]{1,0:T(8,128)S(1)}, f32[512,128]{1,0:T(8,128)S(1)}, u32[]{:S(2)}, u32[]{:S(2)}) collective-permute-start(f32[512,128]{1,0:T(8,128)S(1)} %add_select_fusion.1), channel_id=1, source_target_pairs={{0,1},{1,0},{2,3},{3,2},{4,5},{5,4},{6,7},{7,6},{8,9},{9,8},{10,11... | collective-permute-start | bytes 786440 | tf_op jit(solution)/shard_map/ppermute | solution.py:162
  106.7 6.4 %collective-permute-start.31 = (f32[16,128]{1,0:T(8,128)S(1)}, f32[16,128]{1,0:T(8,128)S(1)}, u32[]{:S(2)}, u32[]{:S(2)}) collective-permute-start(f32[16,128]{1,0:T(8,128)S(1)} %add.188), channel_id=1, source_target_pairs={{0,24},{4,28},{8,16},{12,20},{16,8},{20,12},{24,0},{28,4},{1,25},{... | collective-permute-start | bytes 24584 | tf_op jit(solution)/shard_map/ppermute | solution.py:162
  110.2 7.7 %collective-permute-start.40 = (f32[512,128]{1,0:T(8,128)S(1)}, f32[512,128]{1,0:T(8,128)S(1)}, u32[]{:S(2)}, u32[]{:S(2)}) collective-permute-start(f32[512,128]{1,0:T(8,128)S(1)} %add_select_fusion.3), channel_id=1, source_target_pairs={{0,1},{1,0},{2,3},{3,2},{4,5},{5,4},{6,7},{7,6},{8,9},{9,8},{10,11... | collective-permute-start | bytes 786440 | tf_op jit(solution)/shard_map/ppermute | solution.py:162
  (24 other events, 97.0 us)

commit v3 on v2

--- a/solution.py
+++ b/solution.py
@@ -51,7 +51,15 @@
     return jnp.sum(dot(parts(row), matrix, NN), axis=0, keepdims=True)
 
 
-def state_kernel(k_ref, v_ref, state_ref, norm_ref):
+def state_kernel(k_hbm, v_hbm, state_ref, norm_ref, k_ref, v_ref, sems):
+    copies = [
+        pltpu.make_async_copy(k_hbm, k_ref, sems.at[0]),
+        pltpu.make_async_copy(v_hbm, v_ref, sems.at[1]),
+    ]
+    for copy in copies:
+        copy.start()
+    for copy in copies:
+        copy.wait()
     for h in range(k_ref.shape[1] // HD):
         at = columns(h)
         k_feat = features(k_ref[:, at].astype(F32))
@@ -135,22 +143,27 @@
 
 
 COST = dict(state=1.0, weights=1.0, later=1.0, near=1.0, attend=1.0, query=1.0, key=1.0)
-CHUNKS = (2, 2)
+CHUNKS = ((2, 0), (2, 0))
 RADIX = 2
-EARLY = ("N", "S0<N", "S1<N", "N", "N", "N")
-GATE = "S0"
-LATE = ()
-LAST = ()
+INNER_FIRST = (True, True)
+PIECE = 256
+EARLY = ('S0', 'N', 'N', 'N<S0')
+GATE = "S0.0.0"
+NEAR_GATE = ""
+QUERY_GATE = "L0.5"
+LATE = ('S0', 'L0', 'S0', 'L0', 'S0', 'L0', 'S0', 'L0', 'S0', 'L0', 'S0', 'L0')
+LAST = ('M', 'M', 'M', 'L0')
 VMEM = 16
 
 
-def call(name, kernel, outs, *args):
+def call(name, kernel, outs, *args, **more):
     return pl.pallas_call(
         kernel,
         out_shape=[jax.ShapeDtypeStruct(shape, kind) for shape, kind in outs],
         compiler_params=pltpu.CompilerParams(vmem_limit_bytes=VMEM << 20),
         cost_estimate=pl.CostEstimate(flops=0, bytes_accessed=int(COST[name] * 3.5e6), transcendentals=0),
         name=name,
+        **more,
     )(*args)
 
 
@@ -159,7 +172,10 @@
 
 
 def swap(part, axis, mask):
-    return lax.ppermute(part, axis, [(i, i ^ mask) for i in range(lax.axis_size(axis))])
+    route = [(i, i ^ mask) for i in range(lax.axis_size(axis))]
+    pieces = [part[at : at + PIECE] for at in range(0, part.shape[0], PIECE)]
+    got = [lax.ppermute(piece, axis, route) for piece in pieces]
+    return jnp.concatenate(got) if len(got) > 1 else got[0]
 
 
 def is_late(axis, mask, backward):
@@ -186,32 +202,55 @@
     return before
 
 
-def scan_small(part, backward):
-    levels = groups("inner", 0, RADIX) + [("outer", [1])] + groups("outer", 1, RADIX)
-    return add_up(part, levels, backward)
-
-
-def scan_large(part, backward):
+def scan_small(part, backward, inner_first):
+    if inner_first:
+        levels = groups("inner", 0, RADIX) + [("outer", [1])] + groups("outer", 1, RADIX)
+        return (yield from add_up(part, levels, backward))
+    before = yield from add_up(part, [("outer", [1])] + groups("outer", 1, RADIX), backward)
+    rows = part.shape[0]
+    upto, result = before + part, before
+    for axis, masks in groups("inner", 0, RADIX):
+        both = jnp.concatenate([before, upto])
+        got = yield [(both, axis, mask) for mask in masks]
+        for mask, other in zip(masks, got):
+            result = result + jnp.where(is_late(axis, mask, backward), other[rows:], other[:rows])
+            before, upto = before + other[:rows], upto + other[rows:]
+    return result
+
+
+def scan_large(part, backward, chunks, joined):
+    size = part.shape[0] // chunks
+    parts = [part[i * size : (i + 1) * size] for i in range(chunks)]
     halving = [("inner", 1 << b) for b in range(bits("inner"))] + [("outer", 1)]
     lows = []
-    for axis, mask in halving:
+    for step, (axis, mask) in enumerate(halving):
+        if axis == "outer":
+            parts = [jnp.concatenate(parts)]
         late = is_late(axis, mask, backward)
-        half = part.shape[0] // 2
-        first, second = part[:half], part[half:]
-        mine = jnp.where(late, second, first)
-        (got,) = yield [(jnp.where(late, first, second), axis, mask)]
-        lows.append(jnp.where(late, got, mine))
-        part = mine + got
-    before = yield from add_up(part, groups("outer", 1, RADIX), backward)
+        half = parts[0].shape[0] // 2
+        sends = [jnp.where(late, part[:half], part[half:]) for part in parts]
+        if step < joined:
+            sends = [jnp.concatenate(sends)]
+        got = yield [(send, axis, mask) for send in sends]
+        if len(got) < len(parts):
+            got = [got[0][i * half : (i + 1) * half] for i in range(len(parts))]
+        mine = [jnp.where(late, part[half:], part[:half]) for part in parts]
+        lows.append([jnp.where(late, other, own) for other, own in zip(got, mine)])
+        parts = [own + other for own, other in zip(mine, got)]
+    befores = [(yield from add_up(parts[0], groups("outer", 1, RADIX), backward))]
     for (axis, mask), low in zip(reversed(halving), reversed(lows)):
+        if len(low) > len(befores):
+            size = befores[0].shape[0] // chunks
+            befores = [befores[0][i * size : (i + 1) * size] for i in range(chunks)]
         late = is_late(axis, mask, backward)
-        both = before + low
-        mine = jnp.where(late, both, before)
-        (got,) = yield [(jnp.where(late, before, both), axis, mask)]
-        first = jnp.where(late, got, mine)
-        second = jnp.where(late, mine, got)
-        before = jnp.concatenate([first, second])
-    return before
+        both = [before + other for before, other in zip(befores, low)]
+        got = yield [(jnp.where(late, before, full), axis, mask) for before, full in zip(befores, both)]
+        mine = [jnp.where(late, full, before) for before, full in zip(befores, both)]
+        befores = [
+            jnp.concatenate([jnp.where(late, other, own), jnp.where(late, own, other)])
+            for other, own in zip(got, mine)
+        ]
+    return jnp.concatenate(befores)
 
 
 class Chain:
@@ -231,16 +270,16 @@
 
 
 def split(part, chunks, backward):
-    size = part.shape[0] // chunks
-    return [Chain(scan_large(part[i * size : (i + 1) * size], backward)) for i in range(chunks)]
+    return [Chain(scan_large(part, backward, *chunks))]
 
 
 def last(chains, names):
     found = []
-    for name, _, hop in (entry.partition(".") for entry in names.split(",")):
+    for name, *place in (entry.split(".") for entry in names.split(",")):
         if name in chains and chains[name].arrived:
             arrived = chains[name].arrived
-            found.extend(arrived[min(int(hop), len(arrived) - 1)] if hop else arrived[-1])
+            got = arrived[min(int(place[0]), len(arrived) - 1)] if place else arrived[-1]
+            found.extend(got[int(place[1]) % len(got) :][:1] if place[1:] else got)
     return found
 
 
@@ -266,8 +305,12 @@
     heads = width // HD
     flat, turned, square, pairs = (tokens, width), (width, tokens), (width, HD), (tokens, heads * tokens)
     small, column = (heads, HD), (heads, tokens)
-    local_state, local_norm = call("state", state_kernel, [(square, F32), (small, F32)], keys, values)
-    chains = {"N": Chain(scan_small(local_norm, False))}
+    local_state, local_norm = call(
+        "state", state_kernel, [(square, F32), (small, F32)], keys, values,
+        in_specs=[pl.BlockSpec(memory_space=pltpu.HBM)] * 2,
+        scratch_shapes=[pltpu.VMEM(flat, BF16), pltpu.VMEM(flat, BF16), pltpu.SemaphoreType.DMA((2,))],
+    )
+    chains = {"N": Chain(scan_small(local_norm, False, INNER_FIRST[0]))}
     chains.update(("S%d" % i, chain) for i, chain in enumerate(split(local_state, CHUNKS[0], False)))
     run(chains, EARLY)
     normal = tie(drain(chains, "N"), last(chains, GATE))
@@ -283,19 +326,19 @@
     run(chains, LATE)
     state = drain(chains, "S")
     near_num, near_scores, near_values, plain = call(
-        "near", near_kernel, [(turned, F32), (pairs, F32), (flat, F32), (flat, BF16)], weights, scaled, values
+        "near", near_kernel, [(turned, F32), (pairs, F32), (flat, F32), (flat, BF16)], weights, tie(scaled, last(chains, NEAR_GATE)), values
     )
     ratio, grad_den, local_lnorm = call(
         "attend", attend_kernel, [(turned, BF16), (column, F32), (small, F32)],
         q_feat, q_turned, c_turned, inverse, near_num, state,
     )
-    chains["M"] = Chain(scan_small(local_lnorm, True))
+    chains["M"] = Chain(scan_small(local_lnorm, True, INNER_FIRST[1]))
     run(chains, LAST)
     later_norm = drain(chains, "M")
     later = drain(chains, "L")
     attended, query_grad, near_keys = call(
         "query", query_kernel, [(flat, BF16), (flat, BF16), (flat, F32)],
-        queries, q_feat, k_feat, plain, ratio, grad_den, normal, near_scores, state,
+        queries, q_feat, k_feat, plain, ratio, tie(grad_den, last(chains, QUERY_GATE)), normal, near_scores, state,
     )
     key_grad, value_grad = call(
         "key", key_kernel, [(flat, BF16), (flat, BF16)],

time: 120 us -> 112 us (0.933)
  waiting for transfers between devices: 56.4 us -> 46.4 us
  starting transfers between devices: 49.4 us -> 51.3 us
    ppermute x50 -> x48, waiting for transfers between devices: 56.4 us -> 46.4 us  [swap(): got = [lax.ppermute(piece, axis, route) for piece in pieces]]
    ppermute x50 -> x48, starting transfers between devices: 49.4 us -> 51.3 us  [swap(): got = [lax.ppermute(piece, axis, route) for piece in pieces]]
  transfers between devices with their start and end apart: 50 -> 48, of which waited for: 28 -> 25; matrix products, arithmetic and copies ran while one was open for 2% -> 2% of each run, Pallas kernels for 5% -> 6%
where the time goes in v3:
time: 112 us
  starting transfers between devices  51.3 us (46%)
  waiting for transfers between devices  46.4 us (41%)
  Pallas kernels  8.55 us (8%)
  local copies, waits for them, and re-layouts  2.42 us (2%)
  other arithmetic  1.82 us (2%)
  between operations  1.24 us (1%)
    ppermute x48, starting transfers between devices, swap(): got = [lax.ppermute(piece, axis, route) for piece in pieces]  51.3 us
    ppermute x48, waiting for transfers between devices, swap(): got = [lax.ppermute(piece, axis, route) for piece in pieces]  46.4 us
    pallas_call x7, Pallas kernels, call(): pl.pallas_call(kernel, out_shape=[jax.ShapeDtypeStruct(shape, kind) for s...  8.55 us
  transfers between devices with their start and end apart: 48, of which 25 were waited for; matrix products, arithmetic and copies ran while one was open for 2% of the time, Pallas kernels for 6%

profile of v3, /device:TPU:0, one launch (start us, length us, event | category | flops | bytes accessed | tf_op | source)
XLA Modules:
  0.0 111.7 jit_solution(15304142881224631079)
XLA Ops:
  3.4 5.1 %collective-permute-start.2 = (f32[16,128]{1,0:T(8,128)S(1)}, f32[16,128]{1,0:T(8,128)S(1)}, u32[]{:S(2)}, u32[]{:S(2)}) collective-permute-start(f32[16,128]{1,0:T(8,128)S(1)} %get-tuple-element.36), channel_id=1, source_target_pairs={{0,3},{1,2},{2,1},{3,0},{4,7},{5,6},{6,5},{7,4},{8,11},{9,10},{10,... | collective-permute-start | bytes 24584 | tf_op jit(solution)/shard_map/ppermute | solution.py:177
  9.2 1.5 %collective-permute-start.5 = (f32[256,128]{1,0:T(8,128)S(1)}, f32[256,128]{1,0:T(8,128)S(1)}, u32[]{:S(2)}, u32[]{:S(2)}) collective-permute-start(f32[256,128]{1,0:T(8,128)S(1)} %get-tuple-element.115), channel_id=1, source_target_pairs={{0,1},{1,0},{2,3},{3,2},{4,5},{5,4},{6,7},{7,6},{8,9},{9,8},{10,11... | collective-permute-start | bytes 393224 | tf_op jit(solution)/shard_map/ppermute | solution.py:177
  11.3 1.8 %collective-permute-done.1 = f32[16,128]{1,0:T(8,128)S(1)} collective-permute-done((f32[16,128]{1,0:T(8,128)S(1)}, f32[16,128]{1,0:T(8,128)S(1)}, u32[]{:S(2)}, u32[]{:S(2)}) %collective-permute-start.1) | collective-permute-done | bytes 8224 | tf_op jit(solution)/shard_map/ppermute | solution.py:177
  14.4 2.6 %collective-permute-done.4 = f32[256,128]{1,0:T(8,128)S(1)} collective-permute-done((f32[256,128]{1,0:T(8,128)S(1)}, f32[256,128]{1,0:T(8,128)S(1)}, u32[]{:S(2)}, u32[]{:S(2)}) %collective-permute-start.4) | collective-permute-done | bytes 131104 | tf_op jit(solution)/shard_map/ppermute | solution.py:177
  19.3 2.2 %collective-permute-start.12 = (f32[256,128]{1,0:T(8,128)S(1)}, f32[256,128]{1,0:T(8,128)S(1)}, u32[]{:S(2)}, u32[]{:S(2)}) collective-permute-start(f32[256,128]{1,0:T(8,128)S(1)} %slice_select_fusion.12), channel_id=1, source_target_pairs={{0,2},{1,3},{2,0},{3,1},{4,6},{5,7},{6,4},{7,5},{8,10},{9,11},{10,... | collective-permute-start | bytes 393224 | tf_op jit(solution)/shard_map/ppermute | solution.py:177
  21.5 5.2 %collective-permute-done.6 = f32[256,128]{1,0:T(8,128)S(1)} collective-permute-done((f32[256,128]{1,0:T(8,128)S(1)}, f32[256,128]{1,0:T(8,128)S(1)}, u32[]{:S(2)}, u32[]{:S(2)}) %collective-permute-start.6) | collective-permute-done | bytes 131104 | tf_op jit(solution)/shard_map/ppermute | solution.py:177
  26.9 2.4 %collective-permute-start.10 = (f32[16,128]{1,0:T(8,128)S(1)}, f32[16,128]{1,0:T(8,128)S(1)}, u32[]{:S(2)}, u32[]{:S(2)}) collective-permute-start(f32[16,128]{1,0:T(8,128)S(1)} %add.138), channel_id=1, source_target_pairs={{0,24},{4,28},{8,16},{12,20},{16,8},{20,12},{24,0},{28,4},{1,25},{... | collective-permute-start | bytes 24584 | tf_op jit(solution)/shard_map/ppermute | solution.py:177
  33.5 1.7 %later.1 = (f32[2048,128]{1,0:T(8,128)S(1)}, bf16[2048,128]{1,0:T(8,128)(2,1)S(1)}, f32[16,128]{1,0:T(8,128)S(1)}) custom-call(bf16[2048,128]{1,0:T(8,128)(2,1)S(1)} %get-tuple-element.33.qt_ref, bf16[2048,128]{1,0:T(8,128)(2,1)S(1)} %get-tuple-element.34.ct_ref, f32[16,128]{1,0:T(8,128)S(1)} %get-tuple-element.35.part_ref, ...), custom_call_target="tpu_custom_call" | custom-call | bytes 3500000 | tf_op jit(solution)/shard_map/later/pallas_call | solution.py:160
  35.6 1.7 %collective-permute-start.24 = (f32[256,128]{1,0:T(8,128)S(1)}, f32[256,128]{1,0:T(8,128)S(1)}, u32[]{:S(2)}, u32[]{:S(2)}) collective-permute-start(f32[256,128]{1,0:T(8,128)S(1)} %get-tuple-element.106), channel_id=1, source_target_pairs={{0,1},{1,0},{2,3},{3,2},{4,5},{5,4},{6,7},{7,6},{8,9},{9,8},{10,11... | collective-permute-start | bytes 393224 | tf_op jit(solution)/shard_map/ppermute | solution.py:177
  38.6 1.8 %collective-permute-start.27 = (f32[256,128]{1,0:T(8,128)S(1)}, f32[256,128]{1,0:T(8,128)S(1)}, u32[]{:S(2)}, u32[]{:S(2)}) collective-permute-start(f32[256,128]{1,0:T(8,128)S(1)} %get-tuple-element.108), channel_id=1, source_target_pairs={{0,1},{1,0},{2,3},{3,2},{4,5},{5,4},{6,7},{7,6},{8,9},{9,8},{10,11... | collective-permute-start | bytes 393224 | tf_op jit(solution)/shard_map/ppermute | solution.py:177
  40.5 1.6 %collective-permute-done.24 = f32[256,128]{1,0:T(8,128)S(1)} collective-permute-done((f32[256,128]{1,0:T(8,128)S(1)}, f32[256,128]{1,0:T(8,128)S(1)}, u32[]{:S(2)}, u32[]{:S(2)}) %collective-permute-start.24) | collective-permute-done | bytes 131104 | tf_op jit(solution)/shard_map/ppermute | solution.py:177
  42.1 3.1 %collective-permute-done.27 = f32[256,128]{1,0:T(8,128)S(1)} collective-permute-done((f32[256,128]{1,0:T(8,128)S(1)}, f32[256,128]{1,0:T(8,128)S(1)}, u32[]{:S(2)}, u32[]{:S(2)}) %collective-permute-start.27) | collective-permute-done | bytes 131104 | tf_op jit(solution)/shard_map/ppermute | solution.py:177
  45.4 2.6 %collective-permute-start.29 = (f32[256,128]{1,0:T(8,128)S(1)}, f32[256,128]{1,0:T(8,128)S(1)}, u32[]{:S(2)}, u32[]{:S(2)}) collective-permute-start(f32[256,128]{1,0:T(8,128)S(1)} %slice_select_fusion.8), channel_id=1, source_target_pairs={{0,2},{1,3},{2,0},{3,1},{4,6},{5,7},{6,4},{7,5},{8,10},{9,11},{10,... | collective-permute-start | bytes 393224 | tf_op jit(solution)/shard_map/ppermute | solution.py:177
  48.5 3.4 %collective-permute-start.16 = (f32[256,128]{1,0:T(8,128)S(1)}, f32[256,128]{1,0:T(8,128)S(1)}, u32[]{:S(2)}, u32[]{:S(2)}) collective-permute-start(f32[256,128]{1,0:T(8,128)S(1)} %get-tuple-element.77), channel_id=1, source_target_pairs={{0,24},{4,28},{8,16},{12,20},{16,8},{20,12},{24,0},{28,4},{1,25},{... | collective-permute-start | bytes 393224 | tf_op jit(solution)/shard_map/ppermute | solution.py:177
  52.5 2.1 %collective-permute-done.29 = f32[256,128]{1,0:T(8,128)S(1)} collective-permute-done((f32[256,128]{1,0:T(8,128)S(1)}, f32[256,128]{1,0:T(8,128)S(1)}, u32[]{:S(2)}, u32[]{:S(2)}) %collective-permute-start.29) | collective-permute-done | bytes 131104 | tf_op jit(solution)/shard_map/ppermute | solution.py:177
  57.5 2.9 %collective-permute-start.33 = (f32[256,128]{1,0:T(8,128)S(1)}, f32[256,128]{1,0:T(8,128)S(1)}, u32[]{:S(2)}, u32[]{:S(2)}) collective-permute-start(f32[256,128]{1,0:T(8,128)S(1)} %get-tuple-element.62), channel_id=1, source_target_pairs={{0,24},{4,28},{8,16},{12,20},{16,8},{20,12},{24,0},{28,4},{1,25},{... | collective-permute-start | bytes 393224 | tf_op jit(solution)/shard_map/ppermute | solution.py:177
  62.4 2.1 %collective-permute-done.33 = f32[256,128]{1,0:T(8,128)S(1)} collective-permute-done((f32[256,128]{1,0:T(8,128)S(1)}, f32[256,128]{1,0:T(8,128)S(1)}, u32[]{:S(2)}, u32[]{:S(2)}) %collective-permute-start.33) | collective-permute-done | bytes 131104 | tf_op jit(solution)/shard_map/ppermute | solution.py:177
  64.5 2.6 %collective-permute-done.32 = f32[256,128]{1,0:T(8,128)S(1)} collective-permute-done((f32[256,128]{1,0:T(8,128)S(1)}, f32[256,128]{1,0:T(8,128)S(1)}, u32[]{:S(2)}, u32[]{:S(2)}) %collective-permute-start.32) | collective-permute-done | bytes 131104 | tf_op jit(solution)/shard_map/ppermute | solution.py:177
  67.4 2.5 %collective-permute-done.18 = f32[256,128]{1,0:T(8,128)S(1)} collective-permute-done((f32[256,128]{1,0:T(8,128)S(1)}, f32[256,128]{1,0:T(8,128)S(1)}, u32[]{:S(2)}, u32[]{:S(2)}) %collective-permute-start.18) | collective-permute-done | bytes 131104 | tf_op jit(solution)/shard_map/ppermute | solution.py:177
  70.2 2.7 %collective-permute-start.20 = (f32[256,128]{1,0:T(8,128)S(1)}, f32[256,128]{1,0:T(8,128)S(1)}, u32[]{:S(2)}, u32[]{:S(2)}) collective-permute-start(f32[256,128]{1,0:T(8,128)S(1)} %get-tuple-element.109), channel_id=1, source_target_pairs={{0,1},{1,0},{2,3},{3,2},{4,5},{5,4},{6,7},{7,6},{8,9},{9,8},{10,11... | collective-permute-start | bytes 393224 | tf_op jit(solution)/shard_map/ppermute | solution.py:177
  73.0 2.3 %collective-permute-start.35 = (f32[256,128]{1,0:T(8,128)S(1)}, f32[256,128]{1,0:T(8,128)S(1)}, u32[]{:S(2)}, u32[]{:S(2)}) collective-permute-start(f32[256,128]{1,0:T(8,128)S(1)} %add_select_fusion.11), channel_id=1, source_target_pairs={{0,2},{1,3},{2,0},{3,1},{4,6},{5,7},{6,4},{7,5},{8,10},{9,11},{10,... | collective-permute-start | bytes 393224 | tf_op jit(solution)/shard_map/ppermute | solution.py:177
  75.3 3.6 %collective-permute-done.21 = f32[256,128]{1,0:T(8,128)S(1)} collective-permute-done((f32[256,128]{1,0:T(8,128)S(1)}, f32[256,128]{1,0:T(8,128)S(1)}, u32[]{:S(2)}, u32[]{:S(2)}) %collective-permute-start.21) | collective-permute-done | bytes 131104 | tf_op jit(solution)/shard_map/ppermute | solution.py:177
  79.2 2.0 %collective-permute-start.22 = (f32[256,128]{1,0:T(8,128)S(1)}, f32[256,128]{1,0:T(8,128)S(1)}, u32[]{:S(2)}, u32[]{:S(2)}) collective-permute-start(f32[256,128]{1,0:T(8,128)S(1)} %get-tuple-element.112), channel_id=1, source_target_pairs={{0,1},{1,0},{2,3},{3,2},{4,5},{5,4},{6,7},{7,6},{8,9},{9,8},{10,11... | collective-permute-start | bytes 393224 | tf_op jit(solution)/shard_map/ppermute | solution.py:177
  81.2 4.1 %collective-permute-done.19 = f32[256,128]{1,0:T(8,128)S(1)} collective-permute-done((f32[256,128]{1,0:T(8,128)S(1)}, f32[256,128]{1,0:T(8,128)S(1)}, u32[]{:S(2)}, u32[]{:S(2)}) %collective-permute-start.19) | collective-permute-done | bytes 131104 | tf_op jit(solution)/shard_map/ppermute | solution.py:177
  86.1 2.3 %collective-permute-start.45 = (f32[256,128]{1,0:T(8,128)S(1)}, f32[256,128]{1,0:T(8,128)S(1)}, u32[]{:S(2)}, u32[]{:S(2)}) collective-permute-start(f32[256,128]{1,0:T(8,128)S(1)} %get-tuple-element.101), channel_id=1, source_target_pairs={{0,1},{1,0},{2,3},{3,2},{4,5},{5,4},{6,7},{7,6},{8,9},{9,8},{10,11... | collective-permute-start | bytes 393224 | tf_op jit(solution)/shard_map/ppermute | solution.py:177
  88.5 4.6 %collective-permute-done.22 = f32[256,128]{1,0:T(8,128)S(1)} collective-permute-done((f32[256,128]{1,0:T(8,128)S(1)}, f32[256,128]{1,0:T(8,128)S(1)}, u32[]{:S(2)}, u32[]{:S(2)}) %collective-permute-start.22) | collective-permute-done | bytes 131104 | tf_op jit(solution)/shard_map/ppermute | solution.py:177
  93.9 2.8 %collective-permute-start.39 = (f32[16,128]{1,0:T(8,128)S(1)}, f32[16,128]{1,0:T(8,128)S(1)}, u32[]{:S(2)}, u32[]{:S(2)}) collective-permute-start(f32[16,128]{1,0:T(8,128)S(1)} %get-tuple-element.53), channel_id=1, source_target_pairs={{0,3},{1,2},{2,1},{3,0},{4,7},{5,6},{6,5},{7,4},{8,11},{9,10},{10,... | collective-permute-start | bytes 24584 | tf_op jit(solution)/shard_map/ppermute | solution.py:177
  96.7 1.7 %collective-permute-start.37 = (f32[16,128]{1,0:T(8,128)S(1)}, f32[16,128]{1,0:T(8,128)S(1)}, u32[]{:S(2)}, u32[]{:S(2)}) collective-permute-start(f32[16,128]{1,0:T(8,128)S(1)} %get-tuple-element.53), channel_id=1, source_target_pairs={{0,1},{1,0},{2,3},{3,2},{4,5},{5,4},{6,7},{7,6},{8,9},{9,8},{10,11... | collective-permute-start | bytes 24584 | tf_op jit(solution)/shard_map/ppermute | solution.py:177
  99.5 1.9 %collective-permute-done.38 = f32[16,128]{1,0:T(8,128)S(1)} collective-permute-done((f32[16,128]{1,0:T(8,128)S(1)}, f32[16,128]{1,0:T(8,128)S(1)}, u32[]{:S(2)}, u32[]{:S(2)}) %collective-permute-start.38) | collective-permute-done | bytes 8224 | tf_op jit(solution)/shard_map/ppermute | solution.py:177
  102.7 2.1 %collective-permute-start.43 = (f32[16,128]{1,0:T(8,128)S(1)}, f32[16,128]{1,0:T(8,128)S(1)}, u32[]{:S(2)}, u32[]{:S(2)}) collective-permute-start(f32[16,128]{1,0:T(8,128)S(1)} %add.170), channel_id=1, source_target_pairs={{0,24},{4,28},{8,16},{12,20},{16,8},{20,12},{24,0},{28,4},{1,25},{... | collective-permute-start | bytes 24584 | tf_op jit(solution)/shard_map/ppermute | solution.py:177
  106.3 2.3 %query.1 = (bf16[128,2048]{1,0:T(8,128)(2,1)}, bf16[128,2048]{1,0:T(8,128)(2,1)}, f32[128,2048]{1,0:T(8,128)S(1)}) custom-call(bf16[128,2048]{1,0:T(8,128)(2,1)S(1)} %copy-done.4, bf16[128,2048]{1,0:T(8,128)(2,1)S(1)} %get-tuple-element.30.qf_ref, bf16[128,2048]{1,0:T(8,128)(2,1)S(1)} %get-tuple-element.31.kf_ref, ...), custom_call_target="tpu_custom_call" | custom-call | bytes 3500000 | tf_op jit(solution)/shard_map/query/pallas_call | solution.py:160
  110.0 1.7 %key.1 = (bf16[128,2048]{1,0:T(8,128)(2,1)}, bf16[128,2048]{1,0:T(8,128)(2,1)}) custom-call(bf16[128,2048]{1,0:T(8,128)(2,1)S(1)} %copy-done.1, bf16[128,2048]{1,0:T(8,128)(2,1)S(1)} %get-tuple-element.31.kf_ref, bf16[128,2048]{1,0:T(8,128)(2,1)S(1)} %copy-done.3, f32[128,2048]{1,0:T(8,128)S(1)} %get-tuple-element.51.ki_ref, ...), custom_call_target="tpu_custom_call" | custom-call | bytes 3500000 | tf_op jit(solution)/shard_map/key/pallas_call | solution.py:160
  (148 shorter events, 27.5 us)
Async XLA Ops:
  3.4 7.9 %collective-permute-start.2 = (f32[16,128]{1,0:T(8,128)S(1)}, f32[16,128]{1,0:T(8,128)S(1)}, u32[]{:S(2)}, u32[]{:S(2)}) collective-permute-start(f32[16,128]{1,0:T(8,128)S(1)} %get-tuple-element.36), channel_id=1, source_target_pairs={{0,3},{1,2},{2,1},{3,0},{4,7},{5,6},{6,5},{7,4},{8,11},{9,10},{10,... | collective-permute-start | bytes 24584 | tf_op jit(solution)/shard_map/ppermute | solution.py:177
  9.2 7.8 %collective-permute-start.5 = (f32[256,128]{1,0:T(8,128)S(1)}, f32[256,128]{1,0:T(8,128)S(1)}, u32[]{:S(2)}, u32[]{:S(2)}) collective-permute-start(f32[256,128]{1,0:T(8,128)S(1)} %get-tuple-element.115), channel_id=1, source_target_pairs={{0,1},{1,0},{2,3},{3,2},{4,5},{5,4},{6,7},{7,6},{8,9},{9,8},{10,11... | collective-permute-start | bytes 393224 | tf_op jit(solution)/shard_map/ppermute | solution.py:177
  10.7 6.4 %collective-permute-start.4 = (f32[256,128]{1,0:T(8,128)S(1)}, f32[256,128]{1,0:T(8,128)S(1)}, u32[]{:S(2)}, u32[]{:S(2)}) collective-permute-start(f32[256,128]{1,0:T(8,128)S(1)} %get-tuple-element.116), channel_id=1, source_target_pairs={{0,1},{1,0},{2,3},{3,2},{4,5},{5,4},{6,7},{7,6},{8,9},{9,8},{10,11... | collective-permute-start | bytes 393224 | tf_op jit(solution)/shard_map/ppermute | solution.py:177
  17.2 9.6 %collective-permute-start.7 = (f32[256,128]{1,0:T(8,128)S(1)}, f32[256,128]{1,0:T(8,128)S(1)}, u32[]{:S(2)}, u32[]{:S(2)}) collective-permute-start(f32[256,128]{1,0:T(8,128)S(1)} %get-tuple-element.113), channel_id=1, source_target_pairs={{0,1},{1,0},{2,3},{3,2},{4,5},{5,4},{6,7},{7,6},{8,9},{9,8},{10,11... | collective-permute-start | bytes 393224 | tf_op jit(solution)/shard_map/ppermute | solution.py:177
  18.5 8.3 %collective-permute-start.6 = (f32[256,128]{1,0:T(8,128)S(1)}, f32[256,128]{1,0:T(8,128)S(1)}, u32[]{:S(2)}, u32[]{:S(2)}) collective-permute-start(f32[256,128]{1,0:T(8,128)S(1)} %get-tuple-element.114), channel_id=1, source_target_pairs={{0,1},{1,0},{2,3},{3,2},{4,5},{5,4},{6,7},{7,6},{8,9},{9,8},{10,11... | collective-permute-start | bytes 393224 | tf_op jit(solution)/shard_map/ppermute | solution.py:177
  19.3 19.2 %collective-permute-start.12 = (f32[256,128]{1,0:T(8,128)S(1)}, f32[256,128]{1,0:T(8,128)S(1)}, u32[]{:S(2)}, u32[]{:S(2)}) collective-permute-start(f32[256,128]{1,0:T(8,128)S(1)} %slice_select_fusion.12), channel_id=1, source_target_pairs={{0,2},{1,3},{2,0},{3,1},{4,6},{5,7},{6,4},{7,5},{8,10},{9,11},{10,... | collective-permute-start | bytes 393224 | tf_op jit(solution)/shard_map/ppermute | solution.py:177
  30.5 9.9 %collective-permute-start.11 = (f32[256,128]{1,0:T(8,128)S(1)}, f32[256,128]{1,0:T(8,128)S(1)}, u32[]{:S(2)}, u32[]{:S(2)}) collective-permute-start(f32[256,128]{1,0:T(8,128)S(1)} %slice_select_fusion.14), channel_id=1, source_target_pairs={{0,2},{1,3},{2,0},{3,1},{4,6},{5,7},{6,4},{7,5},{8,10},{9,11},{10,... | collective-permute-start | bytes 393224 | tf_op jit(solution)/shard_map/ppermute | solution.py:177
  35.2 10.0 %collective-permute-start.25 = (f32[256,128]{1,0:T(8,128)S(1)}, f32[256,128]{1,0:T(8,128)S(1)}, u32[]{:S(2)}, u32[]{:S(2)}) collective-permute-start(f32[256,128]{1,0:T(8,128)S(1)} %get-tuple-element.105), channel_id=1, source_target_pairs={{0,1},{1,0},{2,3},{3,2},{4,5},{5,4},{6,7},{7,6},{8,9},{9,8},{10,11... | collective-permute-start | bytes 393224 | tf_op jit(solution)/shard_map/ppermute | solution.py:177
  35.6 6.5 %collective-permute-start.24 = (f32[256,128]{1,0:T(8,128)S(1)}, f32[256,128]{1,0:T(8,128)S(1)}, u32[]{:S(2)}, u32[]{:S(2)}) collective-permute-start(f32[256,128]{1,0:T(8,128)S(1)} %get-tuple-element.106), channel_id=1, source_target_pairs={{0,1},{1,0},{2,3},{3,2},{4,5},{5,4},{6,7},{7,6},{8,9},{9,8},{10,11... | collective-permute-start | bytes 393224 | tf_op jit(solution)/shard_map/ppermute | solution.py:177
  37.3 7.9 %collective-permute-start.28 = (f32[256,128]{1,0:T(8,128)S(1)}, f32[256,128]{1,0:T(8,128)S(1)}, u32[]{:S(2)}, u32[]{:S(2)}) collective-permute-start(f32[256,128]{1,0:T(8,128)S(1)} %get-tuple-element.107), channel_id=1, source_target_pairs={{0,1},{1,0},{2,3},{3,2},{4,5},{5,4},{6,7},{7,6},{8,9},{9,8},{10,11... | collective-permute-start | bytes 393224 | tf_op jit(solution)/shard_map/ppermute | solution.py:177
  38.6 6.6 %collective-permute-start.27 = (f32[256,128]{1,0:T(8,128)S(1)}, f32[256,128]{1,0:T(8,128)S(1)}, u32[]{:S(2)}, u32[]{:S(2)}) collective-permute-start(f32[256,128]{1,0:T(8,128)S(1)} %get-tuple-element.108), channel_id=1, source_target_pairs={{0,1},{1,0},{2,3},{3,2},{4,5},{5,4},{6,7},{7,6},{8,9},{9,8},{10,11... | collective-permute-start | bytes 393224 | tf_op jit(solution)/shard_map/ppermute | solution.py:177
  40.4 8.0 %collective-permute-start.13 = (f32[256,128]{1,0:T(8,128)S(1)}, f32[256,128]{1,0:T(8,128)S(1)}, u32[]{:S(2)}, u32[]{:S(2)}) collective-permute-start(f32[256,128]{1,0:T(8,128)S(1)} %get-tuple-element.79), channel_id=1, source_target_pairs={{0,4},{4,0},{8,12},{12,8},{16,20},{20,16},{24,28},{28,24},{1,5},{5... | collective-permute-start | bytes 393224 | tf_op jit(solution)/shard_map/ppermute | solution.py:177
  45.4 9.2 %collective-permute-start.29 = (f32[256,128]{1,0:T(8,128)S(1)}, f32[256,128]{1,0:T(8,128)S(1)}, u32[]{:S(2)}, u32[]{:S(2)}) collective-permute-start(f32[256,128]{1,0:T(8,128)S(1)} %slice_select_fusion.8), channel_id=1, source_target_pairs={{0,2},{1,3},{2,0},{3,1},{4,6},{5,7},{6,4},{7,5},{8,10},{9,11},{10,... | collective-permute-start | bytes 393224 | tf_op jit(solution)/shard_map/ppermute | solution.py:177
  48.0 8.0 %collective-permute-start.26 = (f32[256,128]{1,0:T(8,128)S(1)}, f32[256,128]{1,0:T(8,128)S(1)}, u32[]{:S(2)}, u32[]{:S(2)}) collective-permute-start(f32[256,128]{1,0:T(8,128)S(1)} %slice_select_fusion.10), channel_id=1, source_target_pairs={{0,2},{1,3},{2,0},{3,1},{4,6},{5,7},{6,4},{7,5},{8,10},{9,11},{10,... | collective-permute-start | bytes 393224 | tf_op jit(solution)/shard_map/ppermute | solution.py:177
  48.5 7.7 %collective-permute-start.16 = (f32[256,128]{1,0:T(8,128)S(1)}, f32[256,128]{1,0:T(8,128)S(1)}, u32[]{:S(2)}, u32[]{:S(2)}) collective-permute-start(f32[256,128]{1,0:T(8,128)S(1)} %get-tuple-element.77), channel_id=1, source_target_pairs={{0,24},{4,28},{8,16},{12,20},{16,8},{20,12},{24,0},{28,4},{1,25},{... | collective-permute-start | bytes 393224 | tf_op jit(solution)/shard_map/ppermute | solution.py:177
  57.5 7.0 %collective-permute-start.33 = (f32[256,128]{1,0:T(8,128)S(1)}, f32[256,128]{1,0:T(8,128)S(1)}, u32[]{:S(2)}, u32[]{:S(2)}) collective-permute-start(f32[256,128]{1,0:T(8,128)S(1)} %get-tuple-element.62), channel_id=1, source_target_pairs={{0,24},{4,28},{8,16},{12,20},{16,8},{20,12},{24,0},{28,4},{1,25},{... | collective-permute-start | bytes 393224 | tf_op jit(solution)/shard_map/ppermute | solution.py:177
  60.4 6.7 %collective-permute-start.32 = (f32[256,128]{1,0:T(8,128)S(1)}, f32[256,128]{1,0:T(8,128)S(1)}, u32[]{:S(2)}, u32[]{:S(2)}) collective-permute-start(f32[256,128]{1,0:T(8,128)S(1)} %get-tuple-element.62), channel_id=1, source_target_pairs={{0,16},{4,20},{8,24},{12,28},{16,0},{20,4},{24,8},{28,12},{1,17},{... | collective-permute-start | bytes 393224 | tf_op jit(solution)/shard_map/ppermute | solution.py:177
  60.8 6.5 %collective-permute-start.31 = (f32[256,128]{1,0:T(8,128)S(1)}, f32[256,128]{1,0:T(8,128)S(1)}, u32[]{:S(2)}, u32[]{:S(2)}) collective-permute-start(f32[256,128]{1,0:T(8,128)S(1)} %get-tuple-element.62), channel_id=1, source_target_pairs={{0,8},{4,12},{8,0},{12,4},{16,24},{20,28},{24,16},{28,20},{1,9},{5... | collective-permute-start | bytes 393224 | tf_op jit(solution)/shard_map/ppermute | solution.py:177
  61.1 8.8 %collective-permute-start.18 = (f32[256,128]{1,0:T(8,128)S(1)}, f32[256,128]{1,0:T(8,128)S(1)}, u32[]{:S(2)}, u32[]{:S(2)}) collective-permute-start(f32[256,128]{1,0:T(8,128)S(1)} %add_select_fusion.17), channel_id=1, source_target_pairs={{0,2},{1,3},{2,0},{3,1},{4,6},{5,7},{6,4},{7,5},{8,10},{9,11},{10,... | collective-permute-start | bytes 393224 | tf_op jit(solution)/shard_map/ppermute | solution.py:177
  67.4 5.7 %collective-permute-start.34 = (f32[256,128]{1,0:T(8,128)S(1)}, f32[256,128]{1,0:T(8,128)S(1)}, u32[]{:S(2)}, u32[]{:S(2)}) collective-permute-start(f32[256,128]{1,0:T(8,128)S(1)} %get-tuple-element.60), channel_id=1, source_target_pairs={{0,4},{4,0},{8,12},{12,8},{16,20},{20,16},{24,28},{28,24},{1,5},{5... | collective-permute-start | bytes 393224 | tf_op jit(solution)/shard_map/ppermute | solution.py:177
  70.0 8.9 %collective-permute-start.21 = (f32[256,128]{1,0:T(8,128)S(1)}, f32[256,128]{1,0:T(8,128)S(1)}, u32[]{:S(2)}, u32[]{:S(2)}) collective-permute-start(f32[256,128]{1,0:T(8,128)S(1)} %get-tuple-element.100), channel_id=1, source_target_pairs={{0,2},{1,3},{2,0},{3,1},{4,6},{5,7},{6,4},{7,5},{8,10},{9,11},{10,... | collective-permute-start | bytes 393224 | tf_op jit(solution)/shard_map/ppermute | solution.py:177
  70.2 15.1 %collective-permute-start.20 = (f32[256,128]{1,0:T(8,128)S(1)}, f32[256,128]{1,0:T(8,128)S(1)}, u32[]{:S(2)}, u32[]{:S(2)}) collective-permute-start(f32[256,128]{1,0:T(8,128)S(1)} %get-tuple-element.109), channel_id=1, source_target_pairs={{0,1},{1,0},{2,3},{3,2},{4,5},{5,4},{6,7},{7,6},{8,9},{9,8},{10,11... | collective-permute-start | bytes 393224 | tf_op jit(solution)/shard_map/ppermute | solution.py:177
  72.9 12.4 %collective-permute-start.19 = (f32[256,128]{1,0:T(8,128)S(1)}, f32[256,128]{1,0:T(8,128)S(1)}, u32[]{:S(2)}, u32[]{:S(2)}) collective-permute-start(f32[256,128]{1,0:T(8,128)S(1)} %get-tuple-element.110), channel_id=1, source_target_pairs={{0,1},{1,0},{2,3},{3,2},{4,5},{5,4},{6,7},{7,6},{8,9},{9,8},{10,11... | collective-permute-start | bytes 393224 | tf_op jit(solution)/shard_map/ppermute | solution.py:177
  73.0 12.4 %collective-permute-start.35 = (f32[256,128]{1,0:T(8,128)S(1)}, f32[256,128]{1,0:T(8,128)S(1)}, u32[]{:S(2)}, u32[]{:S(2)}) collective-permute-start(f32[256,128]{1,0:T(8,128)S(1)} %add_select_fusion.11), channel_id=1, source_target_pairs={{0,2},{1,3},{2,0},{3,1},{4,6},{5,7},{6,4},{7,5},{8,10},{9,11},{10,... | collective-permute-start | bytes 393224 | tf_op jit(solution)/shard_map/ppermute | solution.py:177
  79.1 14.0 %collective-permute-start.23 = (f32[256,128]{1,0:T(8,128)S(1)}, f32[256,128]{1,0:T(8,128)S(1)}, u32[]{:S(2)}, u32[]{:S(2)}) collective-permute-start(f32[256,128]{1,0:T(8,128)S(1)} %get-tuple-element.111), channel_id=1, source_target_pairs={{0,1},{1,0},{2,3},{3,2},{4,5},{5,4},{6,7},{7,6},{8,9},{9,8},{10,11... | collective-permute-start | bytes 393224 | tf_op jit(solution)/shard_map/ppermute | solution.py:177
  79.2 13.9 %collective-permute-start.22 = (f32[256,128]{1,0:T(8,128)S(1)}, f32[256,128]{1,0:T(8,128)S(1)}, u32[]{:S(2)}, u32[]{:S(2)}) collective-permute-start(f32[256,128]{1,0:T(8,128)S(1)} %get-tuple-element.112), channel_id=1, source_target_pairs={{0,1},{1,0},{2,3},{3,2},{4,5},{5,4},{6,7},{7,6},{8,9},{9,8},{10,11... | collective-permute-start | bytes 393224 | tf_op jit(solution)/shard_map/ppermute | solution.py:177
  85.5 11.2 %collective-permute-start.36 = (f32[256,128]{1,0:T(8,128)S(1)}, f32[256,128]{1,0:T(8,128)S(1)}, u32[]{:S(2)}, u32[]{:S(2)}) collective-permute-start(f32[256,128]{1,0:T(8,128)S(1)} %get-tuple-element.99), channel_id=1, source_target_pairs={{0,2},{1,3},{2,0},{3,1},{4,6},{5,7},{6,4},{7,5},{8,10},{9,11},{10,... | collective-permute-start | bytes 393224 | tf_op jit(solution)/shard_map/ppermute | solution.py:177
  86.1 15.5 %collective-permute-start.45 = (f32[256,128]{1,0:T(8,128)S(1)}, f32[256,128]{1,0:T(8,128)S(1)}, u32[]{:S(2)}, u32[]{:S(2)}) collective-permute-start(f32[256,128]{1,0:T(8,128)S(1)} %get-tuple-element.101), channel_id=1, source_target_pairs={{0,1},{1,0},{2,3},{3,2},{4,5},{5,4},{6,7},{7,6},{8,9},{9,8},{10,11... | collective-permute-start | bytes 393224 | tf_op jit(solution)/shard_map/ppermute | solution.py:177
  88.4 13.2 %collective-permute-start.44 = (f32[256,128]{1,0:T(8,128)S(1)}, f32[256,128]{1,0:T(8,128)S(1)}, u32[]{:S(2)}, u32[]{:S(2)}) collective-permute-start(f32[256,128]{1,0:T(8,128)S(1)} %get-tuple-element.102), channel_id=1, source_target_pairs={{0,1},{1,0},{2,3},{3,2},{4,5},{5,4},{6,7},{7,6},{8,9},{9,8},{10,11... | collective-permute-start | bytes 393224 | tf_op jit(solution)/shard_map/ppermute | solution.py:177
  99.5 10.4 %collective-permute-start.47 = (f32[256,128]{1,0:T(8,128)S(1)}, f32[256,128]{1,0:T(8,128)S(1)}, u32[]{:S(2)}, u32[]{:S(2)}) collective-permute-start(f32[256,128]{1,0:T(8,128)S(1)} %get-tuple-element.103), channel_id=1, source_target_pairs={{0,1},{1,0},{2,3},{3,2},{4,5},{5,4},{6,7},{7,6},{8,9},{9,8},{10,11... | collective-permute-start | bytes 393224 | tf_op jit(solution)/shard_map/ppermute | solution.py:177
  101.3 8.5 %collective-permute-start.46 = (f32[256,128]{1,0:T(8,128)S(1)}, f32[256,128]{1,0:T(8,128)S(1)}, u32[]{:S(2)}, u32[]{:S(2)}) collective-permute-start(f32[256,128]{1,0:T(8,128)S(1)} %get-tuple-element.104), channel_id=1, source_target_pairs={{0,1},{1,0},{2,3},{3,2},{4,5},{5,4},{6,7},{7,6},{8,9},{9,8},{10,11... | collective-permute-start | bytes 393224 | tf_op jit(solution)/shard_map/ppermute | solution.py:177
  102.7 5.9 %collective-permute-start.43 = (f32[16,128]{1,0:T(8,128)S(1)}, f32[16,128]{1,0:T(8,128)S(1)}, u32[]{:S(2)}, u32[]{:S(2)}) collective-permute-start(f32[16,128]{1,0:T(8,128)S(1)} %add.170), channel_id=1, source_target_pairs={{0,24},{4,28},{8,16},{12,20},{16,8},{20,12},{24,0},{28,4},{1,25},{... | collective-permute-start | bytes 24584 | tf_op jit(solution)/shard_map/ppermute | solution.py:177
  (22 other events, 84.8 us)

commit v4 on v3

--- a/solution.py
+++ b/solution.py
@@ -51,20 +51,16 @@
     return jnp.sum(dot(parts(row), matrix, NN), axis=0, keepdims=True)
 
 
-def state_kernel(k_hbm, v_hbm, state_ref, norm_ref, k_ref, v_ref, sems):
-    copies = [
-        pltpu.make_async_copy(k_hbm, k_ref, sems.at[0]),
-        pltpu.make_async_copy(v_hbm, v_ref, sems.at[1]),
-    ]
-    for copy in copies:
-        copy.start()
-    for copy in copies:
-        copy.wait()
+def norm_kernel(k_ref, norm_ref):
     for h in range(k_ref.shape[1] // HD):
-        at = columns(h)
-        k_feat = features(k_ref[:, at].astype(F32))
-        state_ref[at, :] = dot(k_feat, v_ref[:, at], TN)
+        k_feat = features(k_ref[:, columns(h)].astype(F32))
         norm_ref[h : h + 1, :] = jnp.sum(k_feat.astype(F32), axis=0, keepdims=True)
+
+
+def state_kernel(k_ref, v_ref, state_ref):
+    for h in range(k_ref.shape[1] // HD):
+        at = columns(h)
+        state_ref[at, :] = dot(features(k_ref[:, at].astype(F32)), v_ref[:, at], TN)
 
 
 def weights_kernel(q_ref, k_ref, c_ref, qf_ref, kf_ref, qt_ref, ct_ref, w_ref, part_ref):
@@ -142,7 +138,7 @@
         vg_ref[:, at] = (vi_ref[:, at] + dot(kf_ref[:, at], later_low, NN)).astype(BF16)
 
 
-COST = dict(state=1.0, weights=1.0, later=1.0, near=1.0, attend=1.0, query=1.0, key=1.0)
+COST = dict(norm=1.0, state=1.0, weights=1.0, later=1.0, near=1.0, attend=1.0, query=1.0, key=1.0)
 CHUNKS = ((2, 0), (2, 0))
 RADIX = 2
 INNER_FIRST = (True, True)
@@ -153,7 +149,7 @@
 QUERY_GATE = "L0.5"
 LATE = ('S0', 'L0', 'S0', 'L0', 'S0', 'L0', 'S0', 'L0', 'S0', 'L0', 'S0', 'L0')
 LAST = ('M', 'M', 'M', 'L0')
-VMEM = 16
+VMEM = 24
 
 
 def call(name, kernel, outs, *args, **more):
@@ -305,11 +301,8 @@
     heads = width // HD
     flat, turned, square, pairs = (tokens, width), (width, tokens), (width, HD), (tokens, heads * tokens)
     small, column = (heads, HD), (heads, tokens)
-    local_state, local_norm = call(
-        "state", state_kernel, [(square, F32), (small, F32)], keys, values,
-        in_specs=[pl.BlockSpec(memory_space=pltpu.HBM)] * 2,
-        scratch_shapes=[pltpu.VMEM(flat, BF16), pltpu.VMEM(flat, BF16), pltpu.SemaphoreType.DMA((2,))],
-    )
+    (local_norm,) = call("norm", norm_kernel, [(small, F32)], keys)
+    (local_state,) = call("state", state_kernel, [(square, F32)], keys, values)
     chains = {"N": Chain(scan_small(local_norm, False, INNER_FIRST[0]))}
     chains.update(("S%d" % i, chain) for i, chain in enumerate(split(local_state, CHUNKS[0], False)))
     run(chains, EARLY)

time: 112 us -> 112 us (level)
    pallas_call x7 -> x8, Pallas kernels: 8.55 us -> 8.68 us  [call(): pl.pallas_call(kernel, out_shape=[jax.ShapeDtypeStruct(shape, kind) for s...]
where the time goes in v4:
time: 112 us
  starting transfers between devices  51.4 us (46%)
  waiting for transfers between devices  46 us (41%)
  Pallas kernels  8.68 us (8%)
  local copies, waits for them, and re-layouts  2.42 us (2%)
  other arithmetic  1.69 us (2%)
  between operations  1.29 us (1%)
    ppermute x48, starting transfers between devices, swap(): got = [lax.ppermute(piece, axis, route) for piece in pieces]  51.4 us
    ppermute x48, waiting for transfers between devices, swap(): got = [lax.ppermute(piece, axis, route) for piece in pieces]  46 us
    pallas_call x8, Pallas kernels, call(): pl.pallas_call(kernel, out_shape=[jax.ShapeDtypeStruct(shape, kind) for s...  8.68 us
  transfers between devices with their start and end apart: 48, of which 25 were waited for; matrix products, arithmetic and copies ran while one was open for 2% of the time, Pallas kernels for 6%

profile of v4, /device:TPU:0, one launch (start us, length us, event | category | flops | bytes accessed | tf_op | source)
XLA Modules:
  0.0 111.6 jit_solution(4350784850092529586)
XLA Ops:
  2.0 5.1 %collective-permute-start.2 = (f32[16,128]{1,0:T(8,128)S(1)}, f32[16,128]{1,0:T(8,128)S(1)}, u32[]{:S(2)}, u32[]{:S(2)}) collective-permute-start(f32[16,128]{1,0:T(8,128)S(1)} %norm.1), channel_id=1, source_target_pairs={{0,3},{1,2},{2,1},{3,0},{4,7},{5,6},{6,5},{7,4},{8,11},{9,10},{10,... | collective-permute-start | bytes 24584 | tf_op jit(solution)/shard_map/ppermute | solution.py:173
  9.4 1.5 %collective-permute-start.5 = (f32[256,128]{1,0:T(8,128)S(1)}, f32[256,128]{1,0:T(8,128)S(1)}, u32[]{:S(2)}, u32[]{:S(2)}) collective-permute-start(f32[256,128]{1,0:T(8,128)S(1)} %get-tuple-element.111), channel_id=1, source_target_pairs={{0,1},{1,0},{2,3},{3,2},{4,5},{5,4},{6,7},{7,6},{8,9},{9,8},{10,11... | collective-permute-start | bytes 393224 | tf_op jit(solution)/shard_map/ppermute | solution.py:173
  13.0 4.0 %collective-permute-done.4 = f32[256,128]{1,0:T(8,128)S(1)} collective-permute-done((f32[256,128]{1,0:T(8,128)S(1)}, f32[256,128]{1,0:T(8,128)S(1)}, u32[]{:S(2)}, u32[]{:S(2)}) %collective-permute-start.4) | collective-permute-done | bytes 131104 | tf_op jit(solution)/shard_map/ppermute | solution.py:173
  19.3 2.3 %collective-permute-start.12 = (f32[256,128]{1,0:T(8,128)S(1)}, f32[256,128]{1,0:T(8,128)S(1)}, u32[]{:S(2)}, u32[]{:S(2)}) collective-permute-start(f32[256,128]{1,0:T(8,128)S(1)} %slice_select_fusion.12), channel_id=1, source_target_pairs={{0,2},{1,3},{2,0},{3,1},{4,6},{5,7},{6,4},{7,5},{8,10},{9,11},{10,... | collective-permute-start | bytes 393224 | tf_op jit(solution)/shard_map/ppermute | solution.py:173
  21.7 5.1 %collective-permute-done.6 = f32[256,128]{1,0:T(8,128)S(1)} collective-permute-done((f32[256,128]{1,0:T(8,128)S(1)}, f32[256,128]{1,0:T(8,128)S(1)}, u32[]{:S(2)}, u32[]{:S(2)}) %collective-permute-start.6) | collective-permute-done | bytes 131104 | tf_op jit(solution)/shard_map/ppermute | solution.py:173
  26.8 2.4 %collective-permute-start.10 = (f32[16,128]{1,0:T(8,128)S(1)}, f32[16,128]{1,0:T(8,128)S(1)}, u32[]{:S(2)}, u32[]{:S(2)}) collective-permute-start(f32[16,128]{1,0:T(8,128)S(1)} %add.138), channel_id=1, source_target_pairs={{0,24},{4,28},{8,16},{12,20},{16,8},{20,12},{24,0},{28,4},{1,25},{... | collective-permute-start | bytes 24584 | tf_op jit(solution)/shard_map/ppermute | solution.py:173
  31.4 1.4 %collective-permute-done.9 = f32[16,128]{1,0:T(8,128)S(1)} collective-permute-done((f32[16,128]{1,0:T(8,128)S(1)}, f32[16,128]{1,0:T(8,128)S(1)}, u32[]{:S(2)}, u32[]{:S(2)}) %collective-permute-start.9) | collective-permute-done | bytes 8224 | tf_op jit(solution)/shard_map/ppermute | solution.py:173
  33.4 1.7 %later.1 = (f32[2048,128]{1,0:T(8,128)S(1)}, bf16[2048,128]{1,0:T(8,128)(2,1)S(1)}, f32[16,128]{1,0:T(8,128)S(1)}) custom-call(bf16[2048,128]{1,0:T(8,128)(2,1)S(1)} %get-tuple-element.31.qt_ref, bf16[2048,128]{1,0:T(8,128)(2,1)S(1)} %get-tuple-element.32.ct_ref, f32[16,128]{1,0:T(8,128)S(1)} %get-tuple-element.33.part_ref, ...), custom_call_target="tpu_custom_call" | custom-call | bytes 3500000 | tf_op jit(solution)/shard_map/later/pallas_call | solution.py:156
  35.7 1.6 %collective-permute-start.24 = (f32[256,128]{1,0:T(8,128)S(1)}, f32[256,128]{1,0:T(8,128)S(1)}, u32[]{:S(2)}, u32[]{:S(2)}) collective-permute-start(f32[256,128]{1,0:T(8,128)S(1)} %get-tuple-element.102), channel_id=1, source_target_pairs={{0,1},{1,0},{2,3},{3,2},{4,5},{5,4},{6,7},{7,6},{8,9},{9,8},{10,11... | collective-permute-start | bytes 393224 | tf_op jit(solution)/shard_map/ppermute | solution.py:173
  38.6 1.6 %collective-permute-start.27 = (f32[256,128]{1,0:T(8,128)S(1)}, f32[256,128]{1,0:T(8,128)S(1)}, u32[]{:S(2)}, u32[]{:S(2)}) collective-permute-start(f32[256,128]{1,0:T(8,128)S(1)} %get-tuple-element.104), channel_id=1, source_target_pairs={{0,1},{1,0},{2,3},{3,2},{4,5},{5,4},{6,7},{7,6},{8,9},{9,8},{10,11... | collective-permute-start | bytes 393224 | tf_op jit(solution)/shard_map/ppermute | solution.py:173
  40.4 1.6 %collective-permute-done.24 = f32[256,128]{1,0:T(8,128)S(1)} collective-permute-done((f32[256,128]{1,0:T(8,128)S(1)}, f32[256,128]{1,0:T(8,128)S(1)}, u32[]{:S(2)}, u32[]{:S(2)}) %collective-permute-start.24) | collective-permute-done | bytes 131104 | tf_op jit(solution)/shard_map/ppermute | solution.py:173
  42.0 3.2 %collective-permute-done.27 = f32[256,128]{1,0:T(8,128)S(1)} collective-permute-done((f32[256,128]{1,0:T(8,128)S(1)}, f32[256,128]{1,0:T(8,128)S(1)}, u32[]{:S(2)}, u32[]{:S(2)}) %collective-permute-start.27) | collective-permute-done | bytes 131104 | tf_op jit(solution)/shard_map/ppermute | solution.py:173
  45.5 2.6 %collective-permute-start.29 = (f32[256,128]{1,0:T(8,128)S(1)}, f32[256,128]{1,0:T(8,128)S(1)}, u32[]{:S(2)}, u32[]{:S(2)}) collective-permute-start(f32[256,128]{1,0:T(8,128)S(1)} %slice_select_fusion.8), channel_id=1, source_target_pairs={{0,2},{1,3},{2,0},{3,1},{4,6},{5,7},{6,4},{7,5},{8,10},{9,11},{10,... | collective-permute-start | bytes 393224 | tf_op jit(solution)/shard_map/ppermute | solution.py:173
  48.6 3.3 %collective-permute-start.16 = (f32[256,128]{1,0:T(8,128)S(1)}, f32[256,128]{1,0:T(8,128)S(1)}, u32[]{:S(2)}, u32[]{:S(2)}) collective-permute-start(f32[256,128]{1,0:T(8,128)S(1)} %get-tuple-element.73), channel_id=1, source_target_pairs={{0,24},{4,28},{8,16},{12,20},{16,8},{20,12},{24,0},{28,4},{1,25},{... | collective-permute-start | bytes 393224 | tf_op jit(solution)/shard_map/ppermute | solution.py:173
  52.6 1.9 %collective-permute-done.29 = f32[256,128]{1,0:T(8,128)S(1)} collective-permute-done((f32[256,128]{1,0:T(8,128)S(1)}, f32[256,128]{1,0:T(8,128)S(1)}, u32[]{:S(2)}, u32[]{:S(2)}) %collective-permute-start.29) | collective-permute-done | bytes 131104 | tf_op jit(solution)/shard_map/ppermute | solution.py:173
  57.6 2.9 %collective-permute-start.33 = (f32[256,128]{1,0:T(8,128)S(1)}, f32[256,128]{1,0:T(8,128)S(1)}, u32[]{:S(2)}, u32[]{:S(2)}) collective-permute-start(f32[256,128]{1,0:T(8,128)S(1)} %get-tuple-element.58), channel_id=1, source_target_pairs={{0,24},{4,28},{8,16},{12,20},{16,8},{20,12},{24,0},{28,4},{1,25},{... | collective-permute-start | bytes 393224 | tf_op jit(solution)/shard_map/ppermute | solution.py:173
  62.4 2.2 %collective-permute-done.33 = f32[256,128]{1,0:T(8,128)S(1)} collective-permute-done((f32[256,128]{1,0:T(8,128)S(1)}, f32[256,128]{1,0:T(8,128)S(1)}, u32[]{:S(2)}, u32[]{:S(2)}) %collective-permute-start.33) | collective-permute-done | bytes 131104 | tf_op jit(solution)/shard_map/ppermute | solution.py:173
  64.7 2.6 %collective-permute-done.32 = f32[256,128]{1,0:T(8,128)S(1)} collective-permute-done((f32[256,128]{1,0:T(8,128)S(1)}, f32[256,128]{1,0:T(8,128)S(1)}, u32[]{:S(2)}, u32[]{:S(2)}) %collective-permute-start.32) | collective-permute-done | bytes 131104 | tf_op jit(solution)/shard_map/ppermute | solution.py:173
  67.5 2.5 %collective-permute-done.18 = f32[256,128]{1,0:T(8,128)S(1)} collective-permute-done((f32[256,128]{1,0:T(8,128)S(1)}, f32[256,128]{1,0:T(8,128)S(1)}, u32[]{:S(2)}, u32[]{:S(2)}) %collective-permute-start.18) | collective-permute-done | bytes 131104 | tf_op jit(solution)/shard_map/ppermute | solution.py:173
  70.3 2.7 %collective-permute-start.20 = (f32[256,128]{1,0:T(8,128)S(1)}, f32[256,128]{1,0:T(8,128)S(1)}, u32[]{:S(2)}, u32[]{:S(2)}) collective-permute-start(f32[256,128]{1,0:T(8,128)S(1)} %get-tuple-element.105), channel_id=1, source_target_pairs={{0,1},{1,0},{2,3},{3,2},{4,5},{5,4},{6,7},{7,6},{8,9},{9,8},{10,11... | collective-permute-start | bytes 393224 | tf_op jit(solution)/shard_map/ppermute | solution.py:173
  73.1 2.3 %collective-permute-start.35 = (f32[256,128]{1,0:T(8,128)S(1)}, f32[256,128]{1,0:T(8,128)S(1)}, u32[]{:S(2)}, u32[]{:S(2)}) collective-permute-start(f32[256,128]{1,0:T(8,128)S(1)} %add_select_fusion.11), channel_id=1, source_target_pairs={{0,2},{1,3},{2,0},{3,1},{4,6},{5,7},{6,4},{7,5},{8,10},{9,11},{10,... | collective-permute-start | bytes 393224 | tf_op jit(solution)/shard_map/ppermute | solution.py:173
  75.4 3.6 %collective-permute-done.21 = f32[256,128]{1,0:T(8,128)S(1)} collective-permute-done((f32[256,128]{1,0:T(8,128)S(1)}, f32[256,128]{1,0:T(8,128)S(1)}, u32[]{:S(2)}, u32[]{:S(2)}) %collective-permute-start.21) | collective-permute-done | bytes 131104 | tf_op jit(solution)/shard_map/ppermute | solution.py:173
  79.2 2.0 %collective-permute-start.22 = (f32[256,128]{1,0:T(8,128)S(1)}, f32[256,128]{1,0:T(8,128)S(1)}, u32[]{:S(2)}, u32[]{:S(2)}) collective-permute-start(f32[256,128]{1,0:T(8,128)S(1)} %get-tuple-element.108), channel_id=1, source_target_pairs={{0,1},{1,0},{2,3},{3,2},{4,5},{5,4},{6,7},{7,6},{8,9},{9,8},{10,11... | collective-permute-start | bytes 393224 | tf_op jit(solution)/shard_map/ppermute | solution.py:173
  81.2 4.5 %collective-permute-done.19 = f32[256,128]{1,0:T(8,128)S(1)} collective-permute-done((f32[256,128]{1,0:T(8,128)S(1)}, f32[256,128]{1,0:T(8,128)S(1)}, u32[]{:S(2)}, u32[]{:S(2)}) %collective-permute-start.19) | collective-permute-done | bytes 131104 | tf_op jit(solution)/shard_map/ppermute | solution.py:173
  86.1 2.3 %collective-permute-start.45 = (f32[256,128]{1,0:T(8,128)S(1)}, f32[256,128]{1,0:T(8,128)S(1)}, u32[]{:S(2)}, u32[]{:S(2)}) collective-permute-start(f32[256,128]{1,0:T(8,128)S(1)} %get-tuple-element.97), channel_id=1, source_target_pairs={{0,1},{1,0},{2,3},{3,2},{4,5},{5,4},{6,7},{7,6},{8,9},{9,8},{10,11... | collective-permute-start | bytes 393224 | tf_op jit(solution)/shard_map/ppermute | solution.py:173
  88.5 4.9 %collective-permute-done.22 = f32[256,128]{1,0:T(8,128)S(1)} collective-permute-done((f32[256,128]{1,0:T(8,128)S(1)}, f32[256,128]{1,0:T(8,128)S(1)}, u32[]{:S(2)}, u32[]{:S(2)}) %collective-permute-start.22) | collective-permute-done | bytes 131104 | tf_op jit(solution)/shard_map/ppermute | solution.py:173
  94.2 2.5 %collective-permute-start.39 = (f32[16,128]{1,0:T(8,128)S(1)}, f32[16,128]{1,0:T(8,128)S(1)}, u32[]{:S(2)}, u32[]{:S(2)}) collective-permute-start(f32[16,128]{1,0:T(8,128)S(1)} %get-tuple-element.49), channel_id=1, source_target_pairs={{0,3},{1,2},{2,1},{3,0},{4,7},{5,6},{6,5},{7,4},{8,11},{9,10},{10,... | collective-permute-start | bytes 24584 | tf_op jit(solution)/shard_map/ppermute | solution.py:173
  96.7 1.9 %collective-permute-start.37 = (f32[16,128]{1,0:T(8,128)S(1)}, f32[16,128]{1,0:T(8,128)S(1)}, u32[]{:S(2)}, u32[]{:S(2)}) collective-permute-start(f32[16,128]{1,0:T(8,128)S(1)} %get-tuple-element.49), channel_id=1, source_target_pairs={{0,1},{1,0},{2,3},{3,2},{4,5},{5,4},{6,7},{7,6},{8,9},{9,8},{10,11... | collective-permute-start | bytes 24584 | tf_op jit(solution)/shard_map/ppermute | solution.py:173
  99.7 1.6 %collective-permute-done.38 = f32[16,128]{1,0:T(8,128)S(1)} collective-permute-done((f32[16,128]{1,0:T(8,128)S(1)}, f32[16,128]{1,0:T(8,128)S(1)}, u32[]{:S(2)}, u32[]{:S(2)}) %collective-permute-start.38) | collective-permute-done | bytes 8224 | tf_op jit(solution)/shard_map/ppermute | solution.py:173
  103.0 2.4 %collective-permute-start.43 = (f32[16,128]{1,0:T(8,128)S(1)}, f32[16,128]{1,0:T(8,128)S(1)}, u32[]{:S(2)}, u32[]{:S(2)}) collective-permute-start(f32[16,128]{1,0:T(8,128)S(1)} %add.170), channel_id=1, source_target_pairs={{0,24},{4,28},{8,16},{12,20},{16,8},{20,12},{24,0},{28,4},{1,25},{... | collective-permute-start | bytes 24584 | tf_op jit(solution)/shard_map/ppermute | solution.py:173
  106.5 2.3 %query.1 = (bf16[128,2048]{1,0:T(8,128)(2,1)}, bf16[128,2048]{1,0:T(8,128)(2,1)}, f32[128,2048]{1,0:T(8,128)S(1)}) custom-call(bf16[128,2048]{1,0:T(8,128)(2,1)S(1)} %copy-done.4, bf16[128,2048]{1,0:T(8,128)(2,1)S(1)} %get-tuple-element.28.qf_ref, bf16[128,2048]{1,0:T(8,128)(2,1)S(1)} %get-tuple-element.29.kf_ref, ...), custom_call_target="tpu_custom_call" | custom-call | bytes 3500000 | tf_op jit(solution)/shard_map/query/pallas_call | solution.py:156
  109.9 1.7 %key.1 = (bf16[128,2048]{1,0:T(8,128)(2,1)}, bf16[128,2048]{1,0:T(8,128)(2,1)}) custom-call(bf16[128,2048]{1,0:T(8,128)(2,1)S(1)} %copy-done.1, bf16[128,2048]{1,0:T(8,128)(2,1)S(1)} %get-tuple-element.29.kf_ref, bf16[128,2048]{1,0:T(8,128)(2,1)S(1)} %copy-done.3, f32[128,2048]{1,0:T(8,128)S(1)} %get-tuple-element.47.ki_ref, ...), custom_call_target="tpu_custom_call" | custom-call | bytes 3500000 | tf_op jit(solution)/shard_map/key/pallas_call | solution.py:156
  (149 shorter events, 26.1 us)
Async XLA Ops:
  2.0 9.5 %collective-permute-start.2 = (f32[16,128]{1,0:T(8,128)S(1)}, f32[16,128]{1,0:T(8,128)S(1)}, u32[]{:S(2)}, u32[]{:S(2)}) collective-permute-start(f32[16,128]{1,0:T(8,128)S(1)} %norm.1), channel_id=1, source_target_pairs={{0,3},{1,2},{2,1},{3,0},{4,7},{5,6},{6,5},{7,4},{8,11},{9,10},{10,... | collective-permute-start | bytes 24584 | tf_op jit(solution)/shard_map/ppermute | solution.py:173
  9.4 7.7 %collective-permute-start.5 = (f32[256,128]{1,0:T(8,128)S(1)}, f32[256,128]{1,0:T(8,128)S(1)}, u32[]{:S(2)}, u32[]{:S(2)}) collective-permute-start(f32[256,128]{1,0:T(8,128)S(1)} %get-tuple-element.111), channel_id=1, source_target_pairs={{0,1},{1,0},{2,3},{3,2},{4,5},{5,4},{6,7},{7,6},{8,9},{9,8},{10,11... | collective-permute-start | bytes 393224 | tf_op jit(solution)/shard_map/ppermute | solution.py:173
  10.9 6.2 %collective-permute-start.4 = (f32[256,128]{1,0:T(8,128)S(1)}, f32[256,128]{1,0:T(8,128)S(1)}, u32[]{:S(2)}, u32[]{:S(2)}) collective-permute-start(f32[256,128]{1,0:T(8,128)S(1)} %get-tuple-element.112), channel_id=1, source_target_pairs={{0,1},{1,0},{2,3},{3,2},{4,5},{5,4},{6,7},{7,6},{8,9},{9,8},{10,11... | collective-permute-start | bytes 393224 | tf_op jit(solution)/shard_map/ppermute | solution.py:173
  17.2 9.5 %collective-permute-start.7 = (f32[256,128]{1,0:T(8,128)S(1)}, f32[256,128]{1,0:T(8,128)S(1)}, u32[]{:S(2)}, u32[]{:S(2)}) collective-permute-start(f32[256,128]{1,0:T(8,128)S(1)} %get-tuple-element.109), channel_id=1, source_target_pairs={{0,1},{1,0},{2,3},{3,2},{4,5},{5,4},{6,7},{7,6},{8,9},{9,8},{10,11... | collective-permute-start | bytes 393224 | tf_op jit(solution)/shard_map/ppermute | solution.py:173
  18.6 8.1 %collective-permute-start.6 = (f32[256,128]{1,0:T(8,128)S(1)}, f32[256,128]{1,0:T(8,128)S(1)}, u32[]{:S(2)}, u32[]{:S(2)}) collective-permute-start(f32[256,128]{1,0:T(8,128)S(1)} %get-tuple-element.110), channel_id=1, source_target_pairs={{0,1},{1,0},{2,3},{3,2},{4,5},{5,4},{6,7},{7,6},{8,9},{9,8},{10,11... | collective-permute-start | bytes 393224 | tf_op jit(solution)/shard_map/ppermute | solution.py:173
  19.3 19.3 %collective-permute-start.12 = (f32[256,128]{1,0:T(8,128)S(1)}, f32[256,128]{1,0:T(8,128)S(1)}, u32[]{:S(2)}, u32[]{:S(2)}) collective-permute-start(f32[256,128]{1,0:T(8,128)S(1)} %slice_select_fusion.12), channel_id=1, source_target_pairs={{0,2},{1,3},{2,0},{3,1},{4,6},{5,7},{6,4},{7,5},{8,10},{9,11},{10,... | collective-permute-start | bytes 393224 | tf_op jit(solution)/shard_map/ppermute | solution.py:173
  30.4 9.9 %collective-permute-start.11 = (f32[256,128]{1,0:T(8,128)S(1)}, f32[256,128]{1,0:T(8,128)S(1)}, u32[]{:S(2)}, u32[]{:S(2)}) collective-permute-start(f32[256,128]{1,0:T(8,128)S(1)} %slice_select_fusion.14), channel_id=1, source_target_pairs={{0,2},{1,3},{2,0},{3,1},{4,6},{5,7},{6,4},{7,5},{8,10},{9,11},{10,... | collective-permute-start | bytes 393224 | tf_op jit(solution)/shard_map/ppermute | solution.py:173
  35.1 10.1 %collective-permute-start.25 = (f32[256,128]{1,0:T(8,128)S(1)}, f32[256,128]{1,0:T(8,128)S(1)}, u32[]{:S(2)}, u32[]{:S(2)}) collective-permute-start(f32[256,128]{1,0:T(8,128)S(1)} %get-tuple-element.101), channel_id=1, source_target_pairs={{0,1},{1,0},{2,3},{3,2},{4,5},{5,4},{6,7},{7,6},{8,9},{9,8},{10,11... | collective-permute-start | bytes 393224 | tf_op jit(solution)/shard_map/ppermute | solution.py:173
  35.7 6.3 %collective-permute-start.24 = (f32[256,128]{1,0:T(8,128)S(1)}, f32[256,128]{1,0:T(8,128)S(1)}, u32[]{:S(2)}, u32[]{:S(2)}) collective-permute-start(f32[256,128]{1,0:T(8,128)S(1)} %get-tuple-element.102), channel_id=1, source_target_pairs={{0,1},{1,0},{2,3},{3,2},{4,5},{5,4},{6,7},{7,6},{8,9},{9,8},{10,11... | collective-permute-start | bytes 393224 | tf_op jit(solution)/shard_map/ppermute | solution.py:173
  37.3 8.1 %collective-permute-start.28 = (f32[256,128]{1,0:T(8,128)S(1)}, f32[256,128]{1,0:T(8,128)S(1)}, u32[]{:S(2)}, u32[]{:S(2)}) collective-permute-start(f32[256,128]{1,0:T(8,128)S(1)} %get-tuple-element.103), channel_id=1, source_target_pairs={{0,1},{1,0},{2,3},{3,2},{4,5},{5,4},{6,7},{7,6},{8,9},{9,8},{10,11... | collective-permute-start | bytes 393224 | tf_op jit(solution)/shard_map/ppermute | solution.py:173
  38.6 6.6 %collective-permute-start.27 = (f32[256,128]{1,0:T(8,128)S(1)}, f32[256,128]{1,0:T(8,128)S(1)}, u32[]{:S(2)}, u32[]{:S(2)}) collective-permute-start(f32[256,128]{1,0:T(8,128)S(1)} %get-tuple-element.104), channel_id=1, source_target_pairs={{0,1},{1,0},{2,3},{3,2},{4,5},{5,4},{6,7},{7,6},{8,9},{9,8},{10,11... | collective-permute-start | bytes 393224 | tf_op jit(solution)/shard_map/ppermute | solution.py:173
  40.3 8.2 %collective-permute-start.13 = (f32[256,128]{1,0:T(8,128)S(1)}, f32[256,128]{1,0:T(8,128)S(1)}, u32[]{:S(2)}, u32[]{:S(2)}) collective-permute-start(f32[256,128]{1,0:T(8,128)S(1)} %get-tuple-element.75), channel_id=1, source_target_pairs={{0,4},{4,0},{8,12},{12,8},{16,20},{20,16},{24,28},{28,24},{1,5},{5... | collective-permute-start | bytes 393224 | tf_op jit(solution)/shard_map/ppermute | solution.py:173
  45.5 9.0 %collective-permute-start.29 = (f32[256,128]{1,0:T(8,128)S(1)}, f32[256,128]{1,0:T(8,128)S(1)}, u32[]{:S(2)}, u32[]{:S(2)}) collective-permute-start(f32[256,128]{1,0:T(8,128)S(1)} %slice_select_fusion.8), channel_id=1, source_target_pairs={{0,2},{1,3},{2,0},{3,1},{4,6},{5,7},{6,4},{7,5},{8,10},{9,11},{10,... | collective-permute-start | bytes 393224 | tf_op jit(solution)/shard_map/ppermute | solution.py:173
  48.1 7.8 %collective-permute-start.26 = (f32[256,128]{1,0:T(8,128)S(1)}, f32[256,128]{1,0:T(8,128)S(1)}, u32[]{:S(2)}, u32[]{:S(2)}) collective-permute-start(f32[256,128]{1,0:T(8,128)S(1)} %slice_select_fusion.10), channel_id=1, source_target_pairs={{0,2},{1,3},{2,0},{3,1},{4,6},{5,7},{6,4},{7,5},{8,10},{9,11},{10,... | collective-permute-start | bytes 393224 | tf_op jit(solution)/shard_map/ppermute | solution.py:173
  48.6 7.4 %collective-permute-start.16 = (f32[256,128]{1,0:T(8,128)S(1)}, f32[256,128]{1,0:T(8,128)S(1)}, u32[]{:S(2)}, u32[]{:S(2)}) collective-permute-start(f32[256,128]{1,0:T(8,128)S(1)} %get-tuple-element.73), channel_id=1, source_target_pairs={{0,24},{4,28},{8,16},{12,20},{16,8},{20,12},{24,0},{28,4},{1,25},{... | collective-permute-start | bytes 393224 | tf_op jit(solution)/shard_map/ppermute | solution.py:173
  57.6 7.1 %collective-permute-start.33 = (f32[256,128]{1,0:T(8,128)S(1)}, f32[256,128]{1,0:T(8,128)S(1)}, u32[]{:S(2)}, u32[]{:S(2)}) collective-permute-start(f32[256,128]{1,0:T(8,128)S(1)} %get-tuple-element.58), channel_id=1, source_target_pairs={{0,24},{4,28},{8,16},{12,20},{16,8},{20,12},{24,0},{28,4},{1,25},{... | collective-permute-start | bytes 393224 | tf_op jit(solution)/shard_map/ppermute | solution.py:173
  60.4 6.8 %collective-permute-start.32 = (f32[256,128]{1,0:T(8,128)S(1)}, f32[256,128]{1,0:T(8,128)S(1)}, u32[]{:S(2)}, u32[]{:S(2)}) collective-permute-start(f32[256,128]{1,0:T(8,128)S(1)} %get-tuple-element.58), channel_id=1, source_target_pairs={{0,16},{4,20},{8,24},{12,28},{16,0},{20,4},{24,8},{28,12},{1,17},{... | collective-permute-start | bytes 393224 | tf_op jit(solution)/shard_map/ppermute | solution.py:173
  60.9 6.4 %collective-permute-start.31 = (f32[256,128]{1,0:T(8,128)S(1)}, f32[256,128]{1,0:T(8,128)S(1)}, u32[]{:S(2)}, u32[]{:S(2)}) collective-permute-start(f32[256,128]{1,0:T(8,128)S(1)} %get-tuple-element.58), channel_id=1, source_target_pairs={{0,8},{4,12},{8,0},{12,4},{16,24},{20,28},{24,16},{28,20},{1,9},{5... | collective-permute-start | bytes 393224 | tf_op jit(solution)/shard_map/ppermute | solution.py:173
  61.2 8.8 %collective-permute-start.18 = (f32[256,128]{1,0:T(8,128)S(1)}, f32[256,128]{1,0:T(8,128)S(1)}, u32[]{:S(2)}, u32[]{:S(2)}) collective-permute-start(f32[256,128]{1,0:T(8,128)S(1)} %add_select_fusion.17), channel_id=1, source_target_pairs={{0,2},{1,3},{2,0},{3,1},{4,6},{5,7},{6,4},{7,5},{8,10},{9,11},{10,... | collective-permute-start | bytes 393224 | tf_op jit(solution)/shard_map/ppermute | solution.py:173
  67.4 5.6 %collective-permute-start.34 = (f32[256,128]{1,0:T(8,128)S(1)}, f32[256,128]{1,0:T(8,128)S(1)}, u32[]{:S(2)}, u32[]{:S(2)}) collective-permute-start(f32[256,128]{1,0:T(8,128)S(1)} %get-tuple-element.56), channel_id=1, source_target_pairs={{0,4},{4,0},{8,12},{12,8},{16,20},{20,16},{24,28},{28,24},{1,5},{5... | collective-permute-start | bytes 393224 | tf_op jit(solution)/shard_map/ppermute | solution.py:173
  70.1 8.9 %collective-permute-start.21 = (f32[256,128]{1,0:T(8,128)S(1)}, f32[256,128]{1,0:T(8,128)S(1)}, u32[]{:S(2)}, u32[]{:S(2)}) collective-permute-start(f32[256,128]{1,0:T(8,128)S(1)} %get-tuple-element.96), channel_id=1, source_target_pairs={{0,2},{1,3},{2,0},{3,1},{4,6},{5,7},{6,4},{7,5},{8,10},{9,11},{10,... | collective-permute-start | bytes 393224 | tf_op jit(solution)/shard_map/ppermute | solution.py:173
  70.3 15.4 %collective-permute-start.20 = (f32[256,128]{1,0:T(8,128)S(1)}, f32[256,128]{1,0:T(8,128)S(1)}, u32[]{:S(2)}, u32[]{:S(2)}) collective-permute-start(f32[256,128]{1,0:T(8,128)S(1)} %get-tuple-element.105), channel_id=1, source_target_pairs={{0,1},{1,0},{2,3},{3,2},{4,5},{5,4},{6,7},{7,6},{8,9},{9,8},{10,11... | collective-permute-start | bytes 393224 | tf_op jit(solution)/shard_map/ppermute | solution.py:173
  73.0 12.7 %collective-permute-start.19 = (f32[256,128]{1,0:T(8,128)S(1)}, f32[256,128]{1,0:T(8,128)S(1)}, u32[]{:S(2)}, u32[]{:S(2)}) collective-permute-start(f32[256,128]{1,0:T(8,128)S(1)} %get-tuple-element.106), channel_id=1, source_target_pairs={{0,1},{1,0},{2,3},{3,2},{4,5},{5,4},{6,7},{7,6},{8,9},{9,8},{10,11... | collective-permute-start | bytes 393224 | tf_op jit(solution)/shard_map/ppermute | solution.py:173
  73.1 12.6 %collective-permute-start.35 = (f32[256,128]{1,0:T(8,128)S(1)}, f32[256,128]{1,0:T(8,128)S(1)}, u32[]{:S(2)}, u32[]{:S(2)}) collective-permute-start(f32[256,128]{1,0:T(8,128)S(1)} %add_select_fusion.11), channel_id=1, source_target_pairs={{0,2},{1,3},{2,0},{3,1},{4,6},{5,7},{6,4},{7,5},{8,10},{9,11},{10,... | collective-permute-start | bytes 393224 | tf_op jit(solution)/shard_map/ppermute | solution.py:173
  79.1 14.3 %collective-permute-start.23 = (f32[256,128]{1,0:T(8,128)S(1)}, f32[256,128]{1,0:T(8,128)S(1)}, u32[]{:S(2)}, u32[]{:S(2)}) collective-permute-start(f32[256,128]{1,0:T(8,128)S(1)} %get-tuple-element.107), channel_id=1, source_target_pairs={{0,1},{1,0},{2,3},{3,2},{4,5},{5,4},{6,7},{7,6},{8,9},{9,8},{10,11... | collective-permute-start | bytes 393224 | tf_op jit(solution)/shard_map/ppermute | solution.py:173
  79.2 14.2 %collective-permute-start.22 = (f32[256,128]{1,0:T(8,128)S(1)}, f32[256,128]{1,0:T(8,128)S(1)}, u32[]{:S(2)}, u32[]{:S(2)}) collective-permute-start(f32[256,128]{1,0:T(8,128)S(1)} %get-tuple-element.108), channel_id=1, source_target_pairs={{0,1},{1,0},{2,3},{3,2},{4,5},{5,4},{6,7},{7,6},{8,9},{9,8},{10,11... | collective-permute-start | bytes 393224 | tf_op jit(solution)/shard_map/ppermute | solution.py:173
  85.9 10.9 %collective-permute-start.36 = (f32[256,128]{1,0:T(8,128)S(1)}, f32[256,128]{1,0:T(8,128)S(1)}, u32[]{:S(2)}, u32[]{:S(2)}) collective-permute-start(f32[256,128]{1,0:T(8,128)S(1)} %get-tuple-element.95), channel_id=1, source_target_pairs={{0,2},{1,3},{2,0},{3,1},{4,6},{5,7},{6,4},{7,5},{8,10},{9,11},{10,... | collective-permute-start | bytes 393224 | tf_op jit(solution)/shard_map/ppermute | solution.py:173
  86.1 15.7 %collective-permute-start.45 = (f32[256,128]{1,0:T(8,128)S(1)}, f32[256,128]{1,0:T(8,128)S(1)}, u32[]{:S(2)}, u32[]{:S(2)}) collective-permute-start(f32[256,128]{1,0:T(8,128)S(1)} %get-tuple-element.97), channel_id=1, source_target_pairs={{0,1},{1,0},{2,3},{3,2},{4,5},{5,4},{6,7},{7,6},{8,9},{9,8},{10,11... | collective-permute-start | bytes 393224 | tf_op jit(solution)/shard_map/ppermute | solution.py:173
  88.4 13.4 %collective-permute-start.44 = (f32[256,128]{1,0:T(8,128)S(1)}, f32[256,128]{1,0:T(8,128)S(1)}, u32[]{:S(2)}, u32[]{:S(2)}) collective-permute-start(f32[256,128]{1,0:T(8,128)S(1)} %get-tuple-element.98), channel_id=1, source_target_pairs={{0,1},{1,0},{2,3},{3,2},{4,5},{5,4},{6,7},{7,6},{8,9},{9,8},{10,11... | collective-permute-start | bytes 393224 | tf_op jit(solution)/shard_map/ppermute | solution.py:173
  99.7 10.0 %collective-permute-start.47 = (f32[256,128]{1,0:T(8,128)S(1)}, f32[256,128]{1,0:T(8,128)S(1)}, u32[]{:S(2)}, u32[]{:S(2)}) collective-permute-start(f32[256,128]{1,0:T(8,128)S(1)} %get-tuple-element.99), channel_id=1, source_target_pairs={{0,1},{1,0},{2,3},{3,2},{4,5},{5,4},{6,7},{7,6},{8,9},{9,8},{10,11... | collective-permute-start | bytes 393224 | tf_op jit(solution)/shard_map/ppermute | solution.py:173
  101.4 8.3 %collective-permute-start.46 = (f32[256,128]{1,0:T(8,128)S(1)}, f32[256,128]{1,0:T(8,128)S(1)}, u32[]{:S(2)}, u32[]{:S(2)}) collective-permute-start(f32[256,128]{1,0:T(8,128)S(1)} %get-tuple-element.100), channel_id=1, source_target_pairs={{0,1},{1,0},{2,3},{3,2},{4,5},{5,4},{6,7},{7,6},{8,9},{9,8},{10,11... | collective-permute-start | bytes 393224 | tf_op jit(solution)/shard_map/ppermute | solution.py:173
  103.0 5.8 %collective-permute-start.43 = (f32[16,128]{1,0:T(8,128)S(1)}, f32[16,128]{1,0:T(8,128)S(1)}, u32[]{:S(2)}, u32[]{:S(2)}) collective-permute-start(f32[16,128]{1,0:T(8,128)S(1)} %add.170), channel_id=1, source_target_pairs={{0,24},{4,28},{8,16},{12,20},{16,8},{20,12},{24,0},{28,4},{1,25},{... | collective-permute-start | bytes 24584 | tf_op jit(solution)/shard_map/ppermute | solution.py:173
  (22 other events, 77.5 us)

commit v5 on v4

--- a/solution.py
+++ b/solution.py
@@ -150,6 +150,7 @@
 LATE = ('S0', 'L0', 'S0', 'L0', 'S0', 'L0', 'S0', 'L0', 'S0', 'L0', 'S0', 'L0')
 LAST = ('M', 'M', 'M', 'L0')
 VMEM = 24
+STEPS = 2
 
 
 def call(name, kernel, outs, *args, **more):
@@ -333,9 +334,14 @@
         "query", query_kernel, [(flat, BF16), (flat, BF16), (flat, F32)],
         queries, q_feat, k_feat, plain, ratio, tie(grad_den, last(chains, QUERY_GATE)), normal, near_scores, state,
     )
+    across = pl.BlockSpec((tokens, width // STEPS), lambda step: (0, step))
+    down = lambda step: (step, 0)
     key_grad, value_grad = call(
         "key", key_kernel, [(flat, BF16), (flat, BF16)],
         keys, k_feat, values, near_keys, near_values, later_norm, later,
+        grid=(STEPS,),
+        in_specs=[across] * 5 + [pl.BlockSpec((heads // STEPS, HD), down), pl.BlockSpec((width // STEPS, HD), down)],
+        out_specs=[across] * 2,
     )
     return attended, query_grad, key_grad, value_grad
 

time: 112 us -> 112 us (level)
  no operation moved by 1% of the time
where the time goes in v5:
time: 112 us
  starting transfers between devices  51.4 us (46%)
  waiting for transfers between devices  46 us (41%)
  Pallas kernels  8.91 us (8%)
  local copies, waits for them, and re-layouts  2.42 us (2%)
  other arithmetic  1.69 us (2%)
  between operations  1.29 us (1%)
    ppermute x48, starting transfers between devices, swap(): got = [lax.ppermute(piece, axis, route) for piece in pieces]  51.4 us
    ppermute x48, waiting for transfers between devices, swap(): got = [lax.ppermute(piece, axis, route) for piece in pieces]  46 us
    pallas_call x8, Pallas kernels, call(): pl.pallas_call(kernel, out_shape=[jax.ShapeDtypeStruct(shape, kind) for s...  8.91 us
  transfers between devices with their start and end apart: 48, of which 25 were waited for; matrix products, arithmetic and copies ran while one was open for 2% of the time, Pallas kernels for 6%

profile of v5, /device:TPU:0, one launch (start us, length us, event | category | flops | bytes accessed | tf_op | source)
XLA Modules:
  0.0 111.8 jit_solution(15737009502781445034)
XLA Ops:
  2.0 5.1 %collective-permute-start.2 = (f32[16,128]{1,0:T(8,128)S(1)}, f32[16,128]{1,0:T(8,128)S(1)}, u32[]{:S(2)}, u32[]{:S(2)}) collective-permute-start(f32[16,128]{1,0:T(8,128)S(1)} %norm.1), channel_id=1, source_target_pairs={{0,3},{1,2},{2,1},{3,0},{4,7},{5,6},{6,5},{7,4},{8,11},{9,10},{10,... | collective-permute-start | bytes 24584 | tf_op jit(solution)/shard_map/ppermute | solution.py:174
  9.4 1.5 %collective-permute-start.5 = (f32[256,128]{1,0:T(8,128)S(1)}, f32[256,128]{1,0:T(8,128)S(1)}, u32[]{:S(2)}, u32[]{:S(2)}) collective-permute-start(f32[256,128]{1,0:T(8,128)S(1)} %get-tuple-element.111), channel_id=1, source_target_pairs={{0,1},{1,0},{2,3},{3,2},{4,5},{5,4},{6,7},{7,6},{8,9},{9,8},{10,11... | collective-permute-start | bytes 393224 | tf_op jit(solution)/shard_map/ppermute | solution.py:174
  13.0 4.0 %collective-permute-done.4 = f32[256,128]{1,0:T(8,128)S(1)} collective-permute-done((f32[256,128]{1,0:T(8,128)S(1)}, f32[256,128]{1,0:T(8,128)S(1)}, u32[]{:S(2)}, u32[]{:S(2)}) %collective-permute-start.4) | collective-permute-done | bytes 131104 | tf_op jit(solution)/shard_map/ppermute | solution.py:174
  19.3 2.3 %collective-permute-start.12 = (f32[256,128]{1,0:T(8,128)S(1)}, f32[256,128]{1,0:T(8,128)S(1)}, u32[]{:S(2)}, u32[]{:S(2)}) collective-permute-start(f32[256,128]{1,0:T(8,128)S(1)} %slice_select_fusion.12), channel_id=1, source_target_pairs={{0,2},{1,3},{2,0},{3,1},{4,6},{5,7},{6,4},{7,5},{8,10},{9,11},{10,... | collective-permute-start | bytes 393224 | tf_op jit(solution)/shard_map/ppermute | solution.py:174
  21.7 5.1 %collective-permute-done.6 = f32[256,128]{1,0:T(8,128)S(1)} collective-permute-done((f32[256,128]{1,0:T(8,128)S(1)}, f32[256,128]{1,0:T(8,128)S(1)}, u32[]{:S(2)}, u32[]{:S(2)}) %collective-permute-start.6) | collective-permute-done | bytes 131104 | tf_op jit(solution)/shard_map/ppermute | solution.py:174
  26.8 2.4 %collective-permute-start.10 = (f32[16,128]{1,0:T(8,128)S(1)}, f32[16,128]{1,0:T(8,128)S(1)}, u32[]{:S(2)}, u32[]{:S(2)}) collective-permute-start(f32[16,128]{1,0:T(8,128)S(1)} %add.138), channel_id=1, source_target_pairs={{0,24},{4,28},{8,16},{12,20},{16,8},{20,12},{24,0},{28,4},{1,25},{... | collective-permute-start | bytes 24584 | tf_op jit(solution)/shard_map/ppermute | solution.py:174
  31.4 1.4 %collective-permute-done.9 = f32[16,128]{1,0:T(8,128)S(1)} collective-permute-done((f32[16,128]{1,0:T(8,128)S(1)}, f32[16,128]{1,0:T(8,128)S(1)}, u32[]{:S(2)}, u32[]{:S(2)}) %collective-permute-start.9) | collective-permute-done | bytes 8224 | tf_op jit(solution)/shard_map/ppermute | solution.py:174
  33.4 1.7 %later.1 = (f32[2048,128]{1,0:T(8,128)S(1)}, bf16[2048,128]{1,0:T(8,128)(2,1)S(1)}, f32[16,128]{1,0:T(8,128)S(1)}) custom-call(bf16[2048,128]{1,0:T(8,128)(2,1)S(1)} %get-tuple-element.31.qt_ref, bf16[2048,128]{1,0:T(8,128)(2,1)S(1)} %get-tuple-element.32.ct_ref, f32[16,128]{1,0:T(8,128)S(1)} %get-tuple-element.33.part_ref, ...), custom_call_target="tpu_custom_call" | custom-call | bytes 3500000 | tf_op jit(solution)/shard_map/later/pallas_call | solution.py:157
  35.7 1.6 %collective-permute-start.24 = (f32[256,128]{1,0:T(8,128)S(1)}, f32[256,128]{1,0:T(8,128)S(1)}, u32[]{:S(2)}, u32[]{:S(2)}) collective-permute-start(f32[256,128]{1,0:T(8,128)S(1)} %get-tuple-element.102), channel_id=1, source_target_pairs={{0,1},{1,0},{2,3},{3,2},{4,5},{5,4},{6,7},{7,6},{8,9},{9,8},{10,11... | collective-permute-start | bytes 393224 | tf_op jit(solution)/shard_map/ppermute | solution.py:174
  38.6 1.6 %collective-permute-start.27 = (f32[256,128]{1,0:T(8,128)S(1)}, f32[256,128]{1,0:T(8,128)S(1)}, u32[]{:S(2)}, u32[]{:S(2)}) collective-permute-start(f32[256,128]{1,0:T(8,128)S(1)} %get-tuple-element.104), channel_id=1, source_target_pairs={{0,1},{1,0},{2,3},{3,2},{4,5},{5,4},{6,7},{7,6},{8,9},{9,8},{10,11... | collective-permute-start | bytes 393224 | tf_op jit(solution)/shard_map/ppermute | solution.py:174
  40.4 1.6 %collective-permute-done.24 = f32[256,128]{1,0:T(8,128)S(1)} collective-permute-done((f32[256,128]{1,0:T(8,128)S(1)}, f32[256,128]{1,0:T(8,128)S(1)}, u32[]{:S(2)}, u32[]{:S(2)}) %collective-permute-start.24) | collective-permute-done | bytes 131104 | tf_op jit(solution)/shard_map/ppermute | solution.py:174
  42.0 3.2 %collective-permute-done.27 = f32[256,128]{1,0:T(8,128)S(1)} collective-permute-done((f32[256,128]{1,0:T(8,128)S(1)}, f32[256,128]{1,0:T(8,128)S(1)}, u32[]{:S(2)}, u32[]{:S(2)}) %collective-permute-start.27) | collective-permute-done | bytes 131104 | tf_op jit(solution)/shard_map/ppermute | solution.py:174
  45.5 2.6 %collective-permute-start.29 = (f32[256,128]{1,0:T(8,128)S(1)}, f32[256,128]{1,0:T(8,128)S(1)}, u32[]{:S(2)}, u32[]{:S(2)}) collective-permute-start(f32[256,128]{1,0:T(8,128)S(1)} %slice_select_fusion.8), channel_id=1, source_target_pairs={{0,2},{1,3},{2,0},{3,1},{4,6},{5,7},{6,4},{7,5},{8,10},{9,11},{10,... | collective-permute-start | bytes 393224 | tf_op jit(solution)/shard_map/ppermute | solution.py:174
  48.6 3.3 %collective-permute-start.16 = (f32[256,128]{1,0:T(8,128)S(1)}, f32[256,128]{1,0:T(8,128)S(1)}, u32[]{:S(2)}, u32[]{:S(2)}) collective-permute-start(f32[256,128]{1,0:T(8,128)S(1)} %get-tuple-element.73), channel_id=1, source_target_pairs={{0,24},{4,28},{8,16},{12,20},{16,8},{20,12},{24,0},{28,4},{1,25},{... | collective-permute-start | bytes 393224 | tf_op jit(solution)/shard_map/ppermute | solution.py:174
  52.6 1.9 %collective-permute-done.29 = f32[256,128]{1,0:T(8,128)S(1)} collective-permute-done((f32[256,128]{1,0:T(8,128)S(1)}, f32[256,128]{1,0:T(8,128)S(1)}, u32[]{:S(2)}, u32[]{:S(2)}) %collective-permute-start.29) | collective-permute-done | bytes 131104 | tf_op jit(solution)/shard_map/ppermute | solution.py:174
  57.6 2.9 %collective-permute-start.33 = (f32[256,128]{1,0:T(8,128)S(1)}, f32[256,128]{1,0:T(8,128)S(1)}, u32[]{:S(2)}, u32[]{:S(2)}) collective-permute-start(f32[256,128]{1,0:T(8,128)S(1)} %get-tuple-element.58), channel_id=1, source_target_pairs={{0,24},{4,28},{8,16},{12,20},{16,8},{20,12},{24,0},{28,4},{1,25},{... | collective-permute-start | bytes 393224 | tf_op jit(solution)/shard_map/ppermute | solution.py:174
  62.4 2.2 %collective-permute-done.33 = f32[256,128]{1,0:T(8,128)S(1)} collective-permute-done((f32[256,128]{1,0:T(8,128)S(1)}, f32[256,128]{1,0:T(8,128)S(1)}, u32[]{:S(2)}, u32[]{:S(2)}) %collective-permute-start.33) | collective-permute-done | bytes 131104 | tf_op jit(solution)/shard_map/ppermute | solution.py:174
  64.7 2.6 %collective-permute-done.32 = f32[256,128]{1,0:T(8,128)S(1)} collective-permute-done((f32[256,128]{1,0:T(8,128)S(1)}, f32[256,128]{1,0:T(8,128)S(1)}, u32[]{:S(2)}, u32[]{:S(2)}) %collective-permute-start.32) | collective-permute-done | bytes 131104 | tf_op jit(solution)/shard_map/ppermute | solution.py:174
  67.5 2.5 %collective-permute-done.18 = f32[256,128]{1,0:T(8,128)S(1)} collective-permute-done((f32[256,128]{1,0:T(8,128)S(1)}, f32[256,128]{1,0:T(8,128)S(1)}, u32[]{:S(2)}, u32[]{:S(2)}) %collective-permute-start.18) | collective-permute-done | bytes 131104 | tf_op jit(solution)/shard_map/ppermute | solution.py:174
  70.3 2.7 %collective-permute-start.20 = (f32[256,128]{1,0:T(8,128)S(1)}, f32[256,128]{1,0:T(8,128)S(1)}, u32[]{:S(2)}, u32[]{:S(2)}) collective-permute-start(f32[256,128]{1,0:T(8,128)S(1)} %get-tuple-element.105), channel_id=1, source_target_pairs={{0,1},{1,0},{2,3},{3,2},{4,5},{5,4},{6,7},{7,6},{8,9},{9,8},{10,11... | collective-permute-start | bytes 393224 | tf_op jit(solution)/shard_map/ppermute | solution.py:174
  73.1 2.3 %collective-permute-start.35 = (f32[256,128]{1,0:T(8,128)S(1)}, f32[256,128]{1,0:T(8,128)S(1)}, u32[]{:S(2)}, u32[]{:S(2)}) collective-permute-start(f32[256,128]{1,0:T(8,128)S(1)} %add_select_fusion.11), channel_id=1, source_target_pairs={{0,2},{1,3},{2,0},{3,1},{4,6},{5,7},{6,4},{7,5},{8,10},{9,11},{10,... | collective-permute-start | bytes 393224 | tf_op jit(solution)/shard_map/ppermute | solution.py:174
  75.4 3.6 %collective-permute-done.21 = f32[256,128]{1,0:T(8,128)S(1)} collective-permute-done((f32[256,128]{1,0:T(8,128)S(1)}, f32[256,128]{1,0:T(8,128)S(1)}, u32[]{:S(2)}, u32[]{:S(2)}) %collective-permute-start.21) | collective-permute-done | bytes 131104 | tf_op jit(solution)/shard_map/ppermute | solution.py:174
  79.2 2.0 %collective-permute-start.22 = (f32[256,128]{1,0:T(8,128)S(1)}, f32[256,128]{1,0:T(8,128)S(1)}, u32[]{:S(2)}, u32[]{:S(2)}) collective-permute-start(f32[256,128]{1,0:T(8,128)S(1)} %get-tuple-element.108), channel_id=1, source_target_pairs={{0,1},{1,0},{2,3},{3,2},{4,5},{5,4},{6,7},{7,6},{8,9},{9,8},{10,11... | collective-permute-start | bytes 393224 | tf_op jit(solution)/shard_map/ppermute | solution.py:174
  81.2 4.5 %collective-permute-done.19 = f32[256,128]{1,0:T(8,128)S(1)} collective-permute-done((f32[256,128]{1,0:T(8,128)S(1)}, f32[256,128]{1,0:T(8,128)S(1)}, u32[]{:S(2)}, u32[]{:S(2)}) %collective-permute-start.19) | collective-permute-done | bytes 131104 | tf_op jit(solution)/shard_map/ppermute | solution.py:174
  86.1 2.3 %collective-permute-start.45 = (f32[256,128]{1,0:T(8,128)S(1)}, f32[256,128]{1,0:T(8,128)S(1)}, u32[]{:S(2)}, u32[]{:S(2)}) collective-permute-start(f32[256,128]{1,0:T(8,128)S(1)} %get-tuple-element.97), channel_id=1, source_target_pairs={{0,1},{1,0},{2,3},{3,2},{4,5},{5,4},{6,7},{7,6},{8,9},{9,8},{10,11... | collective-permute-start | bytes 393224 | tf_op jit(solution)/shard_map/ppermute | solution.py:174
  88.5 4.9 %collective-permute-done.22 = f32[256,128]{1,0:T(8,128)S(1)} collective-permute-done((f32[256,128]{1,0:T(8,128)S(1)}, f32[256,128]{1,0:T(8,128)S(1)}, u32[]{:S(2)}, u32[]{:S(2)}) %collective-permute-start.22) | collective-permute-done | bytes 131104 | tf_op jit(solution)/shard_map/ppermute | solution.py:174
  94.2 2.5 %collective-permute-start.39 = (f32[16,128]{1,0:T(8,128)S(1)}, f32[16,128]{1,0:T(8,128)S(1)}, u32[]{:S(2)}, u32[]{:S(2)}) collective-permute-start(f32[16,128]{1,0:T(8,128)S(1)} %get-tuple-element.49), channel_id=1, source_target_pairs={{0,3},{1,2},{2,1},{3,0},{4,7},{5,6},{6,5},{7,4},{8,11},{9,10},{10,... | collective-permute-start | bytes 24584 | tf_op jit(solution)/shard_map/ppermute | solution.py:174
  96.7 1.9 %collective-permute-start.37 = (f32[16,128]{1,0:T(8,128)S(1)}, f32[16,128]{1,0:T(8,128)S(1)}, u32[]{:S(2)}, u32[]{:S(2)}) collective-permute-start(f32[16,128]{1,0:T(8,128)S(1)} %get-tuple-element.49), channel_id=1, source_target_pairs={{0,1},{1,0},{2,3},{3,2},{4,5},{5,4},{6,7},{7,6},{8,9},{9,8},{10,11... | collective-permute-start | bytes 24584 | tf_op jit(solution)/shard_map/ppermute | solution.py:174
  99.7 1.6 %collective-permute-done.38 = f32[16,128]{1,0:T(8,128)S(1)} collective-permute-done((f32[16,128]{1,0:T(8,128)S(1)}, f32[16,128]{1,0:T(8,128)S(1)}, u32[]{:S(2)}, u32[]{:S(2)}) %collective-permute-start.38) | collective-permute-done | bytes 8224 | tf_op jit(solution)/shard_map/ppermute | solution.py:174
  103.0 2.4 %collective-permute-start.43 = (f32[16,128]{1,0:T(8,128)S(1)}, f32[16,128]{1,0:T(8,128)S(1)}, u32[]{:S(2)}, u32[]{:S(2)}) collective-permute-start(f32[16,128]{1,0:T(8,128)S(1)} %add.170), channel_id=1, source_target_pairs={{0,24},{4,28},{8,16},{12,20},{16,8},{20,12},{24,0},{28,4},{1,25},{... | collective-permute-start | bytes 24584 | tf_op jit(solution)/shard_map/ppermute | solution.py:174
  106.5 2.3 %query.1 = (bf16[128,2048]{1,0:T(8,128)(2,1)}, bf16[128,2048]{1,0:T(8,128)(2,1)}, f32[128,2048]{1,0:T(8,128)S(1)}) custom-call(bf16[128,2048]{1,0:T(8,128)(2,1)S(1)} %copy-done.4, bf16[128,2048]{1,0:T(8,128)(2,1)S(1)} %get-tuple-element.28.qf_ref, bf16[128,2048]{1,0:T(8,128)(2,1)S(1)} %get-tuple-element.29.kf_ref, ...), custom_call_target="tpu_custom_call" | custom-call | bytes 3500000 | tf_op jit(solution)/shard_map/query/pallas_call | solution.py:157
  109.9 1.9 %key.1 = (bf16[128,2048]{1,0:T(8,128)(2,1)}, bf16[128,2048]{1,0:T(8,128)(2,1)}) custom-call(bf16[128,2048]{1,0:T(8,128)(2,1)S(1)} %copy-done.1, bf16[128,2048]{1,0:T(8,128)(2,1)S(1)} %get-tuple-element.29.kf_ref, bf16[128,2048]{1,0:T(8,128)(2,1)S(1)} %copy-done.3, f32[128,2048]{1,0:T(8,128)S(1)} %get-tuple-element.47.ki_ref, ...), custom_call_target="tpu_custom_call" | custom-call | bytes 3500000 | tf_op jit(solution)/shard_map/key/pallas_call | solution.py:157
  (149 shorter events, 26.1 us)
Async XLA Ops:
  2.0 9.5 %collective-permute-start.2 = (f32[16,128]{1,0:T(8,128)S(1)}, f32[16,128]{1,0:T(8,128)S(1)}, u32[]{:S(2)}, u32[]{:S(2)}) collective-permute-start(f32[16,128]{1,0:T(8,128)S(1)} %norm.1), channel_id=1, source_target_pairs={{0,3},{1,2},{2,1},{3,0},{4,7},{5,6},{6,5},{7,4},{8,11},{9,10},{10,... | collective-permute-start | bytes 24584 | tf_op jit(solution)/shard_map/ppermute | solution.py:174
  9.4 7.7 %collective-permute-start.5 = (f32[256,128]{1,0:T(8,128)S(1)}, f32[256,128]{1,0:T(8,128)S(1)}, u32[]{:S(2)}, u32[]{:S(2)}) collective-permute-start(f32[256,128]{1,0:T(8,128)S(1)} %get-tuple-element.111), channel_id=1, source_target_pairs={{0,1},{1,0},{2,3},{3,2},{4,5},{5,4},{6,7},{7,6},{8,9},{9,8},{10,11... | collective-permute-start | bytes 393224 | tf_op jit(solution)/shard_map/ppermute | solution.py:174
  10.9 6.2 %collective-permute-start.4 = (f32[256,128]{1,0:T(8,128)S(1)}, f32[256,128]{1,0:T(8,128)S(1)}, u32[]{:S(2)}, u32[]{:S(2)}) collective-permute-start(f32[256,128]{1,0:T(8,128)S(1)} %get-tuple-element.112), channel_id=1, source_target_pairs={{0,1},{1,0},{2,3},{3,2},{4,5},{5,4},{6,7},{7,6},{8,9},{9,8},{10,11... | collective-permute-start | bytes 393224 | tf_op jit(solution)/shard_map/ppermute | solution.py:174
  17.2 9.5 %collective-permute-start.7 = (f32[256,128]{1,0:T(8,128)S(1)}, f32[256,128]{1,0:T(8,128)S(1)}, u32[]{:S(2)}, u32[]{:S(2)}) collective-permute-start(f32[256,128]{1,0:T(8,128)S(1)} %get-tuple-element.109), channel_id=1, source_target_pairs={{0,1},{1,0},{2,3},{3,2},{4,5},{5,4},{6,7},{7,6},{8,9},{9,8},{10,11... | collective-permute-start | bytes 393224 | tf_op jit(solution)/shard_map/ppermute | solution.py:174
  18.6 8.1 %collective-permute-start.6 = (f32[256,128]{1,0:T(8,128)S(1)}, f32[256,128]{1,0:T(8,128)S(1)}, u32[]{:S(2)}, u32[]{:S(2)}) collective-permute-start(f32[256,128]{1,0:T(8,128)S(1)} %get-tuple-element.110), channel_id=1, source_target_pairs={{0,1},{1,0},{2,3},{3,2},{4,5},{5,4},{6,7},{7,6},{8,9},{9,8},{10,11... | collective-permute-start | bytes 393224 | tf_op jit(solution)/shard_map/ppermute | solution.py:174
  19.3 19.3 %collective-permute-start.12 = (f32[256,128]{1,0:T(8,128)S(1)}, f32[256,128]{1,0:T(8,128)S(1)}, u32[]{:S(2)}, u32[]{:S(2)}) collective-permute-start(f32[256,128]{1,0:T(8,128)S(1)} %slice_select_fusion.12), channel_id=1, source_target_pairs={{0,2},{1,3},{2,0},{3,1},{4,6},{5,7},{6,4},{7,5},{8,10},{9,11},{10,... | collective-permute-start | bytes 393224 | tf_op jit(solution)/shard_map/ppermute | solution.py:174
  30.4 9.9 %collective-permute-start.11 = (f32[256,128]{1,0:T(8,128)S(1)}, f32[256,128]{1,0:T(8,128)S(1)}, u32[]{:S(2)}, u32[]{:S(2)}) collective-permute-start(f32[256,128]{1,0:T(8,128)S(1)} %slice_select_fusion.14), channel_id=1, source_target_pairs={{0,2},{1,3},{2,0},{3,1},{4,6},{5,7},{6,4},{7,5},{8,10},{9,11},{10,... | collective-permute-start | bytes 393224 | tf_op jit(solution)/shard_map/ppermute | solution.py:174
  35.1 10.1 %collective-permute-start.25 = (f32[256,128]{1,0:T(8,128)S(1)}, f32[256,128]{1,0:T(8,128)S(1)}, u32[]{:S(2)}, u32[]{:S(2)}) collective-permute-start(f32[256,128]{1,0:T(8,128)S(1)} %get-tuple-element.101), channel_id=1, source_target_pairs={{0,1},{1,0},{2,3},{3,2},{4,5},{5,4},{6,7},{7,6},{8,9},{9,8},{10,11... | collective-permute-start | bytes 393224 | tf_op jit(solution)/shard_map/ppermute | solution.py:174
  35.7 6.3 %collective-permute-start.24 = (f32[256,128]{1,0:T(8,128)S(1)}, f32[256,128]{1,0:T(8,128)S(1)}, u32[]{:S(2)}, u32[]{:S(2)}) collective-permute-start(f32[256,128]{1,0:T(8,128)S(1)} %get-tuple-element.102), channel_id=1, source_target_pairs={{0,1},{1,0},{2,3},{3,2},{4,5},{5,4},{6,7},{7,6},{8,9},{9,8},{10,11... | collective-permute-start | bytes 393224 | tf_op jit(solution)/shard_map/ppermute | solution.py:174
  37.3 8.1 %collective-permute-start.28 = (f32[256,128]{1,0:T(8,128)S(1)}, f32[256,128]{1,0:T(8,128)S(1)}, u32[]{:S(2)}, u32[]{:S(2)}) collective-permute-start(f32[256,128]{1,0:T(8,128)S(1)} %get-tuple-element.103), channel_id=1, source_target_pairs={{0,1},{1,0},{2,3},{3,2},{4,5},{5,4},{6,7},{7,6},{8,9},{9,8},{10,11... | collective-permute-start | bytes 393224 | tf_op jit(solution)/shard_map/ppermute | solution.py:174
  38.6 6.6 %collective-permute-start.27 = (f32[256,128]{1,0:T(8,128)S(1)}, f32[256,128]{1,0:T(8,128)S(1)}, u32[]{:S(2)}, u32[]{:S(2)}) collective-permute-start(f32[256,128]{1,0:T(8,128)S(1)} %get-tuple-element.104), channel_id=1, source_target_pairs={{0,1},{1,0},{2,3},{3,2},{4,5},{5,4},{6,7},{7,6},{8,9},{9,8},{10,11... | collective-permute-start | bytes 393224 | tf_op jit(solution)/shard_map/ppermute | solution.py:174
  40.3 8.2 %collective-permute-start.13 = (f32[256,128]{1,0:T(8,128)S(1)}, f32[256,128]{1,0:T(8,128)S(1)}, u32[]{:S(2)}, u32[]{:S(2)}) collective-permute-start(f32[256,128]{1,0:T(8,128)S(1)} %get-tuple-element.75), channel_id=1, source_target_pairs={{0,4},{4,0},{8,12},{12,8},{16,20},{20,16},{24,28},{28,24},{1,5},{5... | collective-permute-start | bytes 393224 | tf_op jit(solution)/shard_map/ppermute | solution.py:174
  45.5 9.0 %collective-permute-start.29 = (f32[256,128]{1,0:T(8,128)S(1)}, f32[256,128]{1,0:T(8,128)S(1)}, u32[]{:S(2)}, u32[]{:S(2)}) collective-permute-start(f32[256,128]{1,0:T(8,128)S(1)} %slice_select_fusion.8), channel_id=1, source_target_pairs={{0,2},{1,3},{2,0},{3,1},{4,6},{5,7},{6,4},{7,5},{8,10},{9,11},{10,... | collective-permute-start | bytes 393224 | tf_op jit(solution)/shard_map/ppermute | solution.py:174
  48.1 7.8 %collective-permute-start.26 = (f32[256,128]{1,0:T(8,128)S(1)}, f32[256,128]{1,0:T(8,128)S(1)}, u32[]{:S(2)}, u32[]{:S(2)}) collective-permute-start(f32[256,128]{1,0:T(8,128)S(1)} %slice_select_fusion.10), channel_id=1, source_target_pairs={{0,2},{1,3},{2,0},{3,1},{4,6},{5,7},{6,4},{7,5},{8,10},{9,11},{10,... | collective-permute-start | bytes 393224 | tf_op jit(solution)/shard_map/ppermute | solution.py:174
  48.6 7.4 %collective-permute-start.16 = (f32[256,128]{1,0:T(8,128)S(1)}, f32[256,128]{1,0:T(8,128)S(1)}, u32[]{:S(2)}, u32[]{:S(2)}) collective-permute-start(f32[256,128]{1,0:T(8,128)S(1)} %get-tuple-element.73), channel_id=1, source_target_pairs={{0,24},{4,28},{8,16},{12,20},{16,8},{20,12},{24,0},{28,4},{1,25},{... | collective-permute-start | bytes 393224 | tf_op jit(solution)/shard_map/ppermute | solution.py:174
  57.6 7.1 %collective-permute-start.33 = (f32[256,128]{1,0:T(8,128)S(1)}, f32[256,128]{1,0:T(8,128)S(1)}, u32[]{:S(2)}, u32[]{:S(2)}) collective-permute-start(f32[256,128]{1,0:T(8,128)S(1)} %get-tuple-element.58), channel_id=1, source_target_pairs={{0,24},{4,28},{8,16},{12,20},{16,8},{20,12},{24,0},{28,4},{1,25},{... | collective-permute-start | bytes 393224 | tf_op jit(solution)/shard_map/ppermute | solution.py:174
  60.4 6.8 %collective-permute-start.32 = (f32[256,128]{1,0:T(8,128)S(1)}, f32[256,128]{1,0:T(8,128)S(1)}, u32[]{:S(2)}, u32[]{:S(2)}) collective-permute-start(f32[256,128]{1,0:T(8,128)S(1)} %get-tuple-element.58), channel_id=1, source_target_pairs={{0,16},{4,20},{8,24},{12,28},{16,0},{20,4},{24,8},{28,12},{1,17},{... | collective-permute-start | bytes 393224 | tf_op jit(solution)/shard_map/ppermute | solution.py:174
  60.9 6.4 %collective-permute-start.31 = (f32[256,128]{1,0:T(8,128)S(1)}, f32[256,128]{1,0:T(8,128)S(1)}, u32[]{:S(2)}, u32[]{:S(2)}) collective-permute-start(f32[256,128]{1,0:T(8,128)S(1)} %get-tuple-element.58), channel_id=1, source_target_pairs={{0,8},{4,12},{8,0},{12,4},{16,24},{20,28},{24,16},{28,20},{1,9},{5... | collective-permute-start | bytes 393224 | tf_op jit(solution)/shard_map/ppermute | solution.py:174
  61.2 8.8 %collective-permute-start.18 = (f32[256,128]{1,0:T(8,128)S(1)}, f32[256,128]{1,0:T(8,128)S(1)}, u32[]{:S(2)}, u32[]{:S(2)}) collective-permute-start(f32[256,128]{1,0:T(8,128)S(1)} %add_select_fusion.17), channel_id=1, source_target_pairs={{0,2},{1,3},{2,0},{3,1},{4,6},{5,7},{6,4},{7,5},{8,10},{9,11},{10,... | collective-permute-start | bytes 393224 | tf_op jit(solution)/shard_map/ppermute | solution.py:174
  67.4 5.6 %collective-permute-start.34 = (f32[256,128]{1,0:T(8,128)S(1)}, f32[256,128]{1,0:T(8,128)S(1)}, u32[]{:S(2)}, u32[]{:S(2)}) collective-permute-start(f32[256,128]{1,0:T(8,128)S(1)} %get-tuple-element.56), channel_id=1, source_target_pairs={{0,4},{4,0},{8,12},{12,8},{16,20},{20,16},{24,28},{28,24},{1,5},{5... | collective-permute-start | bytes 393224 | tf_op jit(solution)/shard_map/ppermute | solution.py:174
  70.1 8.9 %collective-permute-start.21 = (f32[256,128]{1,0:T(8,128)S(1)}, f32[256,128]{1,0:T(8,128)S(1)}, u32[]{:S(2)}, u32[]{:S(2)}) collective-permute-start(f32[256,128]{1,0:T(8,128)S(1)} %get-tuple-element.96), channel_id=1, source_target_pairs={{0,2},{1,3},{2,0},{3,1},{4,6},{5,7},{6,4},{7,5},{8,10},{9,11},{10,... | collective-permute-start | bytes 393224 | tf_op jit(solution)/shard_map/ppermute | solution.py:174
  70.3 15.4 %collective-permute-start.20 = (f32[256,128]{1,0:T(8,128)S(1)}, f32[256,128]{1,0:T(8,128)S(1)}, u32[]{:S(2)}, u32[]{:S(2)}) collective-permute-start(f32[256,128]{1,0:T(8,128)S(1)} %get-tuple-element.105), channel_id=1, source_target_pairs={{0,1},{1,0},{2,3},{3,2},{4,5},{5,4},{6,7},{7,6},{8,9},{9,8},{10,11... | collective-permute-start | bytes 393224 | tf_op jit(solution)/shard_map/ppermute | solution.py:174
  73.0 12.7 %collective-permute-start.19 = (f32[256,128]{1,0:T(8,128)S(1)}, f32[256,128]{1,0:T(8,128)S(1)}, u32[]{:S(2)}, u32[]{:S(2)}) collective-permute-start(f32[256,128]{1,0:T(8,128)S(1)} %get-tuple-element.106), channel_id=1, source_target_pairs={{0,1},{1,0},{2,3},{3,2},{4,5},{5,4},{6,7},{7,6},{8,9},{9,8},{10,11... | collective-permute-start | bytes 393224 | tf_op jit(solution)/shard_map/ppermute | solution.py:174
  73.1 12.6 %collective-permute-start.35 = (f32[256,128]{1,0:T(8,128)S(1)}, f32[256,128]{1,0:T(8,128)S(1)}, u32[]{:S(2)}, u32[]{:S(2)}) collective-permute-start(f32[256,128]{1,0:T(8,128)S(1)} %add_select_fusion.11), channel_id=1, source_target_pairs={{0,2},{1,3},{2,0},{3,1},{4,6},{5,7},{6,4},{7,5},{8,10},{9,11},{10,... | collective-permute-start | bytes 393224 | tf_op jit(solution)/shard_map/ppermute | solution.py:174
  79.1 14.3 %collective-permute-start.23 = (f32[256,128]{1,0:T(8,128)S(1)}, f32[256,128]{1,0:T(8,128)S(1)}, u32[]{:S(2)}, u32[]{:S(2)}) collective-permute-start(f32[256,128]{1,0:T(8,128)S(1)} %get-tuple-element.107), channel_id=1, source_target_pairs={{0,1},{1,0},{2,3},{3,2},{4,5},{5,4},{6,7},{7,6},{8,9},{9,8},{10,11... | collective-permute-start | bytes 393224 | tf_op jit(solution)/shard_map/ppermute | solution.py:174
  79.2 14.2 %collective-permute-start.22 = (f32[256,128]{1,0:T(8,128)S(1)}, f32[256,128]{1,0:T(8,128)S(1)}, u32[]{:S(2)}, u32[]{:S(2)}) collective-permute-start(f32[256,128]{1,0:T(8,128)S(1)} %get-tuple-element.108), channel_id=1, source_target_pairs={{0,1},{1,0},{2,3},{3,2},{4,5},{5,4},{6,7},{7,6},{8,9},{9,8},{10,11... | collective-permute-start | bytes 393224 | tf_op jit(solution)/shard_map/ppermute | solution.py:174
  85.9 10.9 %collective-permute-start.36 = (f32[256,128]{1,0:T(8,128)S(1)}, f32[256,128]{1,0:T(8,128)S(1)}, u32[]{:S(2)}, u32[]{:S(2)}) collective-permute-start(f32[256,128]{1,0:T(8,128)S(1)} %get-tuple-element.95), channel_id=1, source_target_pairs={{0,2},{1,3},{2,0},{3,1},{4,6},{5,7},{6,4},{7,5},{8,10},{9,11},{10,... | collective-permute-start | bytes 393224 | tf_op jit(solution)/shard_map/ppermute | solution.py:174
  86.1 15.7 %collective-permute-start.45 = (f32[256,128]{1,0:T(8,128)S(1)}, f32[256,128]{1,0:T(8,128)S(1)}, u32[]{:S(2)}, u32[]{:S(2)}) collective-permute-start(f32[256,128]{1,0:T(8,128)S(1)} %get-tuple-element.97), channel_id=1, source_target_pairs={{0,1},{1,0},{2,3},{3,2},{4,5},{5,4},{6,7},{7,6},{8,9},{9,8},{10,11... | collective-permute-start | bytes 393224 | tf_op jit(solution)/shard_map/ppermute | solution.py:174
  88.4 13.4 %collective-permute-start.44 = (f32[256,128]{1,0:T(8,128)S(1)}, f32[256,128]{1,0:T(8,128)S(1)}, u32[]{:S(2)}, u32[]{:S(2)}) collective-permute-start(f32[256,128]{1,0:T(8,128)S(1)} %get-tuple-element.98), channel_id=1, source_target_pairs={{0,1},{1,0},{2,3},{3,2},{4,5},{5,4},{6,7},{7,6},{8,9},{9,8},{10,11... | collective-permute-start | bytes 393224 | tf_op jit(solution)/shard_map/ppermute | solution.py:174
  99.7 10.0 %collective-permute-start.47 = (f32[256,128]{1,0:T(8,128)S(1)}, f32[256,128]{1,0:T(8,128)S(1)}, u32[]{:S(2)}, u32[]{:S(2)}) collective-permute-start(f32[256,128]{1,0:T(8,128)S(1)} %get-tuple-element.99), channel_id=1, source_target_pairs={{0,1},{1,0},{2,3},{3,2},{4,5},{5,4},{6,7},{7,6},{8,9},{9,8},{10,11... | collective-permute-start | bytes 393224 | tf_op jit(solution)/shard_map/ppermute | solution.py:174
  101.4 8.3 %collective-permute-start.46 = (f32[256,128]{1,0:T(8,128)S(1)}, f32[256,128]{1,0:T(8,128)S(1)}, u32[]{:S(2)}, u32[]{:S(2)}) collective-permute-start(f32[256,128]{1,0:T(8,128)S(1)} %get-tuple-element.100), channel_id=1, source_target_pairs={{0,1},{1,0},{2,3},{3,2},{4,5},{5,4},{6,7},{7,6},{8,9},{9,8},{10,11... | collective-permute-start | bytes 393224 | tf_op jit(solution)/shard_map/ppermute | solution.py:174
  103.0 5.8 %collective-permute-start.43 = (f32[16,128]{1,0:T(8,128)S(1)}, f32[16,128]{1,0:T(8,128)S(1)}, u32[]{:S(2)}, u32[]{:S(2)}) collective-permute-start(f32[16,128]{1,0:T(8,128)S(1)} %add.170), channel_id=1, source_target_pairs={{0,24},{4,28},{8,16},{12,20},{16,8},{20,12},{24,0},{28,4},{1,25},{... | collective-permute-start | bytes 24584 | tf_op jit(solution)/shard_map/ppermute | solution.py:174
  (22 other events, 77.5 us)
